TPU v7x, 256 devices: a whole 4x4x8 slice. The times are simulated.
256 devices in a mesh: row: 8 (over y, z_hi), col: 8 (over z_lo, core), depth: 4 (over x).
Axes of the slice: x: 4, y: 4, z: 8 (z_hi: 2, z_lo: 4; z = z_hi * 4 + z_lo), core: 2. Of those that a mesh axis runs over, the one named last changes fastest.
Arguments:
- left_tiles: float32 [8, 8, 4, 32, 4096], P('row', 'col', 'depth'), may hold values from -2 to 2
- right_tiles: float32 [8, 8, 4, 1, 32, 4096], P('row', 'col', 'depth'), may hold values from -2 to 2
- square_tiles: float32 [8, 8, 128, 4096], P('row', 'col', 'depth'), may hold values from -4 to 4
- pairs: int32 [8, 8, 4, 8, 3, 64], P('row', 'col', 'depth'), may hold values from 0 to 127, as said below
- counts: int32 [8, 8, 4, 8], P('row', 'col', 'depth'), may hold values from 1 to 64
Outputs:
- purified: float32 [8, 8, 128, 4096], P('row', 'col', 'depth')
Inputs may be any that keep to these rules, and one draw needn't show every extreme that they name: pairs[..., 0, :] lies below 32, pairs[..., 1, :] below 32, pairs[..., 2, :] below 128; entries at or beyond the count are padding with valid slots.
All inputs are finite; a program needn't handle non-finite values.
Results may differ from a plain program's by a relative error of at most 0.0003.
Values sent between devices are 32-bit elements; how exact they have to be, the bound alone decides.
No kernel may reach another device: no remote copies, remote signals or barrier semaphores. Data moves between devices by JAX's collectives and lax.ppermute only.
A program may use at most 64 MiB of HBM per device.

v0:
```python
import jax
import jax.numpy as jnp
from jax import lax
from jax.sharding import PartitionSpec as P

TILE_EDGE = 64


def passed_along(x, axis, by):
    count = lax.axis_size(axis)
    return lax.ppermute(x, axis, [(i, (i + by) % count) for i in range(count)])


def tile_products(left_panel, right_panel, triple, weight, tile_edge):
    left_tile = jnp.take(left_panel, triple[0], axis=0).reshape(-1, tile_edge, tile_edge)
    right_tile = jnp.take(right_panel, triple[1], axis=0).reshape(-1, tile_edge, tile_edge)
    products = jnp.einsum(
        "pij,pjk->pik",
        left_tile,
        right_tile,
        preferred_element_type=jnp.float32,
        precision=lax.Precision.HIGHEST,
    )
    return products.reshape(-1, tile_edge * tile_edge) * weight[:, None]


def on_device(left_tiles, right_tiles, square_tiles, pairs, counts):
    tile_edge = TILE_EDGE
    pattern = pairs[0, 0, 0]
    limits = counts[0, 0, 0]
    grid_rows = lax.axis_size("row")
    grid_cols = lax.axis_size("col")
    queue_depth = right_tiles.shape[3]
    row_index = lax.axis_index("row")
    slot_total = square_tiles.shape[2] * lax.axis_size("depth")
    listed = pattern.shape[2]
    slot_iota = lax.broadcasted_iota(jnp.int32, (listed,), 0)

    def accumulate(partial_value, left_panel, right_queue, step_index):
        queue_slot = (row_index + step_index) // grid_rows % queue_depth
        right_panel = lax.dynamic_index_in_dim(right_queue, queue_slot, 0, False)
        triple = lax.dynamic_index_in_dim(pattern, step_index, 0, False)
        live_count = lax.dynamic_index_in_dim(limits, step_index, 0, False)
        weight = (slot_iota < live_count).astype(jnp.float32)
        products = tile_products(left_panel, right_panel, triple, weight, tile_edge)
        return partial_value.at[triple[2]].add(products)

    initial = jnp.zeros((slot_total, tile_edge * tile_edge), jnp.float32)

    def shifted_turn(step_index, carry):
        partial_value, left_panel, right_queue = carry
        partial_value = accumulate(partial_value, left_panel, right_queue, step_index)
        left_panel = passed_along(left_panel, "col", -1)
        right_queue = passed_along(right_queue, "row", -1)
        return (partial_value, left_panel, right_queue)

    partial_value, left_panel, right_queue = lax.fori_loop(
        0, grid_cols - 1, shifted_turn, (initial, left_tiles[0, 0, 0], right_tiles[0, 0, 0])
    )
    partial_value = accumulate(partial_value, left_panel, right_queue, grid_cols - 1)
    share = lax.psum_scatter(partial_value, "depth", scatter_dimension=0, tiled=True)
    purified = 3.0 * square_tiles[0, 0] - 2.0 * share
    return purified[None, None]


def solution(mesh):
    in_specs = (
        P("row", "col", "depth", None, None),
        P("row", "col", "depth", None, None, None),
        P("row", "col", "depth", None),
        P("row", "col", "depth", None, None, None),
        P("row", "col", "depth", None),
    )
    out_specs = P("row", "col", "depth", None)
    return jax.shard_map(
        on_device, mesh=mesh, in_specs=in_specs, out_specs=out_specs, check_vma=False
    )
```

profile of v0, /device:TPU:30, one launch (start us, length us, event | category | flops | bytes accessed | tf_op | source)
XLA Modules:
  0.0 296.5 jit_solution(17295432004939053265)
XLA Ops:
  9.6 223.3 %while.18 = (s32[]{:T(128)}, f32[128,4096]{1,0:T(8,128)}, f32[32,4096]{1,0:T(8,128)S(1)}, f32[1,32,4096]{2,1,0:T(8,128)S(1)}, s32[8,3,64]{2,1,0:T(4,128)S(1)}, /*index=5*/s32[8]{0:T(128)S(1)}, s32[]{:T(128)}) while((s32[]{:T(128)}, f32[128,4096]{1,0:T(8,128)}, f32[32,4096]{1,0:T(8,128)S(1)}, f32[1,32,4096]{2,1,0:T(8,128)S(1)}, ...), condition=%wide.region_2.4_spmd.clone, body=%wide.region_0.3_spmd.clone.sunk | while | flops 202378304 | bytes 27276472 | solution.py:57
  9.7 4.1 %collective-permute-start = (f32[32,4096]{1,0:T(8,128)S(1)}, f32[32,4096]{1,0:T(8,128)S(1)}, u32[]{:S(2)}, u32[]{:S(2)}) collective-permute-start(f32[32,4096]{1,0:T(8,128)S(1)} %copy.16), channel_id=1, source_target_pairs={{0,28},{4,0},{8,4},{12,8},{16,12},{20,16},{24,20},{28,24},{1,29},{... | collective-permute-start | bytes 1572872 | tf_op jit(solution)/shard_map/while/body/eval_jaxpr/ppermute | solution.py:11
  13.8 4.7 %collective-permute-start.1 = (f32[1,32,4096]{2,1,0:T(8,128)S(1)}, f32[1,32,4096]{2,1,0:T(8,128)S(1)}, u32[]{:S(2)}, u32[]{:S(2)}) collective-permute-start(f32[1,32,4096]{2,1,0:T(8,128)S(1)} %copy.17), channel_id=1, source_target_pairs={{0,224},{32,0},{64,32},{96,64},{128,96},{160,128},{192,160},{224,1... | collective-permute-start | bytes 1572872 | tf_op jit(solution)/shard_map/while/body/eval_jaxpr/ppermute | solution.py:11
  20.7 3.1 %reshape.210 = f32[64,64,64]{2,1,0:T(8,128)} reshape(f32[64,4096]{1,0:T(8,128)} %broadcast_select_fusion.6) | data formatting | bytes 2097152 | tf_op jit(solution)/shard_map/while/body/eval_jaxpr/reshape | solution.py:15
  25.8 3.1 %reshape.211 = f32[64,64,64]{2,1,0:T(8,128)} reshape(f32[64,4096]{1,0:T(8,128)} %broadcast_select_fusion.7) | data formatting | bytes 2097152 | tf_op jit(solution)/shard_map/while/body/eval_jaxpr/reshape | solution.py:16
  28.9 5.7 %fusion.26 = f32[64,64,64]{2,1,0:T(8,128)} fusion(f32[64,64,64]{2,1,0:T(8,128)} %reshape.210, f32[64,64,64]{2,1,0:T(8,128)} %reshape.211), kind=kOutput, calls=%fused_computation.39.clone.1 | convolution fusion | flops 201326592 | bytes 3145728 | tf_op jit(solution)/shard_map/while/body/eval_jaxpr/pij,pjk->pik/dot_general | solution.py:17
  38.0 4.9 %scatter_custom_fusion.8 = f32[128,4096]{1,0:T(8,128)} fusion(f32[128,4096]{1,0:T(8,128)} %get-tuple-element.245, s32[64]{0:T(128)S(1)} %fusion.25, f32[64,4096]{1,0:T(8,128)S(1)} %reshape.212, f32[64]{0:T(128)S(1)} %compare_convert_fusion.3), kind=kCustom, calls=%fused_computation.7.clone.1 | custom fusion | flops 524288 | bytes 3146240 | tf_op jit(solution)/shard_map/while/body/eval_jaxpr/scatter-add | solution.py:46
  43.8 4.9 %collective-permute-start.1 = (f32[1,32,4096]{2,1,0:T(8,128)S(1)}, f32[1,32,4096]{2,1,0:T(8,128)S(1)}, u32[]{:S(2)}, u32[]{:S(2)}) collective-permute-start(f32[1,32,4096]{2,1,0:T(8,128)S(1)} %copy.17), channel_id=1, source_target_pairs={{0,224},{32,0},{64,32},{96,64},{128,96},{160,128},{192,160},{224,1... | collective-permute-start | bytes 1572872 | tf_op jit(solution)/shard_map/while/body/eval_jaxpr/ppermute | solution.py:11
  50.7 3.1 %reshape.210 = f32[64,64,64]{2,1,0:T(8,128)} reshape(f32[64,4096]{1,0:T(8,128)} %broadcast_select_fusion.6) | data formatting | bytes 2097152 | tf_op jit(solution)/shard_map/while/body/eval_jaxpr/reshape | solution.py:15
  55.9 3.1 %reshape.211 = f32[64,64,64]{2,1,0:T(8,128)} reshape(f32[64,4096]{1,0:T(8,128)} %broadcast_select_fusion.7) | data formatting | bytes 2097152 | tf_op jit(solution)/shard_map/while/body/eval_jaxpr/reshape | solution.py:16
  59.0 5.7 %fusion.26 = f32[64,64,64]{2,1,0:T(8,128)} fusion(f32[64,64,64]{2,1,0:T(8,128)} %reshape.210, f32[64,64,64]{2,1,0:T(8,128)} %reshape.211), kind=kOutput, calls=%fused_computation.39.clone.1 | convolution fusion | flops 201326592 | bytes 3145728 | tf_op jit(solution)/shard_map/while/body/eval_jaxpr/pij,pjk->pik/dot_general | solution.py:17
  68.1 4.9 %scatter_custom_fusion.8 = f32[128,4096]{1,0:T(8,128)} fusion(f32[128,4096]{1,0:T(8,128)} %get-tuple-element.245, s32[64]{0:T(128)S(1)} %fusion.25, f32[64,4096]{1,0:T(8,128)S(1)} %reshape.212, f32[64]{0:T(128)S(1)} %compare_convert_fusion.3), kind=kCustom, calls=%fused_computation.7.clone.1 | custom fusion | flops 524288 | bytes 3146240 | tf_op jit(solution)/shard_map/while/body/eval_jaxpr/scatter-add | solution.py:46
  73.1 3.2 %collective-permute-start = (f32[32,4096]{1,0:T(8,128)S(1)}, f32[32,4096]{1,0:T(8,128)S(1)}, u32[]{:S(2)}, u32[]{:S(2)}) collective-permute-start(f32[32,4096]{1,0:T(8,128)S(1)} %copy.16), channel_id=1, source_target_pairs={{0,28},{4,0},{8,4},{12,8},{16,12},{20,16},{24,20},{28,24},{1,29},{... | collective-permute-start | bytes 1572872 | tf_op jit(solution)/shard_map/while/body/eval_jaxpr/ppermute | solution.py:11
  76.4 4.3 %collective-permute-start.1 = (f32[1,32,4096]{2,1,0:T(8,128)S(1)}, f32[1,32,4096]{2,1,0:T(8,128)S(1)}, u32[]{:S(2)}, u32[]{:S(2)}) collective-permute-start(f32[1,32,4096]{2,1,0:T(8,128)S(1)} %copy.17), channel_id=1, source_target_pairs={{0,224},{32,0},{64,32},{96,64},{128,96},{160,128},{192,160},{224,1... | collective-permute-start | bytes 1572872 | tf_op jit(solution)/shard_map/while/body/eval_jaxpr/ppermute | solution.py:11
  82.8 3.1 %reshape.210 = f32[64,64,64]{2,1,0:T(8,128)} reshape(f32[64,4096]{1,0:T(8,128)} %broadcast_select_fusion.6) | data formatting | bytes 2097152 | tf_op jit(solution)/shard_map/while/body/eval_jaxpr/reshape | solution.py:15
  87.9 3.1 %reshape.211 = f32[64,64,64]{2,1,0:T(8,128)} reshape(f32[64,4096]{1,0:T(8,128)} %broadcast_select_fusion.7) | data formatting | bytes 2097152 | tf_op jit(solution)/shard_map/while/body/eval_jaxpr/reshape | solution.py:16
  91.0 5.7 %fusion.26 = f32[64,64,64]{2,1,0:T(8,128)} fusion(f32[64,64,64]{2,1,0:T(8,128)} %reshape.210, f32[64,64,64]{2,1,0:T(8,128)} %reshape.211), kind=kOutput, calls=%fused_computation.39.clone.1 | convolution fusion | flops 201326592 | bytes 3145728 | tf_op jit(solution)/shard_map/while/body/eval_jaxpr/pij,pjk->pik/dot_general | solution.py:17
  100.1 4.9 %scatter_custom_fusion.8 = f32[128,4096]{1,0:T(8,128)} fusion(f32[128,4096]{1,0:T(8,128)} %get-tuple-element.245, s32[64]{0:T(128)S(1)} %fusion.25, f32[64,4096]{1,0:T(8,128)S(1)} %reshape.212, f32[64]{0:T(128)S(1)} %compare_convert_fusion.3), kind=kCustom, calls=%fused_computation.7.clone.1 | custom fusion | flops 524288 | bytes 3146240 | tf_op jit(solution)/shard_map/while/body/eval_jaxpr/scatter-add | solution.py:46
  105.1 5.1 %collective-permute-start = (f32[32,4096]{1,0:T(8,128)S(1)}, f32[32,4096]{1,0:T(8,128)S(1)}, u32[]{:S(2)}, u32[]{:S(2)}) collective-permute-start(f32[32,4096]{1,0:T(8,128)S(1)} %copy.16), channel_id=1, source_target_pairs={{0,28},{4,0},{8,4},{12,8},{16,12},{20,16},{24,20},{28,24},{1,29},{... | collective-permute-start | bytes 1572872 | tf_op jit(solution)/shard_map/while/body/eval_jaxpr/ppermute | solution.py:11
  110.3 3.0 %collective-permute-start.1 = (f32[1,32,4096]{2,1,0:T(8,128)S(1)}, f32[1,32,4096]{2,1,0:T(8,128)S(1)}, u32[]{:S(2)}, u32[]{:S(2)}) collective-permute-start(f32[1,32,4096]{2,1,0:T(8,128)S(1)} %copy.17), channel_id=1, source_target_pairs={{0,224},{32,0},{64,32},{96,64},{128,96},{160,128},{192,160},{224,1... | collective-permute-start | bytes 1572872 | tf_op jit(solution)/shard_map/while/body/eval_jaxpr/ppermute | solution.py:11
  115.4 3.1 %reshape.210 = f32[64,64,64]{2,1,0:T(8,128)} reshape(f32[64,4096]{1,0:T(8,128)} %broadcast_select_fusion.6) | data formatting | bytes 2097152 | tf_op jit(solution)/shard_map/while/body/eval_jaxpr/reshape | solution.py:15
  120.5 3.1 %reshape.211 = f32[64,64,64]{2,1,0:T(8,128)} reshape(f32[64,4096]{1,0:T(8,128)} %broadcast_select_fusion.7) | data formatting | bytes 2097152 | tf_op jit(solution)/shard_map/while/body/eval_jaxpr/reshape | solution.py:16
  123.6 5.7 %fusion.26 = f32[64,64,64]{2,1,0:T(8,128)} fusion(f32[64,64,64]{2,1,0:T(8,128)} %reshape.210, f32[64,64,64]{2,1,0:T(8,128)} %reshape.211), kind=kOutput, calls=%fused_computation.39.clone.1 | convolution fusion | flops 201326592 | bytes 3145728 | tf_op jit(solution)/shard_map/while/body/eval_jaxpr/pij,pjk->pik/dot_general | solution.py:17
  132.7 4.9 %scatter_custom_fusion.8 = f32[128,4096]{1,0:T(8,128)} fusion(f32[128,4096]{1,0:T(8,128)} %get-tuple-element.245, s32[64]{0:T(128)S(1)} %fusion.25, f32[64,4096]{1,0:T(8,128)S(1)} %reshape.212, f32[64]{0:T(128)S(1)} %compare_convert_fusion.3), kind=kCustom, calls=%fused_computation.7.clone.1 | custom fusion | flops 524288 | bytes 3146240 | tf_op jit(solution)/shard_map/while/body/eval_jaxpr/scatter-add | solution.py:46
  137.7 3.9 %collective-permute-start = (f32[32,4096]{1,0:T(8,128)S(1)}, f32[32,4096]{1,0:T(8,128)S(1)}, u32[]{:S(2)}, u32[]{:S(2)}) collective-permute-start(f32[32,4096]{1,0:T(8,128)S(1)} %copy.16), channel_id=1, source_target_pairs={{0,28},{4,0},{8,4},{12,8},{16,12},{20,16},{24,20},{28,24},{1,29},{... | collective-permute-start | bytes 1572872 | tf_op jit(solution)/shard_map/while/body/eval_jaxpr/ppermute | solution.py:11
  141.7 3.2 %collective-permute-start.1 = (f32[1,32,4096]{2,1,0:T(8,128)S(1)}, f32[1,32,4096]{2,1,0:T(8,128)S(1)}, u32[]{:S(2)}, u32[]{:S(2)}) collective-permute-start(f32[1,32,4096]{2,1,0:T(8,128)S(1)} %copy.17), channel_id=1, source_target_pairs={{0,224},{32,0},{64,32},{96,64},{128,96},{160,128},{192,160},{224,1... | collective-permute-start | bytes 1572872 | tf_op jit(solution)/shard_map/while/body/eval_jaxpr/ppermute | solution.py:11
  147.0 3.1 %reshape.210 = f32[64,64,64]{2,1,0:T(8,128)} reshape(f32[64,4096]{1,0:T(8,128)} %broadcast_select_fusion.6) | data formatting | bytes 2097152 | tf_op jit(solution)/shard_map/while/body/eval_jaxpr/reshape | solution.py:15
  152.2 3.1 %reshape.211 = f32[64,64,64]{2,1,0:T(8,128)} reshape(f32[64,4096]{1,0:T(8,128)} %broadcast_select_fusion.7) | data formatting | bytes 2097152 | tf_op jit(solution)/shard_map/while/body/eval_jaxpr/reshape | solution.py:16
  155.3 5.7 %fusion.26 = f32[64,64,64]{2,1,0:T(8,128)} fusion(f32[64,64,64]{2,1,0:T(8,128)} %reshape.210, f32[64,64,64]{2,1,0:T(8,128)} %reshape.211), kind=kOutput, calls=%fused_computation.39.clone.1 | convolution fusion | flops 201326592 | bytes 3145728 | tf_op jit(solution)/shard_map/while/body/eval_jaxpr/pij,pjk->pik/dot_general | solution.py:17
  164.4 4.9 %scatter_custom_fusion.8 = f32[128,4096]{1,0:T(8,128)} fusion(f32[128,4096]{1,0:T(8,128)} %get-tuple-element.245, s32[64]{0:T(128)S(1)} %fusion.25, f32[64,4096]{1,0:T(8,128)S(1)} %reshape.212, f32[64]{0:T(128)S(1)} %compare_convert_fusion.3), kind=kCustom, calls=%fused_computation.7.clone.1 | custom fusion | flops 524288 | bytes 3146240 | tf_op jit(solution)/shard_map/while/body/eval_jaxpr/scatter-add | solution.py:46
  169.3 4.2 %collective-permute-start = (f32[32,4096]{1,0:T(8,128)S(1)}, f32[32,4096]{1,0:T(8,128)S(1)}, u32[]{:S(2)}, u32[]{:S(2)}) collective-permute-start(f32[32,4096]{1,0:T(8,128)S(1)} %copy.16), channel_id=1, source_target_pairs={{0,28},{4,0},{8,4},{12,8},{16,12},{20,16},{24,20},{28,24},{1,29},{... | collective-permute-start | bytes 1572872 | tf_op jit(solution)/shard_map/while/body/eval_jaxpr/ppermute | solution.py:11
  173.6 3.3 %collective-permute-start.1 = (f32[1,32,4096]{2,1,0:T(8,128)S(1)}, f32[1,32,4096]{2,1,0:T(8,128)S(1)}, u32[]{:S(2)}, u32[]{:S(2)}) collective-permute-start(f32[1,32,4096]{2,1,0:T(8,128)S(1)} %copy.17), channel_id=1, source_target_pairs={{0,224},{32,0},{64,32},{96,64},{128,96},{160,128},{192,160},{224,1... | collective-permute-start | bytes 1572872 | tf_op jit(solution)/shard_map/while/body/eval_jaxpr/ppermute | solution.py:11
  178.9 3.1 %reshape.210 = f32[64,64,64]{2,1,0:T(8,128)} reshape(f32[64,4096]{1,0:T(8,128)} %broadcast_select_fusion.6) | data formatting | bytes 2097152 | tf_op jit(solution)/shard_map/while/body/eval_jaxpr/reshape | solution.py:15
  184.1 3.1 %reshape.211 = f32[64,64,64]{2,1,0:T(8,128)} reshape(f32[64,4096]{1,0:T(8,128)} %broadcast_select_fusion.7) | data formatting | bytes 2097152 | tf_op jit(solution)/shard_map/while/body/eval_jaxpr/reshape | solution.py:16
  187.2 5.7 %fusion.26 = f32[64,64,64]{2,1,0:T(8,128)} fusion(f32[64,64,64]{2,1,0:T(8,128)} %reshape.210, f32[64,64,64]{2,1,0:T(8,128)} %reshape.211), kind=kOutput, calls=%fused_computation.39.clone.1 | convolution fusion | flops 201326592 | bytes 3145728 | tf_op jit(solution)/shard_map/while/body/eval_jaxpr/pij,pjk->pik/dot_general | solution.py:17
  196.3 4.9 %scatter_custom_fusion.8 = f32[128,4096]{1,0:T(8,128)} fusion(f32[128,4096]{1,0:T(8,128)} %get-tuple-element.245, s32[64]{0:T(128)S(1)} %fusion.25, f32[64,4096]{1,0:T(8,128)S(1)} %reshape.212, f32[64]{0:T(128)S(1)} %compare_convert_fusion.3), kind=kCustom, calls=%fused_computation.7.clone.1 | custom fusion | flops 524288 | bytes 3146240 | tf_op jit(solution)/shard_map/while/body/eval_jaxpr/scatter-add | solution.py:46
  201.3 4.2 %collective-permute-start = (f32[32,4096]{1,0:T(8,128)S(1)}, f32[32,4096]{1,0:T(8,128)S(1)}, u32[]{:S(2)}, u32[]{:S(2)}) collective-permute-start(f32[32,4096]{1,0:T(8,128)S(1)} %copy.16), channel_id=1, source_target_pairs={{0,28},{4,0},{8,4},{12,8},{16,12},{20,16},{24,20},{28,24},{1,29},{... | collective-permute-start | bytes 1572872 | tf_op jit(solution)/shard_map/while/body/eval_jaxpr/ppermute | solution.py:11
  205.5 3.0 %collective-permute-start.1 = (f32[1,32,4096]{2,1,0:T(8,128)S(1)}, f32[1,32,4096]{2,1,0:T(8,128)S(1)}, u32[]{:S(2)}, u32[]{:S(2)}) collective-permute-start(f32[1,32,4096]{2,1,0:T(8,128)S(1)} %copy.17), channel_id=1, source_target_pairs={{0,224},{32,0},{64,32},{96,64},{128,96},{160,128},{192,160},{224,1... | collective-permute-start | bytes 1572872 | tf_op jit(solution)/shard_map/while/body/eval_jaxpr/ppermute | solution.py:11
  210.6 3.1 %reshape.210 = f32[64,64,64]{2,1,0:T(8,128)} reshape(f32[64,4096]{1,0:T(8,128)} %broadcast_select_fusion.6) | data formatting | bytes 2097152 | tf_op jit(solution)/shard_map/while/body/eval_jaxpr/reshape | solution.py:15
  215.8 3.1 %reshape.211 = f32[64,64,64]{2,1,0:T(8,128)} reshape(f32[64,4096]{1,0:T(8,128)} %broadcast_select_fusion.7) | data formatting | bytes 2097152 | tf_op jit(solution)/shard_map/while/body/eval_jaxpr/reshape | solution.py:16
  218.9 5.7 %fusion.26 = f32[64,64,64]{2,1,0:T(8,128)} fusion(f32[64,64,64]{2,1,0:T(8,128)} %reshape.210, f32[64,64,64]{2,1,0:T(8,128)} %reshape.211), kind=kOutput, calls=%fused_computation.39.clone.1 | convolution fusion | flops 201326592 | bytes 3145728 | tf_op jit(solution)/shard_map/while/body/eval_jaxpr/pij,pjk->pik/dot_general | solution.py:17
  228.0 4.9 %scatter_custom_fusion.8 = f32[128,4096]{1,0:T(8,128)} fusion(f32[128,4096]{1,0:T(8,128)} %get-tuple-element.245, s32[64]{0:T(128)S(1)} %fusion.25, f32[64,4096]{1,0:T(8,128)S(1)} %reshape.212, f32[64]{0:T(128)S(1)} %compare_convert_fusion.3), kind=kCustom, calls=%fused_computation.7.clone.1 | custom fusion | flops 524288 | bytes 3146240 | tf_op jit(solution)/shard_map/while/body/eval_jaxpr/scatter-add | solution.py:46
  236.4 2.3 reshape.122
  238.7 2.2 reshape.123
  240.9 5.1 %fusion.12 = f32[64,64,64]{2,1,0:T(8,128)} fusion(f32[64,64,64]{2,1,0:T(8,128)S(1)} %reshape.122, f32[64,64,64]{2,1,0:T(8,128)} %reshape.123), kind=kOutput, calls=%fused_computation.40 | convolution fusion | flops 201326592 | bytes 3145728 | tf_op jit(solution)/shard_map/pij,pjk->pik/dot_general | solution.py:17
  246.0 2.3 reshape.124
  248.9 2.8 scatter_custom_fusion.1
  253.1 34.6 %reduce-scatter.2.cloned.1.call-done = f32[32,4096]{1,0:T(8,128)} async-done(((f32[128,4096]{1,0:T(8,128)}), f32[32,4096]{1,0:T(8,128)}) %reduce-scatter.2.cloned.1.call-update) | async-done | bytes 524304 | tf_op jit(solution)/shard_map/reduce_scatter | solution.py:61
  (136 shorter events, 64.2 us)
Async XLA Ops:
  6.5 3.1 %copy-start = (f32[1,1,1,32,4096]{4,3,2,1,0:T(8,128)S(1)}, f32[1,1,1,32,4096]{4,3,2,1,0:T(8,128)}, u32[]{:S(2)}) copy-start(f32[1,1,1,32,4096]{4,3,2,1,0:T(8,128)} %param.9) | copy-start | bytes 1572868
  6.5 3.1 %copy-start.1 = (f32[1,1,1,1,32,4096]{5,4,3,2,1,0:T(8,128)S(1)}, f32[1,1,1,1,32,4096]{5,4,3,2,1,0:T(8,128)}, u32[]{:S(2)}) copy-start(f32[1,1,1,1,32,4096]{5,4,3,2,1,0:T(8,128)} %param.10) | copy-start | bytes 1572868
  6.5 0.8 copy-start.6
  6.5 0.9 copy-start.7
  6.5 281.2 %reduce-scatter.2.cloned.1.call-start = ((), (), s32[]{:S(2)}) async-start(), calls=%async_computation.1 | async-start | bytes 2621440 | tf_op jit(solution)/shard_map/reduce_scatter | solution.py:61
  9.7 33.3 %collective-permute-start = (f32[32,4096]{1,0:T(8,128)S(1)}, f32[32,4096]{1,0:T(8,128)S(1)}, u32[]{:S(2)}, u32[]{:S(2)}) collective-permute-start(f32[32,4096]{1,0:T(8,128)S(1)} %copy.16), channel_id=1, source_target_pairs={{0,28},{4,0},{8,4},{12,8},{16,12},{20,16},{24,20},{28,24},{1,29},{... | collective-permute-start | bytes 1572872 | tf_op jit(solution)/shard_map/while/body/eval_jaxpr/ppermute | solution.py:11
  13.8 29.1 %collective-permute-start.1 = (f32[1,32,4096]{2,1,0:T(8,128)S(1)}, f32[1,32,4096]{2,1,0:T(8,128)S(1)}, u32[]{:S(2)}, u32[]{:S(2)}) collective-permute-start(f32[1,32,4096]{2,1,0:T(8,128)S(1)} %copy.17), channel_id=1, source_target_pairs={{0,224},{32,0},{64,32},{96,64},{128,96},{160,128},{192,160},{224,1... | collective-permute-start | bytes 1572872 | tf_op jit(solution)/shard_map/while/body/eval_jaxpr/ppermute | solution.py:11
  43.0 30.0 %collective-permute-start = (f32[32,4096]{1,0:T(8,128)S(1)}, f32[32,4096]{1,0:T(8,128)S(1)}, u32[]{:S(2)}, u32[]{:S(2)}) collective-permute-start(f32[32,4096]{1,0:T(8,128)S(1)} %copy.16), channel_id=1, source_target_pairs={{0,28},{4,0},{8,4},{12,8},{16,12},{20,16},{24,20},{28,24},{1,29},{... | collective-permute-start | bytes 1572872 | tf_op jit(solution)/shard_map/while/body/eval_jaxpr/ppermute | solution.py:11
  43.8 29.2 %collective-permute-start.1 = (f32[1,32,4096]{2,1,0:T(8,128)S(1)}, f32[1,32,4096]{2,1,0:T(8,128)S(1)}, u32[]{:S(2)}, u32[]{:S(2)}) collective-permute-start(f32[1,32,4096]{2,1,0:T(8,128)S(1)} %copy.17), channel_id=1, source_target_pairs={{0,224},{32,0},{64,32},{96,64},{128,96},{160,128},{192,160},{224,1... | collective-permute-start | bytes 1572872 | tf_op jit(solution)/shard_map/while/body/eval_jaxpr/ppermute | solution.py:11
  73.1 32.0 %collective-permute-start = (f32[32,4096]{1,0:T(8,128)S(1)}, f32[32,4096]{1,0:T(8,128)S(1)}, u32[]{:S(2)}, u32[]{:S(2)}) collective-permute-start(f32[32,4096]{1,0:T(8,128)S(1)} %copy.16), channel_id=1, source_target_pairs={{0,28},{4,0},{8,4},{12,8},{16,12},{20,16},{24,20},{28,24},{1,29},{... | collective-permute-start | bytes 1572872 | tf_op jit(solution)/shard_map/while/body/eval_jaxpr/ppermute | solution.py:11
  76.4 28.7 %collective-permute-start.1 = (f32[1,32,4096]{2,1,0:T(8,128)S(1)}, f32[1,32,4096]{2,1,0:T(8,128)S(1)}, u32[]{:S(2)}, u32[]{:S(2)}) collective-permute-start(f32[1,32,4096]{2,1,0:T(8,128)S(1)} %copy.17), channel_id=1, source_target_pairs={{0,224},{32,0},{64,32},{96,64},{128,96},{160,128},{192,160},{224,1... | collective-permute-start | bytes 1572872 | tf_op jit(solution)/shard_map/while/body/eval_jaxpr/ppermute | solution.py:11
  105.1 32.5 %collective-permute-start = (f32[32,4096]{1,0:T(8,128)S(1)}, f32[32,4096]{1,0:T(8,128)S(1)}, u32[]{:S(2)}, u32[]{:S(2)}) collective-permute-start(f32[32,4096]{1,0:T(8,128)S(1)} %copy.16), channel_id=1, source_target_pairs={{0,28},{4,0},{8,4},{12,8},{16,12},{20,16},{24,20},{28,24},{1,29},{... | collective-permute-start | bytes 1572872 | tf_op jit(solution)/shard_map/while/body/eval_jaxpr/ppermute | solution.py:11
  110.3 27.4 %collective-permute-start.1 = (f32[1,32,4096]{2,1,0:T(8,128)S(1)}, f32[1,32,4096]{2,1,0:T(8,128)S(1)}, u32[]{:S(2)}, u32[]{:S(2)}) collective-permute-start(f32[1,32,4096]{2,1,0:T(8,128)S(1)} %copy.17), channel_id=1, source_target_pairs={{0,224},{32,0},{64,32},{96,64},{128,96},{160,128},{192,160},{224,1... | collective-permute-start | bytes 1572872 | tf_op jit(solution)/shard_map/while/body/eval_jaxpr/ppermute | solution.py:11
  137.7 31.6 %collective-permute-start = (f32[32,4096]{1,0:T(8,128)S(1)}, f32[32,4096]{1,0:T(8,128)S(1)}, u32[]{:S(2)}, u32[]{:S(2)}) collective-permute-start(f32[32,4096]{1,0:T(8,128)S(1)} %copy.16), channel_id=1, source_target_pairs={{0,28},{4,0},{8,4},{12,8},{16,12},{20,16},{24,20},{28,24},{1,29},{... | collective-permute-start | bytes 1572872 | tf_op jit(solution)/shard_map/while/body/eval_jaxpr/ppermute | solution.py:11
  141.7 27.6 %collective-permute-start.1 = (f32[1,32,4096]{2,1,0:T(8,128)S(1)}, f32[1,32,4096]{2,1,0:T(8,128)S(1)}, u32[]{:S(2)}, u32[]{:S(2)}) collective-permute-start(f32[1,32,4096]{2,1,0:T(8,128)S(1)} %copy.17), channel_id=1, source_target_pairs={{0,224},{32,0},{64,32},{96,64},{128,96},{160,128},{192,160},{224,1... | collective-permute-start | bytes 1572872 | tf_op jit(solution)/shard_map/while/body/eval_jaxpr/ppermute | solution.py:11
  169.3 31.9 %collective-permute-start = (f32[32,4096]{1,0:T(8,128)S(1)}, f32[32,4096]{1,0:T(8,128)S(1)}, u32[]{:S(2)}, u32[]{:S(2)}) collective-permute-start(f32[32,4096]{1,0:T(8,128)S(1)} %copy.16), channel_id=1, source_target_pairs={{0,28},{4,0},{8,4},{12,8},{16,12},{20,16},{24,20},{28,24},{1,29},{... | collective-permute-start | bytes 1572872 | tf_op jit(solution)/shard_map/while/body/eval_jaxpr/ppermute | solution.py:11
  173.6 27.7 %collective-permute-start.1 = (f32[1,32,4096]{2,1,0:T(8,128)S(1)}, f32[1,32,4096]{2,1,0:T(8,128)S(1)}, u32[]{:S(2)}, u32[]{:S(2)}) collective-permute-start(f32[1,32,4096]{2,1,0:T(8,128)S(1)} %copy.17), channel_id=1, source_target_pairs={{0,224},{32,0},{64,32},{96,64},{128,96},{160,128},{192,160},{224,1... | collective-permute-start | bytes 1572872 | tf_op jit(solution)/shard_map/while/body/eval_jaxpr/ppermute | solution.py:11
  201.3 31.7 %collective-permute-start = (f32[32,4096]{1,0:T(8,128)S(1)}, f32[32,4096]{1,0:T(8,128)S(1)}, u32[]{:S(2)}, u32[]{:S(2)}) collective-permute-start(f32[32,4096]{1,0:T(8,128)S(1)} %copy.16), channel_id=1, source_target_pairs={{0,28},{4,0},{8,4},{12,8},{16,12},{20,16},{24,20},{28,24},{1,29},{... | collective-permute-start | bytes 1572872 | tf_op jit(solution)/shard_map/while/body/eval_jaxpr/ppermute | solution.py:11
  205.5 27.4 %collective-permute-start.1 = (f32[1,32,4096]{2,1,0:T(8,128)S(1)}, f32[1,32,4096]{2,1,0:T(8,128)S(1)}, u32[]{:S(2)}, u32[]{:S(2)}) collective-permute-start(f32[1,32,4096]{2,1,0:T(8,128)S(1)} %copy.17), channel_id=1, source_target_pairs={{0,224},{32,0},{64,32},{96,64},{128,96},{160,128},{192,160},{224,1... | collective-permute-start | bytes 1572872 | tf_op jit(solution)/shard_map/while/body/eval_jaxpr/ppermute | solution.py:11
  236.4 2.3 copy-start.4
  246.0 3.0 %copy-start.2 = (f32[128,4096]{1,0:T(8,128)S(1)}, f32[128,4096]{1,0:T(8,128)}, u32[]{:S(2)}) copy-start(f32[128,4096]{1,0:T(8,128)} %get-tuple-element.143) | copy-start | bytes 6291460
  251.8 1.3 copy-start.3
  251.8 36.0 %copy-start.5 = (f32[1,1,32,4096]{3,2,1,0:T(8,128)S(1)}, f32[1,1,32,4096]{3,2,1,0:T(8,128)}, u32[]{:S(2)}) copy-start(f32[1,1,32,4096]{3,2,1,0:T(8,128)} %param.11) | copy-start | bytes 1572868
Sparse Core Ops, SparseCore 0:
  253.3 34.4 reduce-scatter.1
where the time goes:
time: 301 us; the launch traced here: 296 us
  local copies, waits for them, and re-layouts  89 us (30%)
  other arithmetic  61.7 us (20%)
  starting transfers between devices  52.1 us (17%)
  matrix products  45 us (15%)
  waiting for transfers between devices  34.7 us (12%)
  between operations  13.5 us (4%)
    ppermute x14, starting transfers between devices, passed_along(): return lax.ppermute(x, axis, [(i, (i + by) % count) for i in range(count)])  52.1 us
    dot_general x8, matrix products, tile_products(): jnp.einsum('pij,pjk->pik', left_tile, right_tile, preferred_element_type=...  45 us
    scatter-add x8, other arithmetic, accumulate(): return partial_value.at[triple[2]].add(products)  37.3 us
    reduce_scatter x1, waiting for transfers between devices, on_device(): lax.psum_scatter(partial_value, 'depth', scatter_dimension=0, tiled=True)  34.6 us
    reshape x8, local copies, waits for them, and re-layouts, tile_products(): jnp.take(left_panel, triple[0], axis=0).reshape(-1, tile_edge, tile_edge)  24 us
    reshape x8, local copies, waits for them, and re-layouts, tile_products(): jnp.take(right_panel, triple[1], axis=0).reshape(-1, tile_edge, tile_edge)  23.8 us
    reshape x8, local copies, waits for them, and re-layouts, tile_products(): return products.reshape(-1, tile_edge * tile_edge) * weight[:, None]  17.1 us
    select_n x8, other arithmetic, tile_products(): jnp.take(right_panel, triple[1], axis=0).reshape(-1, tile_edge, tile_edge)  9.38 us
  transfers between devices with their start and end apart: 15, of which 1 were waited for; matrix products, arithmetic and copies ran while one was open for 58% of the time, Pallas kernels for 0%

commit v1 on v0

v1 whole, which is shorter than its diff:
```python
import functools

import jax
import jax.numpy as jnp
from jax import lax
from jax.experimental import pallas as pl
from jax.experimental.pallas import tpu as pltpu
from jax.sharding import PartitionSpec as P

AXES = ("row", "col", "depth")
F32 = jnp.float32
BF16 = jnp.bfloat16
TILES = 32
SLOTS = 128
UNROLL = 32


def moved(x, target):
    pairs = []
    for y in range(4):
        for zh in range(2):
            for zl in range(4):
                for c in range(2):
                    for d in range(4):
                        ty, th, tl, tc, td = target(y, zh, zl, c, d)
                        source = ((y * 2 + zh) * 8 + zl * 2 + c) * 4 + d
                        dest = ((ty % 4 * 2 + th % 2) * 8 + tl % 4 * 2 + tc % 2) * 4 + td % 4
                        pairs.append((source, dest))
    return lax.ppermute(x, AXES, pairs)


def by_y(x, k):
    return moved(x, lambda y, zh, zl, c, d: (y + k, zh, zl, c, d))


def by_zl(x, k):
    return moved(x, lambda y, zh, zl, c, d: (y, zh, zl + k, c, d))


def by_depth(x, k):
    return moved(x, lambda y, zh, zl, c, d: (y, zh, zl, c, d + k))


def swap_zh(x):
    return moved(x, lambda y, zh, zl, c, d: (y, zh + 1, zl, c, d))


def swap_core(x):
    return moved(x, lambda y, zh, zl, c, d: (y, zh, zl, c + 1, d))


def split(p):
    high = p.astype(BF16).astype(F32)
    return high, p - high


def section_kernel(jobs, n_left, n_right, has_acc, *refs):
    place, pairs, counts = refs[:3]
    lefts = refs[3 : 3 + n_left]
    rights = refs[3 + n_left : 3 + n_left + n_right]
    rest = refs[3 + n_left + n_right :]
    if has_acc:
        start, rest = rest[0], rest[1:]
    out, lbuf, rbuf, a3, b3, sem, acc_sem = rest
    shift, core, depth = place[0], place[1], place[2]
    lane = lax.broadcasted_iota(jnp.int32, (32, 128), 1) < 64

    def section(job):
        k, odd = job[0], job[1]
        return lax.rem(2 * k + 9 - 2 * core, 8) if odd else 2 * k

    def fetch(j):
        k, odd, left, choices = jobs[j]
        slot = j % 2
        pltpu.make_async_copy(lefts[left], lbuf.at[slot], sem.at[slot, 0]).start()
        if len(choices) == 1:
            pltpu.make_async_copy(rights[choices[0][1]], rbuf.at[slot], sem.at[slot, 1]).start()
        else:
            want = lax.rem(k + shift + 4, 4)
            for offset, index in choices:

                @pl.when(want == offset)
                def _():
                    pltpu.make_async_copy(rights[index], rbuf.at[slot], sem.at[slot, 1]).start()

    def wait(j):
        slot = j % 2
        pltpu.make_async_copy(lefts[0], lbuf.at[slot], sem.at[slot, 0]).wait()
        pltpu.make_async_copy(rights[0], rbuf.at[slot], sem.at[slot, 1]).wait()

    fetch(0)
    if has_acc:
        load = pltpu.make_async_copy(start, out, acc_sem.at[0])
        load.start()
    else:
        out[...] = jnp.zeros_like(out)
    for j in range(len(jobs)):
        if j + 1 < len(jobs):
            fetch(j + 1)
        wait(j)
        slot = j % 2

        @pl.loop(0, TILES, unroll=4)
        def _(t):
            h, low = split(lbuf[slot, t])
            hr = pltpu.roll(h, 64, 1)
            lr = pltpu.roll(low, 64, 1)
            a3[t, 0:32, 0:128] = jnp.where(lane, h, hr).astype(BF16)
            a3[t, 32:64, 0:128] = jnp.where(lane, hr, h).astype(BF16)
            a3[t, 0:32, 128:256] = jnp.where(lane, low, lr).astype(BF16)
            a3[t, 32:64, 128:256] = jnp.where(lane, lr, low).astype(BF16)
            h, low = split(rbuf[slot, t])
            hr = pltpu.roll(h, 64, 1)
            lr = pltpu.roll(low, 64, 1)
            parts = (
                jnp.where(lane, h, hr).astype(BF16),
                jnp.where(lane, hr, h).astype(BF16),
                jnp.where(lane, low, lr).astype(BF16),
                jnp.where(lane, lr, low).astype(BF16),
            )
            for base in (0, 128):
                for i in range(4):
                    b3[t, base + 32 * i : base + 32 * i + 32] = parts[i]

        if j == 0 and has_acc:
            load.wait()
        s = section(jobs[j])
        live = counts[s]

        @pl.loop(0, (live + UNROLL - 1) // UNROLL)
        def _(block):
            sums, slots = [], []
            for u in range(UNROLL):
                p = block * UNROLL + u
                c = jnp.dot(a3[pairs[s, 0, p]], b3[pairs[s, 1, p]], preferred_element_type=F32)
                sums.append(jnp.where(lane, c[0:32], c[32:64]))
                g = lax.rem(pairs[s, 2, p] + (4 - depth) * 32, SLOTS)
                slots.append(jnp.where(p < live, g, SLOTS))
            for u in range(UNROLL):
                out[slots[u]] += sums[u]


def add_sections(jobs, place, pattern, limits, lefts, rights, acc, name):
    smem = pl.BlockSpec(memory_space=pltpu.SMEM)
    anywhere = pl.BlockSpec(memory_space=pl.ANY)
    operands = [place, pattern, limits, *lefts, *rights]
    specs = [smem] * 3 + [anywhere] * (len(lefts) + len(rights))
    if acc is not None:
        operands.append(acc)
        specs.append(anywhere)
    n = len(jobs)
    return pl.pallas_call(
        functools.partial(section_kernel, jobs, len(lefts), len(rights), acc is not None),
        out_shape=jax.ShapeDtypeStruct((SLOTS + 1, 32, 128), F32),
        in_specs=specs,
        out_specs=pl.BlockSpec(memory_space=pltpu.VMEM),
        scratch_shapes=[
            pltpu.VMEM((2, TILES, 32, 128), F32),
            pltpu.VMEM((2, TILES, 32, 128), F32),
            pltpu.VMEM((TILES, 64, 256), BF16),
            pltpu.VMEM((TILES, 256, 128), BF16),
            pltpu.SemaphoreType.DMA((2, 2)),
            pltpu.SemaphoreType.DMA((1,)),
        ],
        compiler_params=pltpu.CompilerParams(vmem_limit_bytes=24 << 20),
        cost_estimate=pl.CostEstimate(
            flops=n * 64 * 2 * 64 * 256 * 128, bytes_accessed=n * (1 << 20) + (4 << 20), transcendentals=0
        ),
        name=name,
    )(*operands)


def on_device(left_tiles, right_tiles, square_tiles, pairs, counts):
    row, col = lax.axis_index("row"), lax.axis_index("col")
    core = col % 2
    place = jnp.stack([row % 2 - core, core, lax.axis_index("depth")]).astype(jnp.int32)
    pattern, limits = pairs[0, 0, 0], counts[0, 0, 0]

    right = right_tiles[0, 0, 0, 0].reshape(TILES, 2, 32, 64).transpose(0, 2, 1, 3).reshape(TILES, 32, 128)
    left = left_tiles[0, 0, 0].reshape(TILES, 32, 128)

    other0 = swap_zh(right)
    left1 = by_zl(left, -1)
    same = [right, by_y(right, -1), by_y(right, 2), by_y(right, 1)]
    left2 = by_zl(left1, -1)
    other = [other0, by_y(other0, -1), by_y(other0, 2), by_y(other0, 1)]
    left3 = by_zl(left2, -1)
    mine = [left, left1, left2, left3]
    twin = [swap_core(x) for x in mine]

    choices = [(i, i) for i in range(4)]
    acc = add_sections([(0, False, 0, [(0, 0)]), (1, False, 1, [(1, 1)])], place, pattern, limits, mine[:2], same[:2], None, "first")
    jobs = [(2, False, 3, [(2, 4)])] + [(k, True, k, choices) for k in range(3)]
    acc = add_sections(jobs, place, pattern, limits, twin[:3] + [mine[2]], other + [same[2]], acc, "second")
    jobs = [(3, False, 1, [(3, 4)]), (3, True, 0, choices)]
    acc = add_sections(jobs, place, pattern, limits, [twin[3], mine[3]], other + [same[3]], acc, "third")

    share = acc[0:32]
    for k in range(1, 4):
        share = share + by_depth(acc[32 * k : 32 * k + 32], k)
    purified = 3.0 * square_tiles[0, 0] - 2.0 * share.reshape(TILES, 4096)
    return purified[None, None]


def solution(mesh):
    in_specs = (
        P("row", "col", "depth", None, None),
        P("row", "col", "depth", None, None, None),
        P("row", "col", "depth", None),
        P("row", "col", "depth", None, None, None),
        P("row", "col", "depth", None),
    )
    out_specs = P("row", "col", "depth", None)
    return jax.shard_map(
        on_device, mesh=mesh, in_specs=in_specs, out_specs=out_specs, check_vma=False
    )
```

time: 301 us -> 134 us (0.45)
  the two profiles are of different devices: /device:TPU:30 before, /device:TPU:81 now
where the time goes in v1:
time: 134 us
  waiting for transfers between devices  68.5 us (51%)
  starting transfers between devices  36.3 us (27%)
  Pallas kernels  16.8 us (13%)
  local copies, waits for them, and re-layouts  11 us (8%)
    ppermute x17, waiting for transfers between devices, moved(): return lax.ppermute(x, AXES, pairs)  68.5 us
    ppermute x17, starting transfers between devices, moved(): return lax.ppermute(x, AXES, pairs)  36.3 us
    pallas_call x3, Pallas kernels, add_sections(): pl.pallas_call(functools.partial(section_kernel, jobs, len(lefts), len(ri...  16.8 us
    unnamed x24, local copies, waits for them, and re-layouts  5.63 us
    another operation x2, local copies, waits for them, and re-layouts, on_device(): right_tiles[0, 0, 0, 0].reshape(TILES, 2, 32, 64).transpose(0, 2, 1, 3)  4.56 us
  transfers between devices with their start and end apart: 17, of which 6 were waited for; matrix products, arithmetic and copies ran while one was open for 4% of the time, Pallas kernels for 9%

profile of v1, /device:TPU:81, one launch (start us, length us, event | category | flops | bytes accessed | tf_op | source)
XLA Modules:
  0.0 134.0 jit_solution(12396562972151376372)
XLA Ops:
  0.0 1.1 copy.8
  1.1 0.1 collective-permute-start
  1.2 2.5 %reshape_squeeze.7 = f32[32,2,32,64]{3,2,1,0:T(8,128)} reshape(f32[1,1,1,1,32,4096]{5,4,3,2,1,0:T(8,128)} %param.6) | data formatting | bytes 1048576 | tf_op jit(solution)/shard_map/reshape;squeeze | solution.py:179
  3.7 2.1 %copy.11 = f32[32,2,32,64]{3,1,2,0:T(2,128)S(1)} copy(f32[32,2,32,64]{3,2,1,0:T(8,128)} %reshape_squeeze.7) | data formatting | bytes 1048576 | tf_op jit(solution)/shard_map/reshape;squeeze | solution.py:179
  5.8 0.6 reshape.16.refs_5_
  6.4 5.9 %collective-permute-start.4 = (f32[32,32,128]{2,1,0:T(8,128)S(1)}, f32[32,32,128]{2,1,0:T(8,128)S(1)}, u32[]{:S(2)}, u32[]{:S(2)}) collective-permute-start(f32[32,32,128]{2,1,0:T(8,128)S(1)} %reshape.16.refs_5_), channel_id=1, source_target_pairs={{0,32},{1,33},{2,34},{3,35},{4,36},{5,37},{6,38},{7,39},{8,40},{9,... | collective-permute-start | bytes 1572872 | tf_op jit(solution)/shard_map/ppermute | solution.py:29
  12.3 0.2 collective-permute-start.13
  12.5 1.9 %collective-permute-done.refs_4_ = f32[32,32,128]{2,1,0:T(8,128)S(1)} collective-permute-done((f32[32,32,128]{2,1,0:T(8,128)S(1)}, f32[32,32,128]{2,1,0:T(8,128)S(1)}, u32[]{:S(2)}, u32[]{:S(2)}) %collective-permute-start) | collective-permute-done | bytes 524320 | tf_op jit(solution)/shard_map/ppermute | solution.py:29
  14.4 0.0 collective-permute-start.1
  14.4 1.4 %collective-permute-start.12 = (f32[32,32,128]{2,1,0:T(8,128)S(1)}, f32[32,32,128]{2,1,0:T(8,128)S(1)}, u32[]{:S(2)}, u32[]{:S(2)}) collective-permute-start(f32[32,32,128]{2,1,0:T(8,128)S(1)} %reshape.16.refs_5_), channel_id=1, source_target_pairs={{0,128},{1,129},{2,130},{3,131},{4,132},{5,133},{6,134},{7,135},{8... | collective-permute-start | bytes 1572872 | tf_op jit(solution)/shard_map/ppermute | solution.py:29
  15.8 2.1 %collective-permute-start.9 = (f32[32,32,128]{2,1,0:T(8,128)S(1)}, f32[32,32,128]{2,1,0:T(8,128)S(1)}, u32[]{:S(2)}, u32[]{:S(2)}) collective-permute-start(f32[32,32,128]{2,1,0:T(8,128)S(1)} %bitcast.17), channel_id=1, source_target_pairs={{0,4},{1,5},{2,6},{3,7},{4,0},{5,1},{6,2},{7,3},{8,12},{9,13},{10,... | collective-permute-start | bytes 1572872 | tf_op jit(solution)/shard_map/ppermute | solution.py:29
  17.9 37.0 %collective-permute-done.4.refs_7_.refs_5_ = f32[32,32,128]{2,1,0:T(8,128)S(1)} collective-permute-done((f32[32,32,128]{2,1,0:T(8,128)S(1)}, f32[32,32,128]{2,1,0:T(8,128)S(1)}, u32[]{:S(2)}, u32[]{:S(2)}) %collective-permute-start.4) | collective-permute-done | bytes 524320 | tf_op jit(solution)/shard_map/ppermute | solution.py:29
  54.9 0.2 collective-permute-start.5
  55.1 0.0 collective-permute-done.13.refs_6_
  55.1 0.8 copy-done.4
  55.9 2.6 %collective-permute-start.6 = (f32[32,32,128]{2,1,0:T(8,128)S(1)}, f32[32,32,128]{2,1,0:T(8,128)S(1)}, u32[]{:S(2)}, u32[]{:S(2)}) collective-permute-start(f32[32,32,128]{2,1,0:T(8,128)S(1)} %collective-permute-done.4.refs_7_.refs_5_), channel_id=1, source_target_pairs={{0,128},{1,129},{2,130},{3,131},{4,132},{5,133},{6,134},{7,135},{8... | collective-permute-start | bytes 1572872 | tf_op jit(solution)/shard_map/ppermute | solution.py:29
  58.6 0.0 collective-permute-done.1.refs_6_
  58.6 0.0 collective-permute-start.2
  58.6 0.0 collective-permute-done.12.refs_11_
  58.6 0.8 copy-done.2
  59.4 0.0 collective-permute-start.7
  59.4 0.0 collective-permute-done.9.refs_3_
  59.4 0.8 copy-done.6
  60.2 1.2 collective-permute-start.10
  61.3 6.6 %collective-permute-done.5.refs_8_.refs_6_ = f32[32,32,128]{2,1,0:T(8,128)S(1)} collective-permute-done((f32[32,32,128]{2,1,0:T(8,128)S(1)}, f32[32,32,128]{2,1,0:T(8,128)S(1)}, u32[]{:S(2)}, u32[]{:S(2)}) %collective-permute-start.5) | collective-permute-done | bytes 524320 | tf_op jit(solution)/shard_map/ppermute | solution.py:29
  67.9 2.4 %collective-permute-start.11 = (f32[32,32,128]{2,1,0:T(8,128)}, f32[32,32,128]{2,1,0:T(8,128)}, u32[]{:S(2)}, u32[]{:S(2)}) collective-permute-start(f32[32,32,128]{2,1,0:T(8,128)} %collective-permute-done.1.refs_6_), channel_id=1, source_target_pairs={{0,4},{1,5},{2,6},{3,7},{4,0},{5,1},{6,2},{7,3},{8,12},{9,13},{10,... | collective-permute-start | bytes 1572872 | tf_op jit(solution)/shard_map/ppermute | solution.py:29
  70.3 12.4 %collective-permute-start.8 = (f32[32,32,128]{2,1,0:T(8,128)S(1)}, f32[32,32,128]{2,1,0:T(8,128)}, u32[]{:S(2)}, u32[]{:S(2)}) collective-permute-start(f32[32,32,128]{2,1,0:T(8,128)S(1)} %reshape.16.refs_5_), channel_id=1, source_target_pairs={{0,64},{1,65},{2,66},{3,67},{4,68},{5,69},{6,70},{7,71},{8,72},{9,... | collective-permute-start | bytes 1572872 | tf_op jit(solution)/shard_map/ppermute | solution.py:29
  82.7 0.3 collective-permute-start.3
  83.0 0.1 pad_add_fusion.refs_0_
  83.1 1.0 copy-done.1
  84.2 1.0 copy-done.5
  85.2 4.2 %first.1.refs_12_ = f32[129,32,128]{2,1,0:T(8,128)S(1)} custom-call(s32[3]{0:T(128)S(1)} %pad_add_fusion.refs_0_, s32[8,3,64]{2,1,0:T(4,128)S(1)} %bitcast.19, s32[8]{0:T(128)S(1)} %bitcast.22, f32[32,32,128]{2,1,0:T(8,128)S(1)} %bitcast.18, f32[32,32,128]{2,1,0:T(8,128)S(1)} %copy-done.1, f32[32,32,128]{2,1,0:T(8,128)S(1)} %reshape.16.refs_5_, ...), custom_call_target="tpu_custom_call" | custom-call | flops 536870912 | bytes 6291456 | tf_op jit(solution)/shard_map/first/pallas_call | solution.py:152
  89.4 0.0 collective-permute-done.7.refs_10_.refs_8_
  89.4 0.0 collective-permute-done.10.refs_4_
  89.4 7.7 %second.1.refs_10_ = f32[129,32,128]{2,1,0:T(8,128)S(1)} custom-call(s32[3]{0:T(128)S(1)} %pad_add_fusion.refs_0_, s32[8,3,64]{2,1,0:T(4,128)S(1)} %bitcast.20, s32[8]{0:T(128)S(1)} %bitcast.23, f32[32,32,128]{2,1,0:T(8,128)S(1)} %copy-done.7, f32[32,32,128]{2,1,0:T(8,128)} %collective-permute-done.10.refs_4_, ...), custom_call_target="tpu_custom_call" | custom-call | flops 1073741824 | bytes 8388608 | tf_op jit(solution)/shard_map/second/pallas_call | solution.py:152
  97.2 0.0 collective-permute-done.8.refs_9_
  97.2 0.0 collective-permute-done.3.refs_3_
  97.2 4.9 %third.1 = f32[129,32,128]{2,1,0:T(8,128)S(1)} custom-call(s32[3]{0:T(128)S(1)} %pad_add_fusion.refs_0_, s32[8,3,64]{2,1,0:T(4,128)S(1)} %bitcast.21, s32[8]{0:T(128)S(1)} %bitcast.24, f32[32,32,128]{2,1,0:T(8,128)} %collective-permute-done.3.refs_3_, f32[32,32,128]{2,1,0:T(8,128)} %collective-permute-done.2.refs_4_, ...), custom_call_target="tpu_custom_call" | custom-call | flops 536870912 | bytes 6291456 | tf_op jit(solution)/shard_map/third/pallas_call | solution.py:152
  102.1 0.1 fusion.3
  102.3 0.0 copy-start.9
  102.3 1.2 collective-permute-start.14
  103.5 6.4 %collective-permute-start.15 = (f32[32,32,128]{2,1,0:T(8,128)S(1)}, f32[32,32,128]{2,1,0:T(8,128)S(1)}, u32[]{:S(2)}, u32[]{:S(2)}) collective-permute-start(f32[32,32,128]{2,1,0:T(8,128)S(1)} %get-tuple-element.7), channel_id=1, source_target_pairs={{0,2},{1,3},{2,0},{3,1},{4,6},{5,7},{6,4},{7,5},{8,10},{9,11},{10,... | collective-permute-start | bytes 1572872 | tf_op jit(solution)/shard_map/ppermute | solution.py:29
  109.9 7.9 %collective-permute-done.14 = f32[32,32,128]{2,1,0:T(8,128)S(1)} collective-permute-done((f32[32,32,128]{2,1,0:T(8,128)S(1)}, f32[32,32,128]{2,1,0:T(8,128)S(1)}, u32[]{:S(2)}, u32[]{:S(2)}) %collective-permute-start.14) | collective-permute-done | bytes 524320 | tf_op jit(solution)/shard_map/ppermute | solution.py:29
  117.7 14.9 %collective-permute-done.15 = f32[32,32,128]{2,1,0:T(8,128)S(1)} collective-permute-done((f32[32,32,128]{2,1,0:T(8,128)S(1)}, f32[32,32,128]{2,1,0:T(8,128)S(1)}, u32[]{:S(2)}, u32[]{:S(2)}) %collective-permute-start.15) | collective-permute-done | bytes 524320 | tf_op jit(solution)/shard_map/ppermute | solution.py:29
  132.7 0.1 collective-permute-done.16
  132.8 0.2 fusion.2
  133.0 0.1 mul.27
  133.2 0.8 multiply_subtract_fusion
  (21 shorter events, 0.0 us)
Async XLA Ops:
  1.1 13.2 %collective-permute-start = (f32[32,32,128]{2,1,0:T(8,128)S(1)}, f32[32,32,128]{2,1,0:T(8,128)S(1)}, u32[]{:S(2)}, u32[]{:S(2)}) collective-permute-start(f32[32,32,128]{2,1,0:T(8,128)S(1)} %bitcast.16), channel_id=1, source_target_pairs={{0,24},{1,25},{2,26},{3,27},{4,28},{5,29},{6,30},{7,31},{8,0},{9,1... | collective-permute-start | bytes 1572872 | tf_op jit(solution)/shard_map/ppermute | solution.py:29
  3.7 79.3 %copy-start.10 = (s32[1,1,1,8,3,64]{5,3,4,2,1,0:T(8,128)S(1)}, s32[1,1,1,8,3,64]{5,3,4,2,1,0:T(8,128)}, u32[]{:S(2)}) copy-start(s32[1,1,1,8,3,64]{5,3,4,2,1,0:T(8,128)} %param.8) | copy-start | bytes 18436
  3.7 79.4 %copy-start.8 = (s32[1,1,1,8]{3,2,1,0:T(1,128)S(1)}, s32[1,1,1,8]{3,2,1,0:T(1,128)}, u32[]{:S(2)}) copy-start(s32[1,1,1,8]{3,2,1,0:T(1,128)} %param.9) | copy-start | bytes 100
  6.4 48.6 %collective-permute-start.4 = (f32[32,32,128]{2,1,0:T(8,128)S(1)}, f32[32,32,128]{2,1,0:T(8,128)S(1)}, u32[]{:S(2)}, u32[]{:S(2)}) collective-permute-start(f32[32,32,128]{2,1,0:T(8,128)S(1)} %reshape.16.refs_5_), channel_id=1, source_target_pairs={{0,32},{1,33},{2,34},{3,35},{4,36},{5,37},{6,38},{7,39},{8,40},{9,... | collective-permute-start | bytes 1572872 | tf_op jit(solution)/shard_map/ppermute | solution.py:29
  12.3 42.8 %collective-permute-start.13 = (f32[32,32,128]{2,1,0:T(8,128)S(1)}, f32[32,32,128]{2,1,0:T(8,128)S(1)}, u32[]{:S(2)}, u32[]{:S(2)}) collective-permute-start(f32[32,32,128]{2,1,0:T(8,128)S(1)} %reshape.16.refs_5_), channel_id=1, source_target_pairs={{0,192},{1,193},{2,194},{3,195},{4,196},{5,197},{6,198},{7,199},{8... | collective-permute-start | bytes 1572872 | tf_op jit(solution)/shard_map/ppermute | solution.py:29
  14.4 44.2 %copy-start = (f32[32,32,128]{2,1,0:T(8,128)}, f32[32,32,128]{2,1,0:T(8,128)S(1)}, u32[]{:S(2)}) copy-start(f32[32,32,128]{2,1,0:T(8,128)S(1)} %collective-permute-done.refs_4_) | copy-start | bytes 1572868
  14.4 44.2 %collective-permute-start.1 = (f32[32,32,128]{2,1,0:T(8,128)S(1)}, f32[32,32,128]{2,1,0:T(8,128)}, u32[]{:S(2)}, u32[]{:S(2)}) collective-permute-start(f32[32,32,128]{2,1,0:T(8,128)S(1)} %collective-permute-done.refs_4_), channel_id=1, source_target_pairs={{0,24},{1,25},{2,26},{3,27},{4,28},{5,29},{6,30},{7,31},{8,0},{9,1... | collective-permute-start | bytes 1572872 | tf_op jit(solution)/shard_map/ppermute | solution.py:29
  14.4 44.2 %collective-permute-start.12 = (f32[32,32,128]{2,1,0:T(8,128)S(1)}, f32[32,32,128]{2,1,0:T(8,128)S(1)}, u32[]{:S(2)}, u32[]{:S(2)}) collective-permute-start(f32[32,32,128]{2,1,0:T(8,128)S(1)} %reshape.16.refs_5_), channel_id=1, source_target_pairs={{0,128},{1,129},{2,130},{3,131},{4,132},{5,133},{6,134},{7,135},{8... | collective-permute-start | bytes 1572872 | tf_op jit(solution)/shard_map/ppermute | solution.py:29
  15.8 43.5 %collective-permute-start.9 = (f32[32,32,128]{2,1,0:T(8,128)S(1)}, f32[32,32,128]{2,1,0:T(8,128)S(1)}, u32[]{:S(2)}, u32[]{:S(2)}) collective-permute-start(f32[32,32,128]{2,1,0:T(8,128)S(1)} %bitcast.17), channel_id=1, source_target_pairs={{0,4},{1,5},{2,6},{3,7},{4,0},{5,1},{6,2},{7,3},{8,12},{9,13},{10,... | collective-permute-start | bytes 1572872 | tf_op jit(solution)/shard_map/ppermute | solution.py:29
  54.9 13.0 %collective-permute-start.5 = (f32[32,32,128]{2,1,0:T(8,128)S(1)}, f32[32,32,128]{2,1,0:T(8,128)S(1)}, u32[]{:S(2)}, u32[]{:S(2)}) collective-permute-start(f32[32,32,128]{2,1,0:T(8,128)S(1)} %collective-permute-done.4.refs_7_.refs_5_), channel_id=1, source_target_pairs={{0,192},{1,193},{2,194},{3,195},{4,196},{5,197},{6,198},{7,199},{8... | collective-permute-start | bytes 1572872 | tf_op jit(solution)/shard_map/ppermute | solution.py:29
  55.1 0.8 copy-start.4
  55.9 14.4 %collective-permute-start.6 = (f32[32,32,128]{2,1,0:T(8,128)S(1)}, f32[32,32,128]{2,1,0:T(8,128)S(1)}, u32[]{:S(2)}, u32[]{:S(2)}) collective-permute-start(f32[32,32,128]{2,1,0:T(8,128)S(1)} %collective-permute-done.4.refs_7_.refs_5_), channel_id=1, source_target_pairs={{0,128},{1,129},{2,130},{3,131},{4,132},{5,133},{6,134},{7,135},{8... | collective-permute-start | bytes 1572872 | tf_op jit(solution)/shard_map/ppermute | solution.py:29
  58.6 24.2 %collective-permute-start.2 = (f32[32,32,128]{2,1,0:T(8,128)}, f32[32,32,128]{2,1,0:T(8,128)}, u32[]{:S(2)}, u32[]{:S(2)}) collective-permute-start(f32[32,32,128]{2,1,0:T(8,128)} %collective-permute-done.1.refs_6_), channel_id=1, source_target_pairs={{0,24},{1,25},{2,26},{3,27},{4,28},{5,29},{6,30},{7,31},{8,0},{9,1... | collective-permute-start | bytes 1572872 | tf_op jit(solution)/shard_map/ppermute | solution.py:29
  58.6 0.8 copy-start.2
  59.4 30.0 %collective-permute-start.7 = (f32[32,32,128]{2,1,0:T(8,128)S(1)}, f32[32,32,128]{2,1,0:T(8,128)S(1)}, u32[]{:S(2)}, u32[]{:S(2)}) collective-permute-start(f32[32,32,128]{2,1,0:T(8,128)S(1)} %collective-permute-done.4.refs_7_.refs_5_), channel_id=1, source_target_pairs={{0,64},{1,65},{2,66},{3,67},{4,68},{5,69},{6,70},{7,71},{8,72},{9,... | collective-permute-start | bytes 1572872 | tf_op jit(solution)/shard_map/ppermute | solution.py:29
  59.4 0.8 copy-start.6
  60.2 29.2 %collective-permute-start.10 = (f32[32,32,128]{2,1,0:T(8,128)}, f32[32,32,128]{2,1,0:T(8,128)}, u32[]{:S(2)}, u32[]{:S(2)}) collective-permute-start(f32[32,32,128]{2,1,0:T(8,128)} %copy-done), channel_id=1, source_target_pairs={{0,4},{1,5},{2,6},{3,7},{4,0},{5,1},{6,2},{7,3},{8,12},{9,13},{10,... | collective-permute-start | bytes 1572872 | tf_op jit(solution)/shard_map/ppermute | solution.py:29
  67.9 21.5 %collective-permute-start.11 = (f32[32,32,128]{2,1,0:T(8,128)}, f32[32,32,128]{2,1,0:T(8,128)}, u32[]{:S(2)}, u32[]{:S(2)}) collective-permute-start(f32[32,32,128]{2,1,0:T(8,128)} %collective-permute-done.1.refs_6_), channel_id=1, source_target_pairs={{0,4},{1,5},{2,6},{3,7},{4,0},{5,1},{6,2},{7,3},{8,12},{9,13},{10,... | collective-permute-start | bytes 1572872 | tf_op jit(solution)/shard_map/ppermute | solution.py:29
  70.3 26.8 %collective-permute-start.8 = (f32[32,32,128]{2,1,0:T(8,128)S(1)}, f32[32,32,128]{2,1,0:T(8,128)}, u32[]{:S(2)}, u32[]{:S(2)}) collective-permute-start(f32[32,32,128]{2,1,0:T(8,128)S(1)} %reshape.16.refs_5_), channel_id=1, source_target_pairs={{0,64},{1,65},{2,66},{3,67},{4,68},{5,69},{6,70},{7,71},{8,72},{9,... | collective-permute-start | bytes 1572872 | tf_op jit(solution)/shard_map/ppermute | solution.py:29
  82.7 14.5 %collective-permute-start.3 = (f32[32,32,128]{2,1,0:T(8,128)}, f32[32,32,128]{2,1,0:T(8,128)}, u32[]{:S(2)}, u32[]{:S(2)}) collective-permute-start(f32[32,32,128]{2,1,0:T(8,128)} %collective-permute-done.2.refs_4_), channel_id=1, source_target_pairs={{0,4},{1,5},{2,6},{3,7},{4,0},{5,1},{6,2},{7,3},{8,12},{9,13},{10,... | collective-permute-start | bytes 1572872 | tf_op jit(solution)/shard_map/ppermute | solution.py:29
  83.1 1.0 copy-start.1
  84.2 1.0 copy-start.5
  85.2 4.2 %copy-start.3 = (f32[32,32,128]{2,1,0:T(8,128)S(1)}, f32[32,32,128]{2,1,0:T(8,128)}, u32[]{:S(2)}) copy-start(f32[32,32,128]{2,1,0:T(8,128)} %copy-done.2) | copy-start | bytes 1572868
  85.2 4.2 %copy-start.7 = (f32[32,32,128]{2,1,0:T(8,128)S(1)}, f32[32,32,128]{2,1,0:T(8,128)}, u32[]{:S(2)}) copy-start(f32[32,32,128]{2,1,0:T(8,128)} %copy-done.6) | copy-start | bytes 1572868
  102.3 30.9 %copy-start.9 = (f32[1,1,32,4096]{3,2,1,0:T(8,128)S(1)}, f32[1,1,32,4096]{3,2,1,0:T(8,128)}, u32[]{:S(2)}) copy-start(f32[1,1,32,4096]{3,2,1,0:T(8,128)} %param.7) | copy-start | bytes 1572868
  102.3 15.5 %collective-permute-start.14 = (f32[32,32,128]{2,1,0:T(8,128)S(1)}, f32[32,32,128]{2,1,0:T(8,128)S(1)}, u32[]{:S(2)}, u32[]{:S(2)}) collective-permute-start(f32[32,32,128]{2,1,0:T(8,128)S(1)} %get-tuple-element.5), channel_id=1, source_target_pairs={{0,1},{1,2},{2,3},{3,0},{4,5},{5,6},{6,7},{7,4},{8,9},{9,10},{10,1... | collective-permute-start | bytes 1572872 | tf_op jit(solution)/shard_map/ppermute | solution.py:29
  103.5 29.2 %collective-permute-start.15 = (f32[32,32,128]{2,1,0:T(8,128)S(1)}, f32[32,32,128]{2,1,0:T(8,128)S(1)}, u32[]{:S(2)}, u32[]{:S(2)}) collective-permute-start(f32[32,32,128]{2,1,0:T(8,128)S(1)} %get-tuple-element.7), channel_id=1, source_target_pairs={{0,2},{1,3},{2,0},{3,1},{4,6},{5,7},{6,4},{7,5},{8,10},{9,11},{10,... | collective-permute-start | bytes 1572872 | tf_op jit(solution)/shard_map/ppermute | solution.py:29
  109.9 22.9 %collective-permute-start.16 = (f32[32,32,128]{2,1,0:T(8,128)S(1)}, f32[32,32,128]{2,1,0:T(8,128)S(1)}, u32[]{:S(2)}, u32[]{:S(2)}) collective-permute-start(f32[32,32,128]{2,1,0:T(8,128)S(1)} %get-tuple-element.6), channel_id=1, source_target_pairs={{0,3},{1,0},{2,1},{3,2},{4,7},{5,4},{6,5},{7,6},{8,11},{9,8},{10,9... | collective-permute-start | bytes 1572872 | tf_op jit(solution)/shard_map/ppermute | solution.py:29

commit v2 on v1

--- a/solution.py
+++ b/solution.py
@@ -61,7 +61,7 @@
     rest = refs[3 + n_left + n_right :]
     if has_acc:
         start, rest = rest[0], rest[1:]
-    out, lbuf, rbuf, a3, b3, sem, acc_sem = rest
+    out, lbuf, rbuf, rows, a3, b3, sem, acc_sem = rest
     shift, core, depth = place[0], place[1], place[2]
     lane = lax.broadcasted_iota(jnp.int32, (32, 128), 1) < 64
 
@@ -109,18 +109,20 @@
             a3[t, 32:64, 0:128] = jnp.where(lane, hr, h).astype(BF16)
             a3[t, 0:32, 128:256] = jnp.where(lane, low, lr).astype(BF16)
             a3[t, 32:64, 128:256] = jnp.where(lane, lr, low).astype(BF16)
-            h, low = split(rbuf[slot, t])
-            hr = pltpu.roll(h, 64, 1)
-            lr = pltpu.roll(low, 64, 1)
-            parts = (
-                jnp.where(lane, h, hr).astype(BF16),
-                jnp.where(lane, hr, h).astype(BF16),
-                jnp.where(lane, low, lr).astype(BF16),
-                jnp.where(lane, lr, low).astype(BF16),
-            )
-            for base in (0, 128):
-                for i in range(4):
-                    b3[t, base + 32 * i : base + 32 * i + 32] = parts[i]
+            r = rbuf[slot, t]
+            rr = pltpu.roll(r, 64, 1)
+            rows[t, pl.ds(0, 32, stride=2)] = jnp.where(lane, r, rr)
+            rows[t, pl.ds(1, 32, stride=2)] = jnp.where(lane, rr, r)
+
+        @pl.loop(0, TILES, unroll=4)
+        def _(t):
+            h, low = split(rows[t])
+            h = h.astype(BF16)
+            low = low.astype(BF16)
+            b3[t, 0:64] = h
+            b3[t, 64:128] = low
+            b3[t, 128:192] = h
+            b3[t, 192:256] = low
 
         if j == 0 and has_acc:
             load.wait()
@@ -140,7 +142,7 @@
                 out[slots[u]] += sums[u]
 
 
-def add_sections(jobs, place, pattern, limits, lefts, rights, acc, name):
+def add_sections(jobs, place, pattern, limits, lefts, rights, acc, name, weight=1):
     smem = pl.BlockSpec(memory_space=pltpu.SMEM)
     anywhere = pl.BlockSpec(memory_space=pl.ANY)
     operands = [place, pattern, limits, *lefts, *rights]
@@ -157,6 +159,7 @@
         scratch_shapes=[
             pltpu.VMEM((2, TILES, 32, 128), F32),
             pltpu.VMEM((2, TILES, 32, 128), F32),
+            pltpu.VMEM((TILES, 64, 128), F32),
             pltpu.VMEM((TILES, 64, 256), BF16),
             pltpu.VMEM((TILES, 256, 128), BF16),
             pltpu.SemaphoreType.DMA((2, 2)),
@@ -164,10 +167,18 @@
         ],
         compiler_params=pltpu.CompilerParams(vmem_limit_bytes=24 << 20),
         cost_estimate=pl.CostEstimate(
-            flops=n * 64 * 2 * 64 * 256 * 128, bytes_accessed=n * (1 << 20) + (4 << 20), transcendentals=0
+            flops=weight * n * 64 * 2 * 64 * 256 * 128, bytes_accessed=n * (1 << 20) + (4 << 20), transcendentals=0
         ),
         name=name,
     )(*operands)
+
+
+def reduce_over_depth(acc):
+    up = by_depth(acc[48:80], 1)
+    down = by_depth(acc[80:112], -1)
+    up2 = by_depth(acc[32:48] + up[16:32], 1)
+    down2 = by_depth(acc[112:128] + down[0:16], -1)
+    return jnp.concatenate([acc[0:16] + down[16:32] + up2, acc[16:32] + up[0:16] + down2])
 
 
 def on_device(left_tiles, right_tiles, square_tiles, pairs, counts):
@@ -176,28 +187,35 @@
     place = jnp.stack([row % 2 - core, core, lax.axis_index("depth")]).astype(jnp.int32)
     pattern, limits = pairs[0, 0, 0], counts[0, 0, 0]
 
-    right = right_tiles[0, 0, 0, 0].reshape(TILES, 2, 32, 64).transpose(0, 2, 1, 3).reshape(TILES, 32, 128)
+    right = right_tiles[0, 0, 0, 0].reshape(TILES, 32, 128)
     left = left_tiles[0, 0, 0].reshape(TILES, 32, 128)
 
+    args = (place, pattern, limits)
+    choices = [(i, i) for i in range(4)]
     other0 = swap_zh(right)
     left1 = by_zl(left, -1)
-    same = [right, by_y(right, -1), by_y(right, 2), by_y(right, 1)]
+    same1, same3, same2 = by_y(right, -1), by_y(right, 1), by_y(right, 2)
     left2 = by_zl(left1, -1)
-    other = [other0, by_y(other0, -1), by_y(other0, 2), by_y(other0, 1)]
+    twin0 = swap_core(left)
+    jobs = [(0, False, 0, [(0, 0)]), (1, False, 1, [(1, 1)])]
+    acc = add_sections(jobs, *args, [left, left1], [right, same1], None, "first")
+    other0, acc, same2, same3 = lax.optimization_barrier((other0, acc, same2, same3))
+
+    other1, other3, other2 = by_y(other0, -1), by_y(other0, 1), by_y(other0, 2)
     left3 = by_zl(left2, -1)
-    mine = [left, left1, left2, left3]
-    twin = [swap_core(x) for x in mine]
-
-    choices = [(i, i) for i in range(4)]
-    acc = add_sections([(0, False, 0, [(0, 0)]), (1, False, 1, [(1, 1)])], place, pattern, limits, mine[:2], same[:2], None, "first")
-    jobs = [(2, False, 3, [(2, 4)])] + [(k, True, k, choices) for k in range(3)]
-    acc = add_sections(jobs, place, pattern, limits, twin[:3] + [mine[2]], other + [same[2]], acc, "second")
+    twin1 = swap_core(left1)
+    twin2 = swap_core(left2)
+    acc = add_sections([(2, False, 0, [(2, 0)])], *args, [left2], [same2], acc, "second")
+
+    other = [other0, other1, other2, other3]
+    jobs = [(k, True, k, choices) for k in range(3)]
+    acc = add_sections(jobs, *args, [twin0, twin1, twin2], other, acc, "third")
+
+    left3, acc = lax.optimization_barrier((left3, acc))
+    twin3 = swap_core(left3)
     jobs = [(3, False, 1, [(3, 4)]), (3, True, 0, choices)]
-    acc = add_sections(jobs, place, pattern, limits, [twin[3], mine[3]], other + [same[3]], acc, "third")
-
-    share = acc[0:32]
-    for k in range(1, 4):
-        share = share + by_depth(acc[32 * k : 32 * k + 32], k)
+    acc = add_sections(jobs, *args, [twin3, left3], other + [same3], acc, "fourth")
+    share = reduce_over_depth(acc)
     purified = 3.0 * square_tiles[0, 0] - 2.0 * share.reshape(TILES, 4096)
     return purified[None, None]
 

time: 134 us -> 131 us (0.978)
  the two profiles are of different devices: /device:TPU:81 before, /device:TPU:72 now
where the time goes in v2:
time: 131 us; the launch traced here: 129 us
  waiting for transfers between devices  85 us (65%)
  starting transfers between devices  20.5 us (16%)
  Pallas kernels  17.9 us (14%)
  local copies, waits for them, and re-layouts  4.32 us (3%)
    ppermute x18, waiting for transfers between devices, moved(): return lax.ppermute(x, AXES, pairs)  85 us
    ppermute x18, starting transfers between devices, moved(): return lax.ppermute(x, AXES, pairs)  20.5 us
    pallas_call x4, Pallas kernels, add_sections(): pl.pallas_call(functools.partial(section_kernel, jobs, len(lefts), len(ri...  17.9 us
    unnamed x13, local copies, waits for them, and re-layouts  4.15 us
  transfers between devices with their start and end apart: 18, of which 11 were waited for; matrix products, arithmetic and copies ran while one was open for 1% of the time, Pallas kernels for 11%

profile of v2, /device:TPU:72, one launch (start us, length us, event | category | flops | bytes accessed | tf_op | source)
XLA Modules:
  0.0 129.0 jit_solution(7315027839748222526)
XLA Ops:
  0.0 1.2 copy.8
  1.2 1.7 %collective-permute-start.9 = (f32[32,32,128]{2,1,0:T(8,128)S(1)}, f32[32,32,128]{2,1,0:T(8,128)S(1)}, u32[]{:S(2)}, u32[]{:S(2)}) collective-permute-start(f32[32,32,128]{2,1,0:T(8,128)S(1)} %bitcast.18), channel_id=1, source_target_pairs={{0,64},{1,65},{2,66},{3,67},{4,68},{5,69},{6,70},{7,71},{8,72},{9,... | collective-permute-start | bytes 1572872 | tf_op jit(solution)/shard_map/ppermute | solution.py:29
  2.8 1.1 copy.7
  4.0 0.2 collective-permute-start
  4.1 0.5 collective-permute-start.7
  4.6 2.3 %collective-permute-start.8 = (f32[32,32,128]{2,1,0:T(8,128)S(1)}, f32[32,32,128]{2,1,0:T(8,128)}, u32[]{:S(2)}, u32[]{:S(2)}) collective-permute-start(f32[32,32,128]{2,1,0:T(8,128)S(1)} %bitcast.20), channel_id=1, source_target_pairs={{0,128},{1,129},{2,130},{3,131},{4,132},{5,133},{6,134},{7,135},{8... | collective-permute-start | bytes 1572872 | tf_op jit(solution)/shard_map/ppermute | solution.py:29
  6.9 6.3 %collective-permute-start.6 = (f32[32,32,128]{2,1,0:T(8,128)S(1)}, f32[32,32,128]{2,1,0:T(8,128)S(1)}, u32[]{:S(2)}, u32[]{:S(2)}) collective-permute-start(f32[32,32,128]{2,1,0:T(8,128)S(1)} %bitcast.21), channel_id=1, source_target_pairs={{0,32},{1,33},{2,34},{3,35},{4,36},{5,37},{6,38},{7,39},{8,40},{9,... | collective-permute-start | bytes 1572872 | tf_op jit(solution)/shard_map/ppermute | solution.py:29
  13.2 2.9 %collective-permute-done.9.refs_9_ = f32[32,32,128]{2,1,0:T(8,128)S(1)} collective-permute-done((f32[32,32,128]{2,1,0:T(8,128)S(1)}, f32[32,32,128]{2,1,0:T(8,128)S(1)}, u32[]{:S(2)}, u32[]{:S(2)}) %collective-permute-start.9) | collective-permute-done | bytes 524320 | tf_op jit(solution)/shard_map/ppermute | solution.py:29
  16.1 0.0 collective-permute-start.3
  16.1 2.9 %collective-permute-done.refs_4_ = f32[32,32,128]{2,1,0:T(8,128)} collective-permute-done((f32[32,32,128]{2,1,0:T(8,128)S(1)}, f32[32,32,128]{2,1,0:T(8,128)}, u32[]{:S(2)}, u32[]{:S(2)}) %collective-permute-start) | collective-permute-done | bytes 524320 | tf_op jit(solution)/shard_map/ppermute | solution.py:29
  19.0 0.0 collective-permute-start.1
  19.0 0.0 collective-permute-done.7.refs_6_
  19.0 0.8 copy-done
  19.8 0.0 collective-permute-start.4
  19.8 0.1 pad_add_fusion.refs_0_
  19.9 1.0 copy-done.1
  20.9 4.1 %first.1.refs_5_ = f32[129,32,128]{2,1,0:T(8,128)S(1)} custom-call(s32[3]{0:T(128)S(1)} %pad_add_fusion.refs_0_, s32[8,3,64]{2,1,0:T(4,128)S(1)} %bitcast.23, s32[8]{0:T(128)S(1)} %bitcast.27, f32[32,32,128]{2,1,0:T(8,128)S(1)} %bitcast.17, f32[32,32,128]{2,1,0:T(8,128)} %collective-permute-done.refs_4_, f32[32,32,128]{2,1,0:T(8,128)S(1)} %bitcast.22, ...), custom_call_target="tpu_custom_call" | custom-call | flops 536870912 | bytes 6291456 | tf_op jit(solution)/shard_map/first/pallas_call | solution.py:154
  25.1 4.5 %collective-permute-done.8.refs_4_ = f32[32,32,128]{2,1,0:T(8,128)} collective-permute-done((f32[32,32,128]{2,1,0:T(8,128)S(1)}, f32[32,32,128]{2,1,0:T(8,128)}, u32[]{:S(2)}, u32[]{:S(2)}) %collective-permute-start.8) | collective-permute-done | bytes 524320 | tf_op jit(solution)/shard_map/ppermute | solution.py:29
  29.6 27.8 %collective-permute-done.6.refs_6_.refs_5_ = f32[32,32,128]{2,1,0:T(8,128)S(1)} collective-permute-done((f32[32,32,128]{2,1,0:T(8,128)S(1)}, f32[32,32,128]{2,1,0:T(8,128)S(1)}, u32[]{:S(2)}, u32[]{:S(2)}) %collective-permute-start.6) | collective-permute-done | bytes 524320 | tf_op jit(solution)/shard_map/ppermute | solution.py:29
  57.4 1.3 collective-permute-start.12
  58.7 1.2 collective-permute-start.11
  59.9 1.1 collective-permute-start.10
  61.1 0.0 collective-permute-done.1.refs_3_
  61.1 0.0 collective-permute-start.5
  61.1 0.1 collective-permute-start.2
  61.2 3.5 %second.1.refs_10_ = f32[129,32,128]{2,1,0:T(8,128)S(1)} custom-call(s32[3]{0:T(128)S(1)} %pad_add_fusion.refs_0_, s32[8,3,64]{2,1,0:T(4,128)S(1)} %bitcast.24, s32[8]{0:T(128)S(1)} %bitcast.28, f32[32,32,128]{2,1,0:T(8,128)S(1)} %collective-permute-done.1.refs_3_, f32[32,32,128]{2,1,0:T(8,128)} %collective-permute-done.8.refs_4_, ...), custom_call_target="tpu_custom_call" | custom-call | flops 268435456 | bytes 5242880 | tf_op jit(solution)/shard_map/second/pallas_call | solution.py:154
  64.6 7.6 %collective-permute-done.12.refs_9_.refs_8_ = f32[32,32,128]{2,1,0:T(8,128)S(1)} collective-permute-done((f32[32,32,128]{2,1,0:T(8,128)S(1)}, f32[32,32,128]{2,1,0:T(8,128)S(1)}, u32[]{:S(2)}, u32[]{:S(2)}) %collective-permute-start.12) | collective-permute-done | bytes 524320 | tf_op jit(solution)/shard_map/ppermute | solution.py:29
  72.2 2.8 %collective-permute-done.11.refs_8_.refs_7_ = f32[32,32,128]{2,1,0:T(8,128)S(1)} collective-permute-done((f32[32,32,128]{2,1,0:T(8,128)S(1)}, f32[32,32,128]{2,1,0:T(8,128)S(1)}, u32[]{:S(2)}, u32[]{:S(2)}) %collective-permute-start.11) | collective-permute-done | bytes 524320 | tf_op jit(solution)/shard_map/ppermute | solution.py:29
  75.0 9.3 %collective-permute-done.10.refs_7_.refs_6_ = f32[32,32,128]{2,1,0:T(8,128)S(1)} collective-permute-done((f32[32,32,128]{2,1,0:T(8,128)S(1)}, f32[32,32,128]{2,1,0:T(8,128)S(1)}, u32[]{:S(2)}, u32[]{:S(2)}) %collective-permute-start.10) | collective-permute-done | bytes 524320 | tf_op jit(solution)/shard_map/ppermute | solution.py:29
  84.4 6.0 %third.1.refs_10_ = f32[129,32,128]{2,1,0:T(8,128)S(1)} custom-call(s32[3]{0:T(128)S(1)} %pad_add_fusion.refs_0_, s32[8,3,64]{2,1,0:T(4,128)S(1)} %bitcast.25, s32[8]{0:T(128)S(1)} %bitcast.29, f32[32,32,128]{2,1,0:T(8,128)S(1)} %collective-permute-done.3.refs_3_, f32[32,32,128]{2,1,0:T(8,128)} %collective-permute-done.4.refs_4_, ...), custom_call_target="tpu_custom_call" | custom-call | flops 805306368 | bytes 7340032 | tf_op jit(solution)/shard_map/third/pallas_call | solution.py:154
  90.4 0.0 collective-permute-done.2.refs_4_
  90.4 0.1 collective-permute-start.13
  90.5 1.9 %collective-permute-done.13.refs_3_ = f32[32,32,128]{2,1,0:T(8,128)S(1)} collective-permute-done((f32[32,32,128]{2,1,0:T(8,128)S(1)}, f32[32,32,128]{2,1,0:T(8,128)S(1)}, u32[]{:S(2)}, u32[]{:S(2)}) %collective-permute-start.13) | collective-permute-done | bytes 524320 | tf_op jit(solution)/shard_map/ppermute | solution.py:29
  92.4 4.2 %fourth.1 = f32[129,32,128]{2,1,0:T(8,128)S(1)} custom-call(s32[3]{0:T(128)S(1)} %pad_add_fusion.refs_0_, s32[8,3,64]{2,1,0:T(4,128)S(1)} %bitcast.26, s32[8]{0:T(128)S(1)} %bitcast.30, f32[32,32,128]{2,1,0:T(8,128)S(1)} %collective-permute-done.13.refs_3_, f32[32,32,128]{2,1,0:T(8,128)S(1)} %collective-permute-done.2.refs_4_, ...), custom_call_target="tpu_custom_call" | custom-call | flops 536870912 | bytes 6291456 | tf_op jit(solution)/shard_map/fourth/pallas_call | solution.py:154
  96.6 0.1 fusion.2
  96.7 1.6 %collective-permute-start.15 = (f32[32,32,128]{2,1,0:T(8,128)S(1)}, f32[32,32,128]{2,1,0:T(8,128)S(1)}, u32[]{:S(2)}, u32[]{:S(2)}) collective-permute-start(f32[32,32,128]{2,1,0:T(8,128)S(1)} %get-tuple-element.19), channel_id=1, source_target_pairs={{0,1},{1,2},{2,3},{3,0},{4,5},{5,6},{6,7},{7,4},{8,9},{9,10},{10,1... | collective-permute-start | bytes 1572872 | tf_op jit(solution)/shard_map/ppermute | solution.py:29
  98.3 3.8 %collective-permute-start.14 = (f32[32,32,128]{2,1,0:T(8,128)S(1)}, f32[32,32,128]{2,1,0:T(8,128)S(1)}, u32[]{:S(2)}, u32[]{:S(2)}) collective-permute-start(f32[32,32,128]{2,1,0:T(8,128)S(1)} %get-tuple-element.20), channel_id=1, source_target_pairs={{0,3},{1,0},{2,1},{3,2},{4,7},{5,4},{6,5},{7,6},{8,11},{9,8},{10,9... | collective-permute-start | bytes 1572872 | tf_op jit(solution)/shard_map/ppermute | solution.py:29
  102.1 11.2 %collective-permute-done.15 = f32[32,32,128]{2,1,0:T(8,128)S(1)} collective-permute-done((f32[32,32,128]{2,1,0:T(8,128)S(1)}, f32[32,32,128]{2,1,0:T(8,128)S(1)}, u32[]{:S(2)}, u32[]{:S(2)}) %collective-permute-start.15) | collective-permute-done | bytes 524320 | tf_op jit(solution)/shard_map/ppermute | solution.py:29
  113.3 0.0 copy-start.3
  113.3 0.1 collective-permute-start.16
  113.4 0.0 collective-permute-done.14
  113.4 7.9 %collective-permute-done.16 = f32[16,32,128]{2,1,0:T(8,128)S(1)} collective-permute-done((f32[16,32,128]{2,1,0:T(8,128)S(1)}, f32[16,32,128]{2,1,0:T(8,128)S(1)}, u32[]{:S(2)}, u32[]{:S(2)}) %collective-permute-start.16) | collective-permute-done | bytes 262176 | tf_op jit(solution)/shard_map/ppermute | solution.py:29
  121.4 0.1 fusion.1
  121.5 0.3 collective-permute-start.17
  121.8 6.1 %collective-permute-done.17 = f32[16,32,128]{2,1,0:T(8,128)S(1)} collective-permute-done((f32[16,32,128]{2,1,0:T(8,128)S(1)}, f32[16,32,128]{2,1,0:T(8,128)S(1)}, u32[]{:S(2)}, u32[]{:S(2)}) %collective-permute-start.17) | collective-permute-done | bytes 262176 | tf_op jit(solution)/shard_map/ppermute | solution.py:29
  127.9 0.1 fusion
  128.0 0.1 mul.27
  128.2 0.8 multiply_subtract_fusion
  (13 shorter events, 0.1 us)
Async XLA Ops:
  0.0 19.8 %copy-start.4 = (s32[1,1,1,8,3,64]{5,3,4,2,1,0:T(8,128)S(1)}, s32[1,1,1,8,3,64]{5,3,4,2,1,0:T(8,128)}, u32[]{:S(2)}) copy-start(s32[1,1,1,8,3,64]{5,3,4,2,1,0:T(8,128)} %param.8) | copy-start | bytes 18436
  0.0 19.9 %copy-start.2 = (s32[1,1,1,8]{3,2,1,0:T(1,128)S(1)}, s32[1,1,1,8]{3,2,1,0:T(1,128)}, u32[]{:S(2)}) copy-start(s32[1,1,1,8]{3,2,1,0:T(1,128)} %param.9) | copy-start | bytes 100
  1.2 14.9 %collective-permute-start.9 = (f32[32,32,128]{2,1,0:T(8,128)S(1)}, f32[32,32,128]{2,1,0:T(8,128)S(1)}, u32[]{:S(2)}, u32[]{:S(2)}) collective-permute-start(f32[32,32,128]{2,1,0:T(8,128)S(1)} %bitcast.18), channel_id=1, source_target_pairs={{0,64},{1,65},{2,66},{3,67},{4,68},{5,69},{6,70},{7,71},{8,72},{9,... | collective-permute-start | bytes 1572872 | tf_op jit(solution)/shard_map/ppermute | solution.py:29
  4.0 15.0 %collective-permute-start = (f32[32,32,128]{2,1,0:T(8,128)S(1)}, f32[32,32,128]{2,1,0:T(8,128)}, u32[]{:S(2)}, u32[]{:S(2)}) collective-permute-start(f32[32,32,128]{2,1,0:T(8,128)S(1)} %bitcast.15), channel_id=1, source_target_pairs={{0,24},{1,25},{2,26},{3,27},{4,28},{5,29},{6,30},{7,31},{8,0},{9,1... | collective-permute-start | bytes 1572872 | tf_op jit(solution)/shard_map/ppermute | solution.py:29
  4.1 14.8 %collective-permute-start.7 = (f32[32,32,128]{2,1,0:T(8,128)S(1)}, f32[32,32,128]{2,1,0:T(8,128)S(1)}, u32[]{:S(2)}, u32[]{:S(2)}) collective-permute-start(f32[32,32,128]{2,1,0:T(8,128)S(1)} %bitcast.19), channel_id=1, source_target_pairs={{0,192},{1,193},{2,194},{3,195},{4,196},{5,197},{6,198},{7,199},{8... | collective-permute-start | bytes 1572872 | tf_op jit(solution)/shard_map/ppermute | solution.py:29
  4.6 25.0 %collective-permute-start.8 = (f32[32,32,128]{2,1,0:T(8,128)S(1)}, f32[32,32,128]{2,1,0:T(8,128)}, u32[]{:S(2)}, u32[]{:S(2)}) collective-permute-start(f32[32,32,128]{2,1,0:T(8,128)S(1)} %bitcast.20), channel_id=1, source_target_pairs={{0,128},{1,129},{2,130},{3,131},{4,132},{5,133},{6,134},{7,135},{8... | collective-permute-start | bytes 1572872 | tf_op jit(solution)/shard_map/ppermute | solution.py:29
  6.9 50.5 %collective-permute-start.6 = (f32[32,32,128]{2,1,0:T(8,128)S(1)}, f32[32,32,128]{2,1,0:T(8,128)S(1)}, u32[]{:S(2)}, u32[]{:S(2)}) collective-permute-start(f32[32,32,128]{2,1,0:T(8,128)S(1)} %bitcast.21), channel_id=1, source_target_pairs={{0,32},{1,33},{2,34},{3,35},{4,36},{5,37},{6,38},{7,39},{8,40},{9,... | collective-permute-start | bytes 1572872 | tf_op jit(solution)/shard_map/ppermute | solution.py:29
  16.1 43.9 %collective-permute-start.3 = (f32[32,32,128]{2,1,0:T(8,128)S(1)}, f32[32,32,128]{2,1,0:T(8,128)S(1)}, u32[]{:S(2)}, u32[]{:S(2)}) collective-permute-start(f32[32,32,128]{2,1,0:T(8,128)S(1)} %bitcast.16), channel_id=1, source_target_pairs={{0,4},{1,5},{2,6},{3,7},{4,0},{5,1},{6,2},{7,3},{8,12},{9,13},{10,... | collective-permute-start | bytes 1572872 | tf_op jit(solution)/shard_map/ppermute | solution.py:29
  19.0 42.1 %collective-permute-start.1 = (f32[32,32,128]{2,1,0:T(8,128)}, f32[32,32,128]{2,1,0:T(8,128)S(1)}, u32[]{:S(2)}, u32[]{:S(2)}) collective-permute-start(f32[32,32,128]{2,1,0:T(8,128)} %collective-permute-done.refs_4_), channel_id=1, source_target_pairs={{0,24},{1,25},{2,26},{3,27},{4,28},{5,29},{6,30},{7,31},{8,0},{9,1... | collective-permute-start | bytes 1572872 | tf_op jit(solution)/shard_map/ppermute | solution.py:29
  19.0 0.8 copy-start
  19.8 41.3 %collective-permute-start.4 = (f32[32,32,128]{2,1,0:T(8,128)}, f32[32,32,128]{2,1,0:T(8,128)}, u32[]{:S(2)}, u32[]{:S(2)}) collective-permute-start(f32[32,32,128]{2,1,0:T(8,128)} %collective-permute-done.refs_4_), channel_id=1, source_target_pairs={{0,4},{1,5},{2,6},{3,7},{4,0},{5,1},{6,2},{7,3},{8,12},{9,13},{10,... | collective-permute-start | bytes 1572872 | tf_op jit(solution)/shard_map/ppermute | solution.py:29
  19.9 1.0 copy-start.1
  57.4 14.8 %collective-permute-start.12 = (f32[32,32,128]{2,1,0:T(8,128)S(1)}, f32[32,32,128]{2,1,0:T(8,128)S(1)}, u32[]{:S(2)}, u32[]{:S(2)}) collective-permute-start(f32[32,32,128]{2,1,0:T(8,128)S(1)} %collective-permute-done.6.refs_6_.refs_5_), channel_id=1, source_target_pairs={{0,64},{1,65},{2,66},{3,67},{4,68},{5,69},{6,70},{7,71},{8,72},{9,... | collective-permute-start | bytes 1572872 | tf_op jit(solution)/shard_map/ppermute | solution.py:29
  58.7 16.3 %collective-permute-start.11 = (f32[32,32,128]{2,1,0:T(8,128)S(1)}, f32[32,32,128]{2,1,0:T(8,128)S(1)}, u32[]{:S(2)}, u32[]{:S(2)}) collective-permute-start(f32[32,32,128]{2,1,0:T(8,128)S(1)} %collective-permute-done.6.refs_6_.refs_5_), channel_id=1, source_target_pairs={{0,128},{1,129},{2,130},{3,131},{4,132},{5,133},{6,134},{7,135},{8... | collective-permute-start | bytes 1572872 | tf_op jit(solution)/shard_map/ppermute | solution.py:29
  59.9 24.4 %collective-permute-start.10 = (f32[32,32,128]{2,1,0:T(8,128)S(1)}, f32[32,32,128]{2,1,0:T(8,128)S(1)}, u32[]{:S(2)}, u32[]{:S(2)}) collective-permute-start(f32[32,32,128]{2,1,0:T(8,128)S(1)} %collective-permute-done.6.refs_6_.refs_5_), channel_id=1, source_target_pairs={{0,192},{1,193},{2,194},{3,195},{4,196},{5,197},{6,198},{7,199},{8... | collective-permute-start | bytes 1572872 | tf_op jit(solution)/shard_map/ppermute | solution.py:29
  61.1 23.3 %collective-permute-start.5 = (f32[32,32,128]{2,1,0:T(8,128)S(1)}, f32[32,32,128]{2,1,0:T(8,128)S(1)}, u32[]{:S(2)}, u32[]{:S(2)}) collective-permute-start(f32[32,32,128]{2,1,0:T(8,128)S(1)} %collective-permute-done.1.refs_3_), channel_id=1, source_target_pairs={{0,4},{1,5},{2,6},{3,7},{4,0},{5,1},{6,2},{7,3},{8,12},{9,13},{10,... | collective-permute-start | bytes 1572872 | tf_op jit(solution)/shard_map/ppermute | solution.py:29
  61.1 29.3 %collective-permute-start.2 = (f32[32,32,128]{2,1,0:T(8,128)S(1)}, f32[32,32,128]{2,1,0:T(8,128)S(1)}, u32[]{:S(2)}, u32[]{:S(2)}) collective-permute-start(f32[32,32,128]{2,1,0:T(8,128)S(1)} %collective-permute-done.1.refs_3_), channel_id=1, source_target_pairs={{0,24},{1,25},{2,26},{3,27},{4,28},{5,29},{6,30},{7,31},{8,0},{9,1... | collective-permute-start | bytes 1572872 | tf_op jit(solution)/shard_map/ppermute | solution.py:29
  90.4 2.0 %collective-permute-start.13 = (f32[32,32,128]{2,1,0:T(8,128)S(1)}, f32[32,32,128]{2,1,0:T(8,128)S(1)}, u32[]{:S(2)}, u32[]{:S(2)}) collective-permute-start(f32[32,32,128]{2,1,0:T(8,128)S(1)} %collective-permute-done.2.refs_4_), channel_id=1, source_target_pairs={{0,4},{1,5},{2,6},{3,7},{4,0},{5,1},{6,2},{7,3},{8,12},{9,13},{10,... | collective-permute-start | bytes 1572872 | tf_op jit(solution)/shard_map/ppermute | solution.py:29
  96.7 16.6 %collective-permute-start.15 = (f32[32,32,128]{2,1,0:T(8,128)S(1)}, f32[32,32,128]{2,1,0:T(8,128)S(1)}, u32[]{:S(2)}, u32[]{:S(2)}) collective-permute-start(f32[32,32,128]{2,1,0:T(8,128)S(1)} %get-tuple-element.19), channel_id=1, source_target_pairs={{0,1},{1,2},{2,3},{3,0},{4,5},{5,6},{6,7},{7,4},{8,9},{9,10},{10,1... | collective-permute-start | bytes 1572872 | tf_op jit(solution)/shard_map/ppermute | solution.py:29
  98.3 15.1 %collective-permute-start.14 = (f32[32,32,128]{2,1,0:T(8,128)S(1)}, f32[32,32,128]{2,1,0:T(8,128)S(1)}, u32[]{:S(2)}, u32[]{:S(2)}) collective-permute-start(f32[32,32,128]{2,1,0:T(8,128)S(1)} %get-tuple-element.20), channel_id=1, source_target_pairs={{0,3},{1,0},{2,1},{3,2},{4,7},{5,4},{6,5},{7,6},{8,11},{9,8},{10,9... | collective-permute-start | bytes 1572872 | tf_op jit(solution)/shard_map/ppermute | solution.py:29
  113.3 14.8 %copy-start.3 = (f32[1,1,32,4096]{3,2,1,0:T(8,128)S(1)}, f32[1,1,32,4096]{3,2,1,0:T(8,128)}, u32[]{:S(2)}) copy-start(f32[1,1,32,4096]{3,2,1,0:T(8,128)} %param.7) | copy-start | bytes 1572868
  113.3 8.0 %collective-permute-start.16 = (f32[16,32,128]{2,1,0:T(8,128)S(1)}, f32[16,32,128]{2,1,0:T(8,128)S(1)}, u32[]{:S(2)}, u32[]{:S(2)}) collective-permute-start(f32[16,32,128]{2,1,0:T(8,128)S(1)} %slice_add_fusion.2), channel_id=1, source_target_pairs={{0,1},{1,2},{2,3},{3,0},{4,5},{5,6},{6,7},{7,4},{8,9},{9,10},{10,1... | collective-permute-start | bytes 786440 | tf_op jit(solution)/shard_map/ppermute | solution.py:29
  121.5 6.4 %collective-permute-start.17 = (f32[16,32,128]{2,1,0:T(8,128)S(1)}, f32[16,32,128]{2,1,0:T(8,128)S(1)}, u32[]{:S(2)}, u32[]{:S(2)}) collective-permute-start(f32[16,32,128]{2,1,0:T(8,128)S(1)} %get-tuple-element.18), channel_id=1, source_target_pairs={{0,3},{1,0},{2,1},{3,2},{4,7},{5,4},{6,5},{7,6},{8,11},{9,8},{10,9... | collective-permute-start | bytes 786440 | tf_op jit(solution)/shard_map/ppermute | solution.py:29

commit v3 on v2

--- a/solution.py
+++ b/solution.py
@@ -142,7 +142,7 @@
                 out[slots[u]] += sums[u]
 
 
-def add_sections(jobs, place, pattern, limits, lefts, rights, acc, name, weight=1):
+def add_sections(jobs, place, pattern, limits, lefts, rights, acc, name):
     smem = pl.BlockSpec(memory_space=pltpu.SMEM)
     anywhere = pl.BlockSpec(memory_space=pl.ANY)
     operands = [place, pattern, limits, *lefts, *rights]
@@ -150,7 +150,6 @@
     if acc is not None:
         operands.append(acc)
         specs.append(anywhere)
-    n = len(jobs)
     return pl.pallas_call(
         functools.partial(section_kernel, jobs, len(lefts), len(rights), acc is not None),
         out_shape=jax.ShapeDtypeStruct((SLOTS + 1, 32, 128), F32),
@@ -166,9 +165,7 @@
             pltpu.SemaphoreType.DMA((1,)),
         ],
         compiler_params=pltpu.CompilerParams(vmem_limit_bytes=24 << 20),
-        cost_estimate=pl.CostEstimate(
-            flops=weight * n * 64 * 2 * 64 * 256 * 128, bytes_accessed=n * (1 << 20) + (4 << 20), transcendentals=0
-        ),
+        cost_estimate=pl.CostEstimate(flops=0, bytes_accessed=0, transcendentals=0),
         name=name,
     )(*operands)
 
@@ -176,8 +173,10 @@
 def reduce_over_depth(acc):
     up = by_depth(acc[48:80], 1)
     down = by_depth(acc[80:112], -1)
+    up, down = lax.optimization_barrier((up, down))
     up2 = by_depth(acc[32:48] + up[16:32], 1)
     down2 = by_depth(acc[112:128] + down[0:16], -1)
+    up2, down2 = lax.optimization_barrier((up2, down2))
     return jnp.concatenate([acc[0:16] + down[16:32] + up2, acc[16:32] + up[0:16] + down2])
 
 
@@ -193,28 +192,29 @@
     args = (place, pattern, limits)
     choices = [(i, i) for i in range(4)]
     other0 = swap_zh(right)
-    left1 = by_zl(left, -1)
     same1, same3, same2 = by_y(right, -1), by_y(right, 1), by_y(right, 2)
+    twin0 = swap_core(left)
+    acc = add_sections([(0, False, 0, [(0, 0)])], *args, [left], [right], None, "sections_a")
+    same1, acc, left_now = lax.optimization_barrier((same1, acc, left))
+    left1 = by_zl(left_now, -1)
+    other0, same1, same3, same2, acc = lax.optimization_barrier((other0, same1, same3, same2, acc))
+
+    other1, other3, other2 = by_y(other0, -1), by_y(other0, 1), by_y(other0, 2)
     left2 = by_zl(left1, -1)
-    twin0 = swap_core(left)
-    jobs = [(0, False, 0, [(0, 0)]), (1, False, 1, [(1, 1)])]
-    acc = add_sections(jobs, *args, [left, left1], [right, same1], None, "first")
-    other0, acc, same2, same3 = lax.optimization_barrier((other0, acc, same2, same3))
-
-    other1, other3, other2 = by_y(other0, -1), by_y(other0, 1), by_y(other0, 2)
+    twin1 = swap_core(left1)
+    acc = add_sections([(1, False, 0, [(1, 0)])], *args, [left1], [same1], acc, "sections_b")
     left3 = by_zl(left2, -1)
-    twin1 = swap_core(left1)
     twin2 = swap_core(left2)
-    acc = add_sections([(2, False, 0, [(2, 0)])], *args, [left2], [same2], acc, "second")
+    acc = add_sections([(2, False, 0, [(2, 0)])], *args, [left2], [same2], acc, "sections_c")
 
     other = [other0, other1, other2, other3]
     jobs = [(k, True, k, choices) for k in range(3)]
-    acc = add_sections(jobs, *args, [twin0, twin1, twin2], other, acc, "third")
+    acc = add_sections(jobs, *args, [twin0, twin1, twin2], other, acc, "sections_d")
 
     left3, acc = lax.optimization_barrier((left3, acc))
     twin3 = swap_core(left3)
     jobs = [(3, False, 1, [(3, 4)]), (3, True, 0, choices)]
-    acc = add_sections(jobs, *args, [twin3, left3], other + [same3], acc, "fourth")
+    acc = add_sections(jobs, *args, [twin3, left3], other + [same3], acc, "sections_e")
     share = reduce_over_depth(acc)
     purified = 3.0 * square_tiles[0, 0] - 2.0 * share.reshape(TILES, 4096)
     return purified[None, None]

time: 131 us -> 116 us (0.89)
  the two profiles are of different devices: /device:TPU:72 before, /device:TPU:1 now
where the time goes in v3:
time: 116 us
  waiting for transfers between devices  56.7 us (49%)
  starting transfers between devices  36.4 us (31%)
  Pallas kernels  18.2 us (16%)
  local copies, waits for them, and re-layouts  3.17 us (3%)
  other arithmetic  1.21 us (1%)
    ppermute x18, waiting for transfers between devices, moved(): return lax.ppermute(x, AXES, pairs)  56.7 us
    ppermute x18, starting transfers between devices, moved(): return lax.ppermute(x, AXES, pairs)  36.4 us
    pallas_call x5, Pallas kernels, add_sections(): pl.pallas_call(functools.partial(section_kernel, jobs, len(lefts), len(ri...  18.2 us
    unnamed x7, local copies, waits for them, and re-layouts  3.01 us
  transfers between devices with their start and end apart: 18, of which 10 were waited for; matrix products, arithmetic and copies ran while one was open for 2% of the time, Pallas kernels for 12%

profile of v3, /device:TPU:1, one launch (start us, length us, event | category | flops | bytes accessed | tf_op | source)
XLA Modules:
  0.0 115.9 jit_solution(10554922600458740064)
XLA Ops:
  0.0 1.1 copy.7
  1.2 3.6 %collective-permute-start = (f32[32,32,128]{2,1,0:T(8,128)S(1)}, f32[32,32,128]{2,1,0:T(8,128)S(1)}, u32[]{:S(2)}, u32[]{:S(2)}) collective-permute-start(f32[32,32,128]{2,1,0:T(8,128)S(1)} %bitcast.15), channel_id=1, source_target_pairs={{0,192},{1,193},{2,194},{3,195},{4,196},{5,197},{6,198},{7,199},{8... | collective-permute-start | bytes 1572872 | tf_op jit(solution)/shard_map/ppermute | solution.py:29
  4.8 0.3 collective-permute-start.9
  5.1 0.7 collective-permute-start.8
  5.8 6.9 %collective-permute-start.7 = (f32[32,32,128]{2,1,0:T(8,128)S(1)}, f32[32,32,128]{2,1,0:T(8,128)S(1)}, u32[]{:S(2)}, u32[]{:S(2)}) collective-permute-start(f32[32,32,128]{2,1,0:T(8,128)S(1)} %bitcast.18), channel_id=1, source_target_pairs={{0,32},{1,33},{2,34},{3,35},{4,36},{5,37},{6,38},{7,39},{8,40},{9,... | collective-permute-start | bytes 1572872 | tf_op jit(solution)/shard_map/ppermute | solution.py:29
  12.7 0.7 copy.10
  13.5 1.1 copy.8
  14.6 0.1 pad_add_fusion.refs_0_
  14.7 2.6 %sections_a.1.refs_5_ = f32[129,32,128]{2,1,0:T(8,128)S(1)} custom-call(s32[3]{0:T(128)S(1)} %pad_add_fusion.refs_0_, s32[8,3,64]{2,1,0:T(4,128)S(1)} %bitcast.23, s32[8]{0:T(128)S(1)} %bitcast.28, f32[32,32,128]{2,1,0:T(8,128)S(1)} %bitcast.20, f32[32,32,128]{2,1,0:T(8,128)S(1)} %bitcast.19), custom_call_target="tpu_custom_call" | custom-call | tf_op jit(solution)/shard_map/sections_a/pallas_call | solution.py:153
  17.3 9.2 %collective-permute-done.refs_4_ = f32[32,32,128]{2,1,0:T(8,128)S(1)} collective-permute-done((f32[32,32,128]{2,1,0:T(8,128)S(1)}, f32[32,32,128]{2,1,0:T(8,128)S(1)}, u32[]{:S(2)}, u32[]{:S(2)}) %collective-permute-start) | collective-permute-done | bytes 524320 | tf_op jit(solution)/shard_map/ppermute | solution.py:29
  26.5 0.0 collective-permute-start.1
  26.5 6.3 %collective-permute-start.4 = (f32[32,32,128]{2,1,0:T(8,128)S(1)}, f32[32,32,128]{2,1,0:T(8,128)S(1)}, u32[]{:S(2)}, u32[]{:S(2)}) collective-permute-start(f32[32,32,128]{2,1,0:T(8,128)S(1)} %bitcast.22), channel_id=1, source_target_pairs={{0,4},{1,5},{2,6},{3,7},{4,0},{5,1},{6,2},{7,3},{8,12},{9,13},{10,... | collective-permute-start | bytes 1572872 | tf_op jit(solution)/shard_map/ppermute | solution.py:29
  32.8 0.0 collective-permute-done.9.refs_4_
  32.8 0.0 collective-permute-done.8.refs_9_
  32.8 13.7 %collective-permute-done.1.refs_3_ = f32[32,32,128]{2,1,0:T(8,128)S(1)} collective-permute-done((f32[32,32,128]{2,1,0:T(8,128)S(1)}, f32[32,32,128]{2,1,0:T(8,128)S(1)}, u32[]{:S(2)}, u32[]{:S(2)}) %collective-permute-start.1) | collective-permute-done | bytes 524320 | tf_op jit(solution)/shard_map/ppermute | solution.py:29
  46.5 0.0 collective-permute-start.2
  46.5 1.6 %collective-permute-start.12 = (f32[32,32,128]{2,1,0:T(8,128)S(1)}, f32[32,32,128]{2,1,0:T(8,128)S(1)}, u32[]{:S(2)}, u32[]{:S(2)}) collective-permute-start(f32[32,32,128]{2,1,0:T(8,128)S(1)} %collective-permute-done.7.refs_6_.refs_5_), channel_id=1, source_target_pairs={{0,64},{1,65},{2,66},{3,67},{4,68},{5,69},{6,70},{7,71},{8,72},{9,... | collective-permute-start | bytes 1572872 | tf_op jit(solution)/shard_map/ppermute | solution.py:29
  48.1 5.3 %collective-permute-start.11 = (f32[32,32,128]{2,1,0:T(8,128)S(1)}, f32[32,32,128]{2,1,0:T(8,128)S(1)}, u32[]{:S(2)}, u32[]{:S(2)}) collective-permute-start(f32[32,32,128]{2,1,0:T(8,128)S(1)} %collective-permute-done.7.refs_6_.refs_5_), channel_id=1, source_target_pairs={{0,128},{1,129},{2,130},{3,131},{4,132},{5,133},{6,134},{7,135},{8... | collective-permute-start | bytes 1572872 | tf_op jit(solution)/shard_map/ppermute | solution.py:29
  53.4 0.0 collective-permute-start.10
  53.4 0.0 collective-permute-done.4.refs_3_
  53.4 2.6 %collective-permute-start.5 = (f32[32,32,128]{2,1,0:T(8,128)S(1)}, f32[32,32,128]{2,1,0:T(8,128)S(1)}, u32[]{:S(2)}, u32[]{:S(2)}) collective-permute-start(f32[32,32,128]{2,1,0:T(8,128)S(1)} %collective-permute-done.1.refs_3_), channel_id=1, source_target_pairs={{0,4},{1,5},{2,6},{3,7},{4,0},{5,1},{6,2},{7,3},{8,12},{9,13},{10,... | collective-permute-start | bytes 1572872 | tf_op jit(solution)/shard_map/ppermute | solution.py:29
  56.0 2.4 %collective-permute-done.2.refs_3_ = f32[32,32,128]{2,1,0:T(8,128)S(1)} collective-permute-done((f32[32,32,128]{2,1,0:T(8,128)S(1)}, f32[32,32,128]{2,1,0:T(8,128)S(1)}, u32[]{:S(2)}, u32[]{:S(2)}) %collective-permute-start.2) | collective-permute-done | bytes 524320 | tf_op jit(solution)/shard_map/ppermute | solution.py:29
  58.4 2.9 %collective-permute-start.6 = (f32[32,32,128]{2,1,0:T(8,128)S(1)}, f32[32,32,128]{2,1,0:T(8,128)S(1)}, u32[]{:S(2)}, u32[]{:S(2)}) collective-permute-start(f32[32,32,128]{2,1,0:T(8,128)S(1)} %collective-permute-done.2.refs_3_), channel_id=1, source_target_pairs={{0,4},{1,5},{2,6},{3,7},{4,0},{5,1},{6,2},{7,3},{8,12},{9,13},{10,... | collective-permute-start | bytes 1572872 | tf_op jit(solution)/shard_map/ppermute | solution.py:29
  61.2 1.1 collective-permute-done.12.refs_9_.refs_8_
  62.4 0.3 collective-permute-start.3
  62.7 2.6 %sections_b.1.refs_5_ = f32[129,32,128]{2,1,0:T(8,128)S(1)} custom-call(s32[3]{0:T(128)S(1)} %pad_add_fusion.refs_0_, s32[8,3,64]{2,1,0:T(4,128)S(1)} %bitcast.24, s32[8]{0:T(128)S(1)} %bitcast.29, f32[32,32,128]{2,1,0:T(8,128)S(1)} %collective-permute-done.1.refs_3_, f32[32,32,128]{2,1,0:T(8,128)S(1)} %collective-permute-done.refs_4_, ...), custom_call_target="tpu_custom_call" | custom-call | tf_op jit(solution)/shard_map/sections_b/pallas_call | solution.py:153
  65.3 2.6 %sections_c.1.refs_10_ = f32[129,32,128]{2,1,0:T(8,128)S(1)} custom-call(s32[3]{0:T(128)S(1)} %pad_add_fusion.refs_0_, s32[8,3,64]{2,1,0:T(4,128)S(1)} %bitcast.25, s32[8]{0:T(128)S(1)} %bitcast.30, f32[32,32,128]{2,1,0:T(8,128)S(1)} %collective-permute-done.2.refs_3_, f32[32,32,128]{2,1,0:T(8,128)S(1)} %collective-permute-done.9.refs_4_, ...), custom_call_target="tpu_custom_call" | custom-call | tf_op jit(solution)/shard_map/sections_c/pallas_call | solution.py:153
  67.9 7.8 %collective-permute-done.11.refs_8_.refs_7_ = f32[32,32,128]{2,1,0:T(8,128)S(1)} collective-permute-done((f32[32,32,128]{2,1,0:T(8,128)S(1)}, f32[32,32,128]{2,1,0:T(8,128)S(1)}, u32[]{:S(2)}, u32[]{:S(2)}) %collective-permute-start.11) | collective-permute-done | bytes 524320 | tf_op jit(solution)/shard_map/ppermute | solution.py:29
  75.8 0.0 collective-permute-done.10.refs_7_.refs_6_
  75.8 0.0 collective-permute-done.5.refs_4_
  75.8 0.0 collective-permute-done.6.refs_5_
  75.8 6.1 %sections_d.1.refs_10_ = f32[129,32,128]{2,1,0:T(8,128)S(1)} custom-call(s32[3]{0:T(128)S(1)} %pad_add_fusion.refs_0_, s32[8,3,64]{2,1,0:T(4,128)S(1)} %bitcast.26, s32[8]{0:T(128)S(1)} %bitcast.31, f32[32,32,128]{2,1,0:T(8,128)S(1)} %collective-permute-done.4.refs_3_, f32[32,32,128]{2,1,0:T(8,128)S(1)} %collective-permute-done.5.refs_4_, ...), custom_call_target="tpu_custom_call" | custom-call | tf_op jit(solution)/shard_map/sections_d/pallas_call | solution.py:153
  81.9 1.8 %collective-permute-start.13 = (f32[32,32,128]{2,1,0:T(8,128)S(1)}, f32[32,32,128]{2,1,0:T(8,128)S(1)}, u32[]{:S(2)}, u32[]{:S(2)}) collective-permute-start(f32[32,32,128]{2,1,0:T(8,128)S(1)} %collective-permute-done.3.refs_4_), channel_id=1, source_target_pairs={{0,4},{1,5},{2,6},{3,7},{4,0},{5,1},{6,2},{7,3},{8,12},{9,13},{10,... | collective-permute-start | bytes 1572872 | tf_op jit(solution)/shard_map/ppermute | solution.py:29
  83.7 1.5 %collective-permute-done.13.refs_3_ = f32[32,32,128]{2,1,0:T(8,128)S(1)} collective-permute-done((f32[32,32,128]{2,1,0:T(8,128)S(1)}, f32[32,32,128]{2,1,0:T(8,128)S(1)}, u32[]{:S(2)}, u32[]{:S(2)}) %collective-permute-start.13) | collective-permute-done | bytes 524320 | tf_op jit(solution)/shard_map/ppermute | solution.py:29
  85.2 4.3 %sections_e.1 = f32[129,32,128]{2,1,0:T(8,128)S(1)} custom-call(s32[3]{0:T(128)S(1)} %pad_add_fusion.refs_0_, s32[8,3,64]{2,1,0:T(4,128)S(1)} %bitcast.27, s32[8]{0:T(128)S(1)} %bitcast.32, f32[32,32,128]{2,1,0:T(8,128)S(1)} %collective-permute-done.13.refs_3_, f32[32,32,128]{2,1,0:T(8,128)S(1)} %collective-permute-done.3.refs_4_, ...), custom_call_target="tpu_custom_call" | custom-call | tf_op jit(solution)/shard_map/sections_e/pallas_call | solution.py:153
  89.5 0.1 fusion.2
  89.5 2.6 %collective-permute-start.15 = (f32[32,32,128]{2,1,0:T(8,128)S(1)}, f32[32,32,128]{2,1,0:T(8,128)S(1)}, u32[]{:S(2)}, u32[]{:S(2)}) collective-permute-start(f32[32,32,128]{2,1,0:T(8,128)S(1)} %get-tuple-element.37), channel_id=1, source_target_pairs={{0,3},{1,0},{2,1},{3,2},{4,7},{5,4},{6,5},{7,6},{8,11},{9,8},{10,9... | collective-permute-start | bytes 1572872 | tf_op jit(solution)/shard_map/ppermute | solution.py:29
  92.1 11.0 %collective-permute-done.15 = f32[32,32,128]{2,1,0:T(8,128)S(1)} collective-permute-done((f32[32,32,128]{2,1,0:T(8,128)S(1)}, f32[32,32,128]{2,1,0:T(8,128)S(1)}, u32[]{:S(2)}, u32[]{:S(2)}) %collective-permute-start.15) | collective-permute-done | bytes 524320 | tf_op jit(solution)/shard_map/ppermute | solution.py:29
  103.1 3.1 %collective-permute-done.14 = f32[32,32,128]{2,1,0:T(8,128)S(1)} collective-permute-done((f32[32,32,128]{2,1,0:T(8,128)S(1)}, f32[32,32,128]{2,1,0:T(8,128)S(1)}, u32[]{:S(2)}, u32[]{:S(2)}) %collective-permute-start.14) | collective-permute-done | bytes 524320 | tf_op jit(solution)/shard_map/ppermute | solution.py:29
  106.2 0.1 slice_add_fusion.1
  106.3 0.0 copy-start.1
  106.3 0.6 collective-permute-start.17
  106.9 0.9 collective-permute-start.16
  107.8 4.9 %collective-permute-done.17 = f32[16,32,128]{2,1,0:T(8,128)S(1)} collective-permute-done((f32[16,32,128]{2,1,0:T(8,128)S(1)}, f32[16,32,128]{2,1,0:T(8,128)S(1)}, u32[]{:S(2)}, u32[]{:S(2)}) %collective-permute-start.17) | collective-permute-done | bytes 262176 | tf_op jit(solution)/shard_map/ppermute | solution.py:29
  112.7 2.1 %collective-permute-done.16 = f32[16,32,128]{2,1,0:T(8,128)S(1)} collective-permute-done((f32[16,32,128]{2,1,0:T(8,128)S(1)}, f32[16,32,128]{2,1,0:T(8,128)S(1)}, u32[]{:S(2)}, u32[]{:S(2)}) %collective-permute-start.16) | collective-permute-done | bytes 262176 | tf_op jit(solution)/shard_map/ppermute | solution.py:29
  114.7 0.2 fusion.1
  115.0 0.1 mul.27
  115.1 0.8 multiply_subtract_fusion
  (7 shorter events, 0.1 us)
Async XLA Ops:
  0.0 14.7 %copy-start = (s32[1,1,1,8]{3,2,1,0:T(1,128)S(1)}, s32[1,1,1,8]{3,2,1,0:T(1,128)}, u32[]{:S(2)}) copy-start(s32[1,1,1,8]{3,2,1,0:T(1,128)} %param.9) | copy-start | bytes 100
  1.2 25.3 %collective-permute-start = (f32[32,32,128]{2,1,0:T(8,128)S(1)}, f32[32,32,128]{2,1,0:T(8,128)S(1)}, u32[]{:S(2)}, u32[]{:S(2)}) collective-permute-start(f32[32,32,128]{2,1,0:T(8,128)S(1)} %bitcast.15), channel_id=1, source_target_pairs={{0,192},{1,193},{2,194},{3,195},{4,196},{5,197},{6,198},{7,199},{8... | collective-permute-start | bytes 1572872 | tf_op jit(solution)/shard_map/ppermute | solution.py:29
  4.8 28.0 %collective-permute-start.9 = (f32[32,32,128]{2,1,0:T(8,128)S(1)}, f32[32,32,128]{2,1,0:T(8,128)S(1)}, u32[]{:S(2)}, u32[]{:S(2)}) collective-permute-start(f32[32,32,128]{2,1,0:T(8,128)S(1)} %bitcast.16), channel_id=1, source_target_pairs={{0,128},{1,129},{2,130},{3,131},{4,132},{5,133},{6,134},{7,135},{8... | collective-permute-start | bytes 1572872 | tf_op jit(solution)/shard_map/ppermute | solution.py:29
  5.1 27.7 %collective-permute-start.8 = (f32[32,32,128]{2,1,0:T(8,128)S(1)}, f32[32,32,128]{2,1,0:T(8,128)S(1)}, u32[]{:S(2)}, u32[]{:S(2)}) collective-permute-start(f32[32,32,128]{2,1,0:T(8,128)S(1)} %bitcast.17), channel_id=1, source_target_pairs={{0,64},{1,65},{2,66},{3,67},{4,68},{5,69},{6,70},{7,71},{8,72},{9,... | collective-permute-start | bytes 1572872 | tf_op jit(solution)/shard_map/ppermute | solution.py:29
  5.8 27.0 %collective-permute-start.7 = (f32[32,32,128]{2,1,0:T(8,128)S(1)}, f32[32,32,128]{2,1,0:T(8,128)S(1)}, u32[]{:S(2)}, u32[]{:S(2)}) collective-permute-start(f32[32,32,128]{2,1,0:T(8,128)S(1)} %bitcast.18), channel_id=1, source_target_pairs={{0,32},{1,33},{2,34},{3,35},{4,36},{5,37},{6,38},{7,39},{8,40},{9,... | collective-permute-start | bytes 1572872 | tf_op jit(solution)/shard_map/ppermute | solution.py:29
  26.5 20.0 %collective-permute-start.1 = (f32[32,32,128]{2,1,0:T(8,128)S(1)}, f32[32,32,128]{2,1,0:T(8,128)S(1)}, u32[]{:S(2)}, u32[]{:S(2)}) collective-permute-start(f32[32,32,128]{2,1,0:T(8,128)S(1)} %bitcast.21), channel_id=1, source_target_pairs={{0,24},{1,25},{2,26},{3,27},{4,28},{5,29},{6,30},{7,31},{8,0},{9,1... | collective-permute-start | bytes 1572872 | tf_op jit(solution)/shard_map/ppermute | solution.py:29
  26.5 26.9 %collective-permute-start.4 = (f32[32,32,128]{2,1,0:T(8,128)S(1)}, f32[32,32,128]{2,1,0:T(8,128)S(1)}, u32[]{:S(2)}, u32[]{:S(2)}) collective-permute-start(f32[32,32,128]{2,1,0:T(8,128)S(1)} %bitcast.22), channel_id=1, source_target_pairs={{0,4},{1,5},{2,6},{3,7},{4,0},{5,1},{6,2},{7,3},{8,12},{9,13},{10,... | collective-permute-start | bytes 1572872 | tf_op jit(solution)/shard_map/ppermute | solution.py:29
  46.5 11.9 %collective-permute-start.2 = (f32[32,32,128]{2,1,0:T(8,128)S(1)}, f32[32,32,128]{2,1,0:T(8,128)S(1)}, u32[]{:S(2)}, u32[]{:S(2)}) collective-permute-start(f32[32,32,128]{2,1,0:T(8,128)S(1)} %collective-permute-done.1.refs_3_), channel_id=1, source_target_pairs={{0,24},{1,25},{2,26},{3,27},{4,28},{5,29},{6,30},{7,31},{8,0},{9,1... | collective-permute-start | bytes 1572872 | tf_op jit(solution)/shard_map/ppermute | solution.py:29
  46.5 15.9 %collective-permute-start.12 = (f32[32,32,128]{2,1,0:T(8,128)S(1)}, f32[32,32,128]{2,1,0:T(8,128)S(1)}, u32[]{:S(2)}, u32[]{:S(2)}) collective-permute-start(f32[32,32,128]{2,1,0:T(8,128)S(1)} %collective-permute-done.7.refs_6_.refs_5_), channel_id=1, source_target_pairs={{0,64},{1,65},{2,66},{3,67},{4,68},{5,69},{6,70},{7,71},{8,72},{9,... | collective-permute-start | bytes 1572872 | tf_op jit(solution)/shard_map/ppermute | solution.py:29
  48.1 27.7 %collective-permute-start.11 = (f32[32,32,128]{2,1,0:T(8,128)S(1)}, f32[32,32,128]{2,1,0:T(8,128)S(1)}, u32[]{:S(2)}, u32[]{:S(2)}) collective-permute-start(f32[32,32,128]{2,1,0:T(8,128)S(1)} %collective-permute-done.7.refs_6_.refs_5_), channel_id=1, source_target_pairs={{0,128},{1,129},{2,130},{3,131},{4,132},{5,133},{6,134},{7,135},{8... | collective-permute-start | bytes 1572872 | tf_op jit(solution)/shard_map/ppermute | solution.py:29
  53.4 22.4 %collective-permute-start.10 = (f32[32,32,128]{2,1,0:T(8,128)S(1)}, f32[32,32,128]{2,1,0:T(8,128)S(1)}, u32[]{:S(2)}, u32[]{:S(2)}) collective-permute-start(f32[32,32,128]{2,1,0:T(8,128)S(1)} %collective-permute-done.7.refs_6_.refs_5_), channel_id=1, source_target_pairs={{0,192},{1,193},{2,194},{3,195},{4,196},{5,197},{6,198},{7,199},{8... | collective-permute-start | bytes 1572872 | tf_op jit(solution)/shard_map/ppermute | solution.py:29
  53.4 22.4 %collective-permute-start.5 = (f32[32,32,128]{2,1,0:T(8,128)S(1)}, f32[32,32,128]{2,1,0:T(8,128)S(1)}, u32[]{:S(2)}, u32[]{:S(2)}) collective-permute-start(f32[32,32,128]{2,1,0:T(8,128)S(1)} %collective-permute-done.1.refs_3_), channel_id=1, source_target_pairs={{0,4},{1,5},{2,6},{3,7},{4,0},{5,1},{6,2},{7,3},{8,12},{9,13},{10,... | collective-permute-start | bytes 1572872 | tf_op jit(solution)/shard_map/ppermute | solution.py:29
  58.4 17.4 %collective-permute-start.6 = (f32[32,32,128]{2,1,0:T(8,128)S(1)}, f32[32,32,128]{2,1,0:T(8,128)S(1)}, u32[]{:S(2)}, u32[]{:S(2)}) collective-permute-start(f32[32,32,128]{2,1,0:T(8,128)S(1)} %collective-permute-done.2.refs_3_), channel_id=1, source_target_pairs={{0,4},{1,5},{2,6},{3,7},{4,0},{5,1},{6,2},{7,3},{8,12},{9,13},{10,... | collective-permute-start | bytes 1572872 | tf_op jit(solution)/shard_map/ppermute | solution.py:29
  62.4 19.5 %collective-permute-start.3 = (f32[32,32,128]{2,1,0:T(8,128)S(1)}, f32[32,32,128]{2,1,0:T(8,128)S(1)}, u32[]{:S(2)}, u32[]{:S(2)}) collective-permute-start(f32[32,32,128]{2,1,0:T(8,128)S(1)} %collective-permute-done.2.refs_3_), channel_id=1, source_target_pairs={{0,24},{1,25},{2,26},{3,27},{4,28},{5,29},{6,30},{7,31},{8,0},{9,1... | collective-permute-start | bytes 1572872 | tf_op jit(solution)/shard_map/ppermute | solution.py:29
  81.9 3.3 %collective-permute-start.13 = (f32[32,32,128]{2,1,0:T(8,128)S(1)}, f32[32,32,128]{2,1,0:T(8,128)S(1)}, u32[]{:S(2)}, u32[]{:S(2)}) collective-permute-start(f32[32,32,128]{2,1,0:T(8,128)S(1)} %collective-permute-done.3.refs_4_), channel_id=1, source_target_pairs={{0,4},{1,5},{2,6},{3,7},{4,0},{5,1},{6,2},{7,3},{8,12},{9,13},{10,... | collective-permute-start | bytes 1572872 | tf_op jit(solution)/shard_map/ppermute | solution.py:29
  89.5 13.5 %collective-permute-start.15 = (f32[32,32,128]{2,1,0:T(8,128)S(1)}, f32[32,32,128]{2,1,0:T(8,128)S(1)}, u32[]{:S(2)}, u32[]{:S(2)}) collective-permute-start(f32[32,32,128]{2,1,0:T(8,128)S(1)} %get-tuple-element.37), channel_id=1, source_target_pairs={{0,3},{1,0},{2,1},{3,2},{4,7},{5,4},{6,5},{7,6},{8,11},{9,8},{10,9... | collective-permute-start | bytes 1572872 | tf_op jit(solution)/shard_map/ppermute | solution.py:29
  92.1 14.1 %collective-permute-start.14 = (f32[32,32,128]{2,1,0:T(8,128)S(1)}, f32[32,32,128]{2,1,0:T(8,128)S(1)}, u32[]{:S(2)}, u32[]{:S(2)}) collective-permute-start(f32[32,32,128]{2,1,0:T(8,128)S(1)} %get-tuple-element.38), channel_id=1, source_target_pairs={{0,1},{1,2},{2,3},{3,0},{4,5},{5,6},{6,7},{7,4},{8,9},{9,10},{10,1... | collective-permute-start | bytes 1572872 | tf_op jit(solution)/shard_map/ppermute | solution.py:29
  106.3 8.8 %copy-start.1 = (f32[1,1,32,4096]{3,2,1,0:T(8,128)S(1)}, f32[1,1,32,4096]{3,2,1,0:T(8,128)}, u32[]{:S(2)}) copy-start(f32[1,1,32,4096]{3,2,1,0:T(8,128)} %param.7) | copy-start | bytes 1572868
  106.3 6.4 %collective-permute-start.17 = (f32[16,32,128]{2,1,0:T(8,128)S(1)}, f32[16,32,128]{2,1,0:T(8,128)S(1)}, u32[]{:S(2)}, u32[]{:S(2)}) collective-permute-start(f32[16,32,128]{2,1,0:T(8,128)S(1)} %get-tuple-element.35), channel_id=1, source_target_pairs={{0,3},{1,0},{2,1},{3,2},{4,7},{5,4},{6,5},{7,6},{8,11},{9,8},{10,9... | collective-permute-start | bytes 786440 | tf_op jit(solution)/shard_map/ppermute | solution.py:29
  106.9 7.8 %collective-permute-start.16 = (f32[16,32,128]{2,1,0:T(8,128)S(1)}, f32[16,32,128]{2,1,0:T(8,128)S(1)}, u32[]{:S(2)}, u32[]{:S(2)}) collective-permute-start(f32[16,32,128]{2,1,0:T(8,128)S(1)} %get-tuple-element.36), channel_id=1, source_target_pairs={{0,1},{1,2},{2,3},{3,0},{4,5},{5,6},{6,7},{7,4},{8,9},{9,10},{10,1... | collective-permute-start | bytes 786440 | tf_op jit(solution)/shard_map/ppermute | solution.py:29

commit v4 on v3

--- a/solution.py
+++ b/solution.py
@@ -13,6 +13,7 @@
 TILES = 32
 SLOTS = 128
 UNROLL = 32
+PARTS = ((0, 32), (32, 48), (48, 80), (80, 112), (112, 128))
 
 
 def moved(x, target):
@@ -54,25 +55,33 @@
     return high, p - high
 
 
-def section_kernel(jobs, n_left, n_right, has_acc, *refs):
+def section_kernel(jobs, n_left, n_right, has_acc, half, *refs):
     place, pairs, counts = refs[:3]
     lefts = refs[3 : 3 + n_left]
     rights = refs[3 + n_left : 3 + n_left + n_right]
     rest = refs[3 + n_left + n_right :]
     if has_acc:
         start, rest = rest[0], rest[1:]
-    out, lbuf, rbuf, rows, a3, b3, sem, acc_sem = rest
+    if half is None:
+        outs, (out, lbuf, rbuf, rows, a3, b3, sem, acc_sem) = (), rest
+    else:
+        outs, (lbuf, rbuf, rows, a3, b3, sem, acc_sem, out) = rest[:5], rest[5:]
     shift, core, depth = place[0], place[1], place[2]
     lane = lax.broadcasted_iota(jnp.int32, (32, 128), 1) < 64
+    height = out.shape[1]
+    lane_left = lane[:height]
 
     def section(job):
         k, odd = job[0], job[1]
         return lax.rem(2 * k + 9 - 2 * core, 8) if odd else 2 * k
 
+    def own_rows(ref):
+        return ref if half is None else ref.at[:, pl.ds(height * half, height)]
+
     def fetch(j):
         k, odd, left, choices = jobs[j]
         slot = j % 2
-        pltpu.make_async_copy(lefts[left], lbuf.at[slot], sem.at[slot, 0]).start()
+        pltpu.make_async_copy(own_rows(lefts[left]), lbuf.at[slot], sem.at[slot, 0]).start()
         if len(choices) == 1:
             pltpu.make_async_copy(rights[choices[0][1]], rbuf.at[slot], sem.at[slot, 1]).start()
         else:
@@ -85,12 +94,12 @@
 
     def wait(j):
         slot = j % 2
-        pltpu.make_async_copy(lefts[0], lbuf.at[slot], sem.at[slot, 0]).wait()
+        pltpu.make_async_copy(own_rows(lefts[0]), lbuf.at[slot], sem.at[slot, 0]).wait()
         pltpu.make_async_copy(rights[0], rbuf.at[slot], sem.at[slot, 1]).wait()
 
     fetch(0)
     if has_acc:
-        load = pltpu.make_async_copy(start, out, acc_sem.at[0])
+        load = pltpu.make_async_copy(own_rows(start), out, acc_sem.at[0])
         load.start()
     else:
         out[...] = jnp.zeros_like(out)
@@ -105,10 +114,10 @@
             h, low = split(lbuf[slot, t])
             hr = pltpu.roll(h, 64, 1)
             lr = pltpu.roll(low, 64, 1)
-            a3[t, 0:32, 0:128] = jnp.where(lane, h, hr).astype(BF16)
-            a3[t, 32:64, 0:128] = jnp.where(lane, hr, h).astype(BF16)
-            a3[t, 0:32, 128:256] = jnp.where(lane, low, lr).astype(BF16)
-            a3[t, 32:64, 128:256] = jnp.where(lane, lr, low).astype(BF16)
+            a3[t, 0:height, 0:128] = jnp.where(lane_left, h, hr).astype(BF16)
+            a3[t, height : 2 * height, 0:128] = jnp.where(lane_left, hr, h).astype(BF16)
+            a3[t, 0:height, 128:256] = jnp.where(lane_left, low, lr).astype(BF16)
+            a3[t, height : 2 * height, 128:256] = jnp.where(lane_left, lr, low).astype(BF16)
             r = rbuf[slot, t]
             rr = pltpu.roll(r, 64, 1)
             rows[t, pl.ds(0, 32, stride=2)] = jnp.where(lane, r, rr)
@@ -135,14 +144,17 @@
             for u in range(UNROLL):
                 p = block * UNROLL + u
                 c = jnp.dot(a3[pairs[s, 0, p]], b3[pairs[s, 1, p]], preferred_element_type=F32)
-                sums.append(jnp.where(lane, c[0:32], c[32:64]))
+                sums.append(jnp.where(lane_left, c[0:height], c[height : 2 * height]))
                 g = lax.rem(pairs[s, 2, p] + (4 - depth) * 32, SLOTS)
                 slots.append(jnp.where(p < live, g, SLOTS))
             for u in range(UNROLL):
                 out[slots[u]] += sums[u]
 
-
-def add_sections(jobs, place, pattern, limits, lefts, rights, acc, name):
+    for ref, (first, last) in zip(outs, PARTS):
+        ref[...] = out[first:last]
+
+
+def add_sections(jobs, place, pattern, limits, lefts, rights, acc, name, half=None):
     smem = pl.BlockSpec(memory_space=pltpu.SMEM)
     anywhere = pl.BlockSpec(memory_space=pl.ANY)
     operands = [place, pattern, limits, *lefts, *rights]
@@ -150,34 +162,42 @@
     if acc is not None:
         operands.append(acc)
         specs.append(anywhere)
+    height = 32 if half is None else 16
+    vmem = pl.BlockSpec(memory_space=pltpu.VMEM)
+    shape = jax.ShapeDtypeStruct((SLOTS + 1, height, 128), F32)
+    scratch = []
+    if half is not None:
+        shape = [jax.ShapeDtypeStruct((last - first, height, 128), F32) for first, last in PARTS]
+        scratch = [pltpu.VMEM((SLOTS + 1, height, 128), F32)]
     return pl.pallas_call(
-        functools.partial(section_kernel, jobs, len(lefts), len(rights), acc is not None),
-        out_shape=jax.ShapeDtypeStruct((SLOTS + 1, 32, 128), F32),
+        functools.partial(section_kernel, jobs, len(lefts), len(rights), acc is not None, half),
+        out_shape=shape,
         in_specs=specs,
-        out_specs=pl.BlockSpec(memory_space=pltpu.VMEM),
+        out_specs=vmem if half is None else [vmem] * len(PARTS),
         scratch_shapes=[
-            pltpu.VMEM((2, TILES, 32, 128), F32),
+            pltpu.VMEM((2, TILES, height, 128), F32),
             pltpu.VMEM((2, TILES, 32, 128), F32),
             pltpu.VMEM((TILES, 64, 128), F32),
-            pltpu.VMEM((TILES, 64, 256), BF16),
+            pltpu.VMEM((TILES, 2 * height, 256), BF16),
             pltpu.VMEM((TILES, 256, 128), BF16),
             pltpu.SemaphoreType.DMA((2, 2)),
             pltpu.SemaphoreType.DMA((1,)),
-        ],
+        ]
+        + scratch,
         compiler_params=pltpu.CompilerParams(vmem_limit_bytes=24 << 20),
         cost_estimate=pl.CostEstimate(flops=0, bytes_accessed=0, transcendentals=0),
         name=name,
     )(*operands)
 
 
-def reduce_over_depth(acc):
-    up = by_depth(acc[48:80], 1)
-    down = by_depth(acc[80:112], -1)
+def reduce_over_depth(parts):
+    own, low, up, down, high = parts
+    up, down = by_depth(up, 1), by_depth(down, -1)
     up, down = lax.optimization_barrier((up, down))
-    up2 = by_depth(acc[32:48] + up[16:32], 1)
-    down2 = by_depth(acc[112:128] + down[0:16], -1)
+    up2 = by_depth(low + up[16:32], 1)
+    down2 = by_depth(high + down[0:16], -1)
     up2, down2 = lax.optimization_barrier((up2, down2))
-    return jnp.concatenate([acc[0:16] + down[16:32] + up2, acc[16:32] + up[0:16] + down2])
+    return jnp.concatenate([own[0:16] + down[16:32] + up2, own[16:32] + up[0:16] + down2])
 
 
 def on_device(left_tiles, right_tiles, square_tiles, pairs, counts):
@@ -203,19 +223,22 @@
     left2 = by_zl(left1, -1)
     twin1 = swap_core(left1)
     acc = add_sections([(1, False, 0, [(1, 0)])], *args, [left1], [same1], acc, "sections_b")
+    left2, other1, other3, other2, acc = lax.optimization_barrier((left2, other1, other3, other2, acc))
+
     left3 = by_zl(left2, -1)
     twin2 = swap_core(left2)
-    acc = add_sections([(2, False, 0, [(2, 0)])], *args, [left2], [same2], acc, "sections_c")
-
     other = [other0, other1, other2, other3]
-    jobs = [(k, True, k, choices) for k in range(3)]
-    acc = add_sections(jobs, *args, [twin0, twin1, twin2], other, acc, "sections_d")
-
+    jobs = [(2, False, 0, [(2, 4)])] + [(k, True, k + 1, choices) for k in range(3)]
+    acc = add_sections(jobs, *args, [left2, twin0, twin1, twin2], other + [same2], acc, "sections_c")
+
+    jobs = [(3, False, 1, [(3, 4)]), (3, True, 0, choices)]
     left3, acc = lax.optimization_barrier((left3, acc))
     twin3 = swap_core(left3)
-    jobs = [(3, False, 1, [(3, 4)]), (3, True, 0, choices)]
-    acc = add_sections(jobs, *args, [twin3, left3], other + [same3], acc, "sections_e")
-    share = reduce_over_depth(acc)
+    share = [
+        add_sections(jobs, *args, [twin3, left3], other + [same3], acc, f"sections_e{h}", h) for h in range(2)
+    ]
+    share = [reduce_over_depth(half) for half in share]
+    share = jnp.concatenate(share, axis=1)
     purified = 3.0 * square_tiles[0, 0] - 2.0 * share.reshape(TILES, 4096)
     return purified[None, None]
 

time: 116 us -> 119 us (1.026)
  the two profiles are of different devices: /device:TPU:1 before, /device:TPU:46 now
where the time goes in v4:
time: 119 us
  waiting for transfers between devices  67.5 us (57%)
  starting transfers between devices  25.7 us (22%)
  Pallas kernels  21 us (18%)
  local copies, waits for them, and re-layouts  3.11 us (3%)
    ppermute x22, waiting for transfers between devices, moved(): return lax.ppermute(x, AXES, pairs)  67.5 us
    ppermute x22, starting transfers between devices, moved(): return lax.ppermute(x, AXES, pairs)  25.7 us
    pallas_call x5, Pallas kernels, add_sections(): pl.pallas_call(functools.partial(section_kernel, jobs, len(lefts), len(ri...  21 us
    unnamed x7, local copies, waits for them, and re-layouts  3.01 us
  transfers between devices with their start and end apart: 22, of which 18 were waited for; matrix products, arithmetic and copies ran while one was open for 2% of the time, Pallas kernels for 14%

profile of v4, /device:TPU:46, one launch (start us, length us, event | category | flops | bytes accessed | tf_op | source)
XLA Modules:
  0.0 118.6 jit_solution(15251612068150226247)
XLA Ops:
  0.0 1.1 copy.7
  1.2 0.5 collective-permute-start
  1.7 2.6 %collective-permute-start.5 = (f32[32,32,128]{2,1,0:T(8,128)S(1)}, f32[32,32,128]{2,1,0:T(8,128)S(1)}, u32[]{:S(2)}, u32[]{:S(2)}) collective-permute-start(f32[32,32,128]{2,1,0:T(8,128)S(1)} %bitcast.16), channel_id=1, source_target_pairs={{0,128},{1,129},{2,130},{3,131},{4,132},{5,133},{6,134},{7,135},{8... | collective-permute-start | bytes 1572872 | tf_op jit(solution)/shard_map/ppermute | solution.py:30
  4.3 1.9 %collective-permute-start.4 = (f32[32,32,128]{2,1,0:T(8,128)S(1)}, f32[32,32,128]{2,1,0:T(8,128)S(1)}, u32[]{:S(2)}, u32[]{:S(2)}) collective-permute-start(f32[32,32,128]{2,1,0:T(8,128)S(1)} %bitcast.17), channel_id=1, source_target_pairs={{0,64},{1,65},{2,66},{3,67},{4,68},{5,69},{6,70},{7,71},{8,72},{9,... | collective-permute-start | bytes 1572872 | tf_op jit(solution)/shard_map/ppermute | solution.py:30
  6.2 6.3 %collective-permute-start.3 = (f32[32,32,128]{2,1,0:T(8,128)S(1)}, f32[32,32,128]{2,1,0:T(8,128)S(1)}, u32[]{:S(2)}, u32[]{:S(2)}) collective-permute-start(f32[32,32,128]{2,1,0:T(8,128)S(1)} %bitcast.18), channel_id=1, source_target_pairs={{0,32},{1,33},{2,34},{3,35},{4,36},{5,37},{6,38},{7,39},{8,40},{9,... | collective-permute-start | bytes 1572872 | tf_op jit(solution)/shard_map/ppermute | solution.py:30
  12.4 0.7 copy.10
  13.2 0.1 pad_add_fusion.refs_0_
  13.2 1.1 copy.8
  14.4 2.6 %sections_a.1.refs_5_ = f32[129,32,128]{2,1,0:T(8,128)S(1)} custom-call(s32[3]{0:T(128)S(1)} %pad_add_fusion.refs_0_, s32[8,3,64]{2,1,0:T(4,128)S(1)} %bitcast.23, s32[8]{0:T(128)S(1)} %bitcast.28, f32[32,32,128]{2,1,0:T(8,128)S(1)} %bitcast.20, f32[32,32,128]{2,1,0:T(8,128)S(1)} %bitcast.19), custom_call_target="tpu_custom_call" | custom-call | tf_op jit(solution)/shard_map/sections_a/pallas_call | solution.py:172
  17.0 1.1 collective-permute-start.1
  18.1 9.1 %collective-permute-done.5.refs_11_ = f32[32,32,128]{2,1,0:T(8,128)S(1)} collective-permute-done((f32[32,32,128]{2,1,0:T(8,128)S(1)}, f32[32,32,128]{2,1,0:T(8,128)S(1)}, u32[]{:S(2)}, u32[]{:S(2)}) %collective-permute-start.5) | collective-permute-done | bytes 524320 | tf_op jit(solution)/shard_map/ppermute | solution.py:30
  27.1 0.8 collective-permute-done.4.refs_9_
  28.0 8.3 %collective-permute-done.3.refs_7_.refs_5_ = f32[32,32,128]{2,1,0:T(8,128)S(1)} collective-permute-done((f32[32,32,128]{2,1,0:T(8,128)S(1)}, f32[32,32,128]{2,1,0:T(8,128)S(1)}, u32[]{:S(2)}, u32[]{:S(2)}) %collective-permute-start.3) | collective-permute-done | bytes 524320 | tf_op jit(solution)/shard_map/ppermute | solution.py:30
  36.2 1.0 collective-permute-start.8
  37.2 0.6 collective-permute-start.7
  37.9 1.4 %collective-permute-start.6 = (f32[32,32,128]{2,1,0:T(8,128)S(1)}, f32[32,32,128]{2,1,0:T(8,128)S(1)}, u32[]{:S(2)}, u32[]{:S(2)}) collective-permute-start(f32[32,32,128]{2,1,0:T(8,128)S(1)} %collective-permute-done.3.refs_7_.refs_5_), channel_id=1, source_target_pairs={{0,192},{1,193},{2,194},{3,195},{4,196},{5,197},{6,198},{7,199},{8... | collective-permute-start | bytes 1572872 | tf_op jit(solution)/shard_map/ppermute | solution.py:30
  39.2 6.8 %collective-permute-done.1.refs_3_ = f32[32,32,128]{2,1,0:T(8,128)S(1)} collective-permute-done((f32[32,32,128]{2,1,0:T(8,128)S(1)}, f32[32,32,128]{2,1,0:T(8,128)S(1)}, u32[]{:S(2)}, u32[]{:S(2)}) %collective-permute-start.1) | collective-permute-done | bytes 524320 | tf_op jit(solution)/shard_map/ppermute | solution.py:30
  46.0 1.7 %collective-permute-start.2 = (f32[32,32,128]{2,1,0:T(8,128)S(1)}, f32[32,32,128]{2,1,0:T(8,128)S(1)}, u32[]{:S(2)}, u32[]{:S(2)}) collective-permute-start(f32[32,32,128]{2,1,0:T(8,128)S(1)} %collective-permute-done.1.refs_3_), channel_id=1, source_target_pairs={{0,24},{1,25},{2,26},{3,27},{4,28},{5,29},{6,30},{7,31},{8,0},{9,1... | collective-permute-start | bytes 1572872 | tf_op jit(solution)/shard_map/ppermute | solution.py:30
  47.7 2.6 %sections_b.1.refs_12_ = f32[129,32,128]{2,1,0:T(8,128)S(1)} custom-call(s32[3]{0:T(128)S(1)} %pad_add_fusion.refs_0_, s32[8,3,64]{2,1,0:T(4,128)S(1)} %bitcast.24, s32[8]{0:T(128)S(1)} %bitcast.29, f32[32,32,128]{2,1,0:T(8,128)S(1)} %collective-permute-done.1.refs_3_, f32[32,32,128]{2,1,0:T(8,128)S(1)} %collective-permute-done.refs_4_, ...), custom_call_target="tpu_custom_call" | custom-call | tf_op jit(solution)/shard_map/sections_b/pallas_call | solution.py:172
  50.4 2.2 %collective-permute-done.8.refs_9_.refs_7_ = f32[32,32,128]{2,1,0:T(8,128)S(1)} collective-permute-done((f32[32,32,128]{2,1,0:T(8,128)S(1)}, f32[32,32,128]{2,1,0:T(8,128)S(1)}, u32[]{:S(2)}, u32[]{:S(2)}) %collective-permute-start.8) | collective-permute-done | bytes 524320 | tf_op jit(solution)/shard_map/ppermute | solution.py:30
  52.6 5.8 %collective-permute-done.7.refs_10_.refs_8_ = f32[32,32,128]{2,1,0:T(8,128)S(1)} collective-permute-done((f32[32,32,128]{2,1,0:T(8,128)S(1)}, f32[32,32,128]{2,1,0:T(8,128)S(1)}, u32[]{:S(2)}, u32[]{:S(2)}) %collective-permute-start.7) | collective-permute-done | bytes 524320 | tf_op jit(solution)/shard_map/ppermute | solution.py:30
  58.4 0.3 collective-permute-done.6.refs_8_.refs_6_
  58.6 1.9 %collective-permute-done.2.refs_3_ = f32[32,32,128]{2,1,0:T(8,128)S(1)} collective-permute-done((f32[32,32,128]{2,1,0:T(8,128)S(1)}, f32[32,32,128]{2,1,0:T(8,128)S(1)}, u32[]{:S(2)}, u32[]{:S(2)}) %collective-permute-start.2) | collective-permute-done | bytes 524320 | tf_op jit(solution)/shard_map/ppermute | solution.py:30
  60.5 1.9 %collective-permute-done.12.refs_6_ = f32[32,32,128]{2,1,0:T(8,128)S(1)} collective-permute-done((f32[32,32,128]{2,1,0:T(8,128)S(1)}, f32[32,32,128]{2,1,0:T(8,128)S(1)}, u32[]{:S(2)}, u32[]{:S(2)}) %collective-permute-start.12) | collective-permute-done | bytes 524320 | tf_op jit(solution)/shard_map/ppermute | solution.py:30
  62.4 7.6 %sections_c.1.refs_10_ = f32[129,32,128]{2,1,0:T(8,128)S(1)} custom-call(s32[3]{0:T(128)S(1)} %pad_add_fusion.refs_0_, s32[8,3,64]{2,1,0:T(4,128)S(1)} %bitcast.25, s32[8]{0:T(128)S(1)} %bitcast.30, f32[32,32,128]{2,1,0:T(8,128)S(1)} %collective-permute-done.2.refs_3_, f32[32,32,128]{2,1,0:T(8,128)S(1)} %collective-permute-done.10.refs_4_, ...), custom_call_target="tpu_custom_call" | custom-call | tf_op jit(solution)/shard_map/sections_c/pallas_call | solution.py:172
  70.0 15.8 %collective-permute-done.9.refs_4_ = f32[32,32,128]{2,1,0:T(8,128)S(1)} collective-permute-done((f32[32,32,128]{2,1,0:T(8,128)S(1)}, f32[32,32,128]{2,1,0:T(8,128)S(1)}, u32[]{:S(2)}, u32[]{:S(2)}) %collective-permute-start.9) | collective-permute-done | bytes 524320 | tf_op jit(solution)/shard_map/ppermute | solution.py:30
  85.8 1.9 %collective-permute-done.13.refs_3_ = f32[32,32,128]{2,1,0:T(8,128)S(1)} collective-permute-done((f32[32,32,128]{2,1,0:T(8,128)S(1)}, f32[32,32,128]{2,1,0:T(8,128)S(1)}, u32[]{:S(2)}, u32[]{:S(2)}) %collective-permute-start.13) | collective-permute-done | bytes 524320 | tf_op jit(solution)/shard_map/ppermute | solution.py:30
  87.7 4.1 %sections_e1.1 = (f32[32,16,128]{2,1,0:T(8,128)S(1)}, f32[16,16,128]{2,1,0:T(8,128)S(1)}, f32[32,16,128]{2,1,0:T(8,128)S(1)}, f32[32,16,128]{2,1,0:T(8,128)S(1)}, f32[16,16,128]{2,1,0:T(8,128)S(1)}) custom-call(s32[3]{0:T(128)S(1)} %pad_add_fusion.refs_0_, s32[8,3,64]{2,1,0:T(4,128)S(1)} %bitcast.26, s32[8]{0:T(128)S(1)} %bitcast.31, ...), custom_call_target="tpu_custom_call" | custom-call | tf_op jit(solution)/shard_map/sections_e1/pallas_call | solution.py:172
  91.8 0.6 collective-permute-start.18
  92.4 1.5 %collective-permute-start.19 = (f32[32,16,128]{2,1,0:T(8,128)S(1)}, f32[32,16,128]{2,1,0:T(8,128)S(1)}, u32[]{:S(2)}, u32[]{:S(2)}) collective-permute-start(f32[32,16,128]{2,1,0:T(8,128)S(1)} %get-tuple-element.64), channel_id=1, source_target_pairs={{0,3},{1,0},{2,1},{3,2},{4,7},{5,4},{6,5},{7,6},{8,11},{9,8},{10,9... | collective-permute-start | bytes 786440 | tf_op jit(solution)/shard_map/ppermute | solution.py:30
  93.9 4.1 %sections_e0.1 = (f32[32,16,128]{2,1,0:T(8,128)S(1)}, f32[16,16,128]{2,1,0:T(8,128)S(1)}, f32[32,16,128]{2,1,0:T(8,128)S(1)}, f32[32,16,128]{2,1,0:T(8,128)S(1)}, f32[16,16,128]{2,1,0:T(8,128)S(1)}) custom-call(s32[3]{0:T(128)S(1)} %pad_add_fusion.refs_0_, s32[8,3,64]{2,1,0:T(4,128)S(1)} %bitcast.27, s32[8]{0:T(128)S(1)} %bitcast.32, ...), custom_call_target="tpu_custom_call" | custom-call | tf_op jit(solution)/shard_map/sections_e0/pallas_call | solution.py:172
  98.0 1.8 %collective-permute-start.14 = (f32[32,16,128]{2,1,0:T(8,128)S(1)}, f32[32,16,128]{2,1,0:T(8,128)S(1)}, u32[]{:S(2)}, u32[]{:S(2)}) collective-permute-start(f32[32,16,128]{2,1,0:T(8,128)S(1)} %get-tuple-element.54), channel_id=1, source_target_pairs={{0,1},{1,2},{2,3},{3,0},{4,5},{5,6},{6,7},{7,4},{8,9},{9,10},{10,1... | collective-permute-start | bytes 786440 | tf_op jit(solution)/shard_map/ppermute | solution.py:30
  99.8 0.3 collective-permute-start.15
  100.1 0.1 collective-permute-done.18
  100.2 2.4 %collective-permute-done.19 = f32[32,16,128]{2,1,0:T(8,128)S(1)} collective-permute-done((f32[32,16,128]{2,1,0:T(8,128)S(1)}, f32[32,16,128]{2,1,0:T(8,128)S(1)}, u32[]{:S(2)}, u32[]{:S(2)}) %collective-permute-start.19) | collective-permute-done | bytes 262176 | tf_op jit(solution)/shard_map/ppermute | solution.py:30
  102.6 0.5 collective-permute-start.20
  103.1 1.7 %collective-permute-start.21 = (f32[16,16,128]{2,1,0:T(8,128)S(1)}, f32[16,16,128]{2,1,0:T(8,128)S(1)}, u32[]{:S(2)}, u32[]{:S(2)}) collective-permute-start(f32[16,16,128]{2,1,0:T(8,128)S(1)} %slice_add_fusion), channel_id=1, source_target_pairs={{0,3},{1,0},{2,1},{3,2},{4,7},{5,4},{6,5},{7,6},{8,11},{9,8},{10,9... | collective-permute-start | bytes 393224 | tf_op jit(solution)/shard_map/ppermute | solution.py:30
  104.8 1.5 %collective-permute-done.14 = f32[32,16,128]{2,1,0:T(8,128)S(1)} collective-permute-done((f32[32,16,128]{2,1,0:T(8,128)S(1)}, f32[32,16,128]{2,1,0:T(8,128)S(1)}, u32[]{:S(2)}, u32[]{:S(2)}) %collective-permute-start.14) | collective-permute-done | bytes 262176 | tf_op jit(solution)/shard_map/ppermute | solution.py:30
  106.4 3.5 %collective-permute-done.15 = f32[32,16,128]{2,1,0:T(8,128)S(1)} collective-permute-done((f32[32,16,128]{2,1,0:T(8,128)S(1)}, f32[32,16,128]{2,1,0:T(8,128)S(1)}, u32[]{:S(2)}, u32[]{:S(2)}) %collective-permute-start.15) | collective-permute-done | bytes 262176 | tf_op jit(solution)/shard_map/ppermute | solution.py:30
  109.9 1.2 %collective-permute-start.16 = (f32[16,16,128]{2,1,0:T(8,128)S(1)}, f32[16,16,128]{2,1,0:T(8,128)S(1)}, u32[]{:S(2)}, u32[]{:S(2)}) collective-permute-start(f32[16,16,128]{2,1,0:T(8,128)S(1)} %slice_add_fusion.3), channel_id=1, source_target_pairs={{0,1},{1,2},{2,3},{3,0},{4,5},{5,6},{6,7},{7,4},{8,9},{9,10},{10,1... | collective-permute-start | bytes 393224 | tf_op jit(solution)/shard_map/ppermute | solution.py:30
  111.2 1.0 collective-permute-start.17
  112.1 0.6 collective-permute-done.21
  112.7 3.4 %collective-permute-done.16 = f32[16,16,128]{2,1,0:T(8,128)S(1)} collective-permute-done((f32[16,16,128]{2,1,0:T(8,128)S(1)}, f32[16,16,128]{2,1,0:T(8,128)S(1)}, u32[]{:S(2)}, u32[]{:S(2)}) %collective-permute-start.16) | collective-permute-done | bytes 131104 | tf_op jit(solution)/shard_map/ppermute | solution.py:30
  116.1 1.3 %collective-permute-done.17 = f32[16,16,128]{2,1,0:T(8,128)S(1)} collective-permute-done((f32[16,16,128]{2,1,0:T(8,128)S(1)}, f32[16,16,128]{2,1,0:T(8,128)S(1)}, u32[]{:S(2)}, u32[]{:S(2)}) %collective-permute-start.17) | collective-permute-done | bytes 131104 | tf_op jit(solution)/shard_map/ppermute | solution.py:30
  117.4 0.1 add_add_fusion.1
  117.5 0.1 maximum_multiply_fusion
  117.6 0.1 mul.27
  117.7 0.8 multiply_subtract_fusion
  (17 shorter events, 0.1 us)
Async XLA Ops:
  0.0 14.4 %copy-start = (s32[1,1,1,8]{3,2,1,0:T(1,128)S(1)}, s32[1,1,1,8]{3,2,1,0:T(1,128)}, u32[]{:S(2)}) copy-start(s32[1,1,1,8]{3,2,1,0:T(1,128)} %param.9) | copy-start | bytes 100
  1.2 15.8 %collective-permute-start = (f32[32,32,128]{2,1,0:T(8,128)S(1)}, f32[32,32,128]{2,1,0:T(8,128)S(1)}, u32[]{:S(2)}, u32[]{:S(2)}) collective-permute-start(f32[32,32,128]{2,1,0:T(8,128)S(1)} %bitcast.15), channel_id=1, source_target_pairs={{0,192},{1,193},{2,194},{3,195},{4,196},{5,197},{6,198},{7,199},{8... | collective-permute-start | bytes 1572872 | tf_op jit(solution)/shard_map/ppermute | solution.py:30
  1.7 25.5 %collective-permute-start.5 = (f32[32,32,128]{2,1,0:T(8,128)S(1)}, f32[32,32,128]{2,1,0:T(8,128)S(1)}, u32[]{:S(2)}, u32[]{:S(2)}) collective-permute-start(f32[32,32,128]{2,1,0:T(8,128)S(1)} %bitcast.16), channel_id=1, source_target_pairs={{0,128},{1,129},{2,130},{3,131},{4,132},{5,133},{6,134},{7,135},{8... | collective-permute-start | bytes 1572872 | tf_op jit(solution)/shard_map/ppermute | solution.py:30
  4.3 23.7 %collective-permute-start.4 = (f32[32,32,128]{2,1,0:T(8,128)S(1)}, f32[32,32,128]{2,1,0:T(8,128)S(1)}, u32[]{:S(2)}, u32[]{:S(2)}) collective-permute-start(f32[32,32,128]{2,1,0:T(8,128)S(1)} %bitcast.17), channel_id=1, source_target_pairs={{0,64},{1,65},{2,66},{3,67},{4,68},{5,69},{6,70},{7,71},{8,72},{9,... | collective-permute-start | bytes 1572872 | tf_op jit(solution)/shard_map/ppermute | solution.py:30
  6.2 30.1 %collective-permute-start.3 = (f32[32,32,128]{2,1,0:T(8,128)S(1)}, f32[32,32,128]{2,1,0:T(8,128)S(1)}, u32[]{:S(2)}, u32[]{:S(2)}) collective-permute-start(f32[32,32,128]{2,1,0:T(8,128)S(1)} %bitcast.18), channel_id=1, source_target_pairs={{0,32},{1,33},{2,34},{3,35},{4,36},{5,37},{6,38},{7,39},{8,40},{9,... | collective-permute-start | bytes 1572872 | tf_op jit(solution)/shard_map/ppermute | solution.py:30
  17.0 29.0 %collective-permute-start.1 = (f32[32,32,128]{2,1,0:T(8,128)S(1)}, f32[32,32,128]{2,1,0:T(8,128)S(1)}, u32[]{:S(2)}, u32[]{:S(2)}) collective-permute-start(f32[32,32,128]{2,1,0:T(8,128)S(1)} %bitcast.21), channel_id=1, source_target_pairs={{0,24},{1,25},{2,26},{3,27},{4,28},{5,29},{6,30},{7,31},{8,0},{9,1... | collective-permute-start | bytes 1572872 | tf_op jit(solution)/shard_map/ppermute | solution.py:30
  36.2 16.4 %collective-permute-start.8 = (f32[32,32,128]{2,1,0:T(8,128)S(1)}, f32[32,32,128]{2,1,0:T(8,128)S(1)}, u32[]{:S(2)}, u32[]{:S(2)}) collective-permute-start(f32[32,32,128]{2,1,0:T(8,128)S(1)} %collective-permute-done.3.refs_7_.refs_5_), channel_id=1, source_target_pairs={{0,128},{1,129},{2,130},{3,131},{4,132},{5,133},{6,134},{7,135},{8... | collective-permute-start | bytes 1572872 | tf_op jit(solution)/shard_map/ppermute | solution.py:30
  37.2 21.2 %collective-permute-start.7 = (f32[32,32,128]{2,1,0:T(8,128)S(1)}, f32[32,32,128]{2,1,0:T(8,128)S(1)}, u32[]{:S(2)}, u32[]{:S(2)}) collective-permute-start(f32[32,32,128]{2,1,0:T(8,128)S(1)} %collective-permute-done.3.refs_7_.refs_5_), channel_id=1, source_target_pairs={{0,64},{1,65},{2,66},{3,67},{4,68},{5,69},{6,70},{7,71},{8,72},{9,... | collective-permute-start | bytes 1572872 | tf_op jit(solution)/shard_map/ppermute | solution.py:30
  37.9 20.8 %collective-permute-start.6 = (f32[32,32,128]{2,1,0:T(8,128)S(1)}, f32[32,32,128]{2,1,0:T(8,128)S(1)}, u32[]{:S(2)}, u32[]{:S(2)}) collective-permute-start(f32[32,32,128]{2,1,0:T(8,128)S(1)} %collective-permute-done.3.refs_7_.refs_5_), channel_id=1, source_target_pairs={{0,192},{1,193},{2,194},{3,195},{4,196},{5,197},{6,198},{7,199},{8... | collective-permute-start | bytes 1572872 | tf_op jit(solution)/shard_map/ppermute | solution.py:30
  46.0 14.5 %collective-permute-start.2 = (f32[32,32,128]{2,1,0:T(8,128)S(1)}, f32[32,32,128]{2,1,0:T(8,128)S(1)}, u32[]{:S(2)}, u32[]{:S(2)}) collective-permute-start(f32[32,32,128]{2,1,0:T(8,128)S(1)} %collective-permute-done.1.refs_3_), channel_id=1, source_target_pairs={{0,24},{1,25},{2,26},{3,27},{4,28},{5,29},{6,30},{7,31},{8,0},{9,1... | collective-permute-start | bytes 1572872 | tf_op jit(solution)/shard_map/ppermute | solution.py:30
  47.7 12.8 %collective-permute-start.10 = (f32[32,32,128]{2,1,0:T(8,128)S(1)}, f32[32,32,128]{2,1,0:T(8,128)S(1)}, u32[]{:S(2)}, u32[]{:S(2)}) collective-permute-start(f32[32,32,128]{2,1,0:T(8,128)S(1)} %bitcast.22), channel_id=1, source_target_pairs={{0,4},{1,5},{2,6},{3,7},{4,0},{5,1},{6,2},{7,3},{8,12},{9,13},{10,... | collective-permute-start | bytes 1572872 | tf_op jit(solution)/shard_map/ppermute | solution.py:30
  52.6 7.9 %collective-permute-start.11 = (f32[32,32,128]{2,1,0:T(8,128)S(1)}, f32[32,32,128]{2,1,0:T(8,128)S(1)}, u32[]{:S(2)}, u32[]{:S(2)}) collective-permute-start(f32[32,32,128]{2,1,0:T(8,128)S(1)} %collective-permute-done.1.refs_3_), channel_id=1, source_target_pairs={{0,4},{1,5},{2,6},{3,7},{4,0},{5,1},{6,2},{7,3},{8,12},{9,13},{10,... | collective-permute-start | bytes 1572872 | tf_op jit(solution)/shard_map/ppermute | solution.py:30
  60.5 1.9 %collective-permute-start.12 = (f32[32,32,128]{2,1,0:T(8,128)S(1)}, f32[32,32,128]{2,1,0:T(8,128)S(1)}, u32[]{:S(2)}, u32[]{:S(2)}) collective-permute-start(f32[32,32,128]{2,1,0:T(8,128)S(1)} %collective-permute-done.2.refs_3_), channel_id=1, source_target_pairs={{0,4},{1,5},{2,6},{3,7},{4,0},{5,1},{6,2},{7,3},{8,12},{9,13},{10,... | collective-permute-start | bytes 1572872 | tf_op jit(solution)/shard_map/ppermute | solution.py:30
  60.5 25.3 %collective-permute-start.9 = (f32[32,32,128]{2,1,0:T(8,128)S(1)}, f32[32,32,128]{2,1,0:T(8,128)S(1)}, u32[]{:S(2)}, u32[]{:S(2)}) collective-permute-start(f32[32,32,128]{2,1,0:T(8,128)S(1)} %collective-permute-done.2.refs_3_), channel_id=1, source_target_pairs={{0,24},{1,25},{2,26},{3,27},{4,28},{5,29},{6,30},{7,31},{8,0},{9,1... | collective-permute-start | bytes 1572872 | tf_op jit(solution)/shard_map/ppermute | solution.py:30
  85.8 1.9 %collective-permute-start.13 = (f32[32,32,128]{2,1,0:T(8,128)S(1)}, f32[32,32,128]{2,1,0:T(8,128)S(1)}, u32[]{:S(2)}, u32[]{:S(2)}) collective-permute-start(f32[32,32,128]{2,1,0:T(8,128)S(1)} %collective-permute-done.9.refs_4_), channel_id=1, source_target_pairs={{0,4},{1,5},{2,6},{3,7},{4,0},{5,1},{6,2},{7,3},{8,12},{9,13},{10,... | collective-permute-start | bytes 1572872 | tf_op jit(solution)/shard_map/ppermute | solution.py:30
  91.8 8.4 %collective-permute-start.18 = (f32[32,16,128]{2,1,0:T(8,128)S(1)}, f32[32,16,128]{2,1,0:T(8,128)S(1)}, u32[]{:S(2)}, u32[]{:S(2)}) collective-permute-start(f32[32,16,128]{2,1,0:T(8,128)S(1)} %get-tuple-element.63), channel_id=1, source_target_pairs={{0,1},{1,2},{2,3},{3,0},{4,5},{5,6},{6,7},{7,4},{8,9},{9,10},{10,1... | collective-permute-start | bytes 786440 | tf_op jit(solution)/shard_map/ppermute | solution.py:30
  92.4 10.3 %collective-permute-start.19 = (f32[32,16,128]{2,1,0:T(8,128)S(1)}, f32[32,16,128]{2,1,0:T(8,128)S(1)}, u32[]{:S(2)}, u32[]{:S(2)}) collective-permute-start(f32[32,16,128]{2,1,0:T(8,128)S(1)} %get-tuple-element.64), channel_id=1, source_target_pairs={{0,3},{1,0},{2,1},{3,2},{4,7},{5,4},{6,5},{7,6},{8,11},{9,8},{10,9... | collective-permute-start | bytes 786440 | tf_op jit(solution)/shard_map/ppermute | solution.py:30
  98.0 8.4 %collective-permute-start.14 = (f32[32,16,128]{2,1,0:T(8,128)S(1)}, f32[32,16,128]{2,1,0:T(8,128)S(1)}, u32[]{:S(2)}, u32[]{:S(2)}) collective-permute-start(f32[32,16,128]{2,1,0:T(8,128)S(1)} %get-tuple-element.54), channel_id=1, source_target_pairs={{0,1},{1,2},{2,3},{3,0},{4,5},{5,6},{6,7},{7,4},{8,9},{9,10},{10,1... | collective-permute-start | bytes 786440 | tf_op jit(solution)/shard_map/ppermute | solution.py:30
  99.8 10.1 %collective-permute-start.15 = (f32[32,16,128]{2,1,0:T(8,128)S(1)}, f32[32,16,128]{2,1,0:T(8,128)S(1)}, u32[]{:S(2)}, u32[]{:S(2)}) collective-permute-start(f32[32,16,128]{2,1,0:T(8,128)S(1)} %get-tuple-element.55), channel_id=1, source_target_pairs={{0,3},{1,0},{2,1},{3,2},{4,7},{5,4},{6,5},{7,6},{8,11},{9,8},{10,9... | collective-permute-start | bytes 786440 | tf_op jit(solution)/shard_map/ppermute | solution.py:30
  102.6 9.5 %collective-permute-start.20 = (f32[16,16,128]{2,1,0:T(8,128)S(1)}, f32[16,16,128]{2,1,0:T(8,128)S(1)}, u32[]{:S(2)}, u32[]{:S(2)}) collective-permute-start(f32[16,16,128]{2,1,0:T(8,128)S(1)} %slice_add_fusion.1), channel_id=1, source_target_pairs={{0,1},{1,2},{2,3},{3,0},{4,5},{5,6},{6,7},{7,4},{8,9},{9,10},{10,1... | collective-permute-start | bytes 393224 | tf_op jit(solution)/shard_map/ppermute | solution.py:30
  103.1 9.5 %collective-permute-start.21 = (f32[16,16,128]{2,1,0:T(8,128)S(1)}, f32[16,16,128]{2,1,0:T(8,128)S(1)}, u32[]{:S(2)}, u32[]{:S(2)}) collective-permute-start(f32[16,16,128]{2,1,0:T(8,128)S(1)} %slice_add_fusion), channel_id=1, source_target_pairs={{0,3},{1,0},{2,1},{3,2},{4,7},{5,4},{6,5},{7,6},{8,11},{9,8},{10,9... | collective-permute-start | bytes 393224 | tf_op jit(solution)/shard_map/ppermute | solution.py:30
  109.9 6.2 %collective-permute-start.16 = (f32[16,16,128]{2,1,0:T(8,128)S(1)}, f32[16,16,128]{2,1,0:T(8,128)S(1)}, u32[]{:S(2)}, u32[]{:S(2)}) collective-permute-start(f32[16,16,128]{2,1,0:T(8,128)S(1)} %slice_add_fusion.3), channel_id=1, source_target_pairs={{0,1},{1,2},{2,3},{3,0},{4,5},{5,6},{6,7},{7,4},{8,9},{9,10},{10,1... | collective-permute-start | bytes 393224 | tf_op jit(solution)/shard_map/ppermute | solution.py:30
  111.1 6.6 %copy-start.1 = (f32[1,1,32,4096]{3,2,1,0:T(8,128)S(1)}, f32[1,1,32,4096]{3,2,1,0:T(8,128)}, u32[]{:S(2)}) copy-start(f32[1,1,32,4096]{3,2,1,0:T(8,128)} %param.7) | copy-start | bytes 1572868
  111.2 6.3 %collective-permute-start.17 = (f32[16,16,128]{2,1,0:T(8,128)S(1)}, f32[16,16,128]{2,1,0:T(8,128)S(1)}, u32[]{:S(2)}, u32[]{:S(2)}) collective-permute-start(f32[16,16,128]{2,1,0:T(8,128)S(1)} %slice_add_fusion.2), channel_id=1, source_target_pairs={{0,3},{1,0},{2,1},{3,2},{4,7},{5,4},{6,5},{7,6},{8,11},{9,8},{10,9... | collective-permute-start | bytes 393224 | tf_op jit(solution)/shard_map/ppermute | solution.py:30

commit v5 on v4

--- a/solution.py
+++ b/solution.py
@@ -215,15 +215,14 @@
     same1, same3, same2 = by_y(right, -1), by_y(right, 1), by_y(right, 2)
     twin0 = swap_core(left)
     acc = add_sections([(0, False, 0, [(0, 0)])], *args, [left], [right], None, "sections_a")
-    same1, acc, left_now = lax.optimization_barrier((same1, acc, left))
+    same1, same3, same2, other0, acc, left_now = lax.optimization_barrier((same1, same3, same2, other0, acc, left))
+
     left1 = by_zl(left_now, -1)
-    other0, same1, same3, same2, acc = lax.optimization_barrier((other0, same1, same3, same2, acc))
-
     other1, other3, other2 = by_y(other0, -1), by_y(other0, 1), by_y(other0, 2)
     left2 = by_zl(left1, -1)
     twin1 = swap_core(left1)
     acc = add_sections([(1, False, 0, [(1, 0)])], *args, [left1], [same1], acc, "sections_b")
-    left2, other1, other3, other2, acc = lax.optimization_barrier((left2, other1, other3, other2, acc))
+    other1, other3, other2, left2, acc = lax.optimization_barrier((other1, other3, other2, left2, acc))
 
     left3 = by_zl(left2, -1)
     twin2 = swap_core(left2)

time: 119 us -> 112 us (0.941)
  the two profiles are of different devices: /device:TPU:46 before, /device:TPU:30 now
where the time goes in v5:
time: 112 us; the launch traced here: 111 us
  waiting for transfers between devices  48.9 us (44%)
  starting transfers between devices  32.6 us (29%)
  Pallas kernels  25.5 us (23%)
  local copies, waits for them, and re-layouts  3.11 us (3%)
  other arithmetic  1.16 us (1%)
    ppermute x22, waiting for transfers between devices, moved(): return lax.ppermute(x, AXES, pairs)  48.9 us
    ppermute x22, starting transfers between devices, moved(): return lax.ppermute(x, AXES, pairs)  32.6 us
    pallas_call x5, Pallas kernels, add_sections(): pl.pallas_call(functools.partial(section_kernel, jobs, len(lefts), len(ri...  25.5 us
    unnamed x7, local copies, waits for them, and re-layouts  3.01 us
  transfers between devices with their start and end apart: 22, of which 15 were waited for; matrix products, arithmetic and copies ran while one was open for 2% of the time, Pallas kernels for 18%

profile of v5, /device:TPU:30, one launch (start us, length us, event | category | flops | bytes accessed | tf_op | source)
XLA Modules:
  0.0 111.4 jit_solution(16262431154343514628)
XLA Ops:
  0.0 1.1 %copy.7 = f32[4,8,32,128]{3,2,1,0:T(8,128)S(1)} copy(f32[4,8,32,128]{3,1,2,0:T(8,128)} %bitcast.33) | data formatting | bytes 1048576
  1.2 7.3 %collective-permute-start.3 = (f32[32,32,128]{2,1,0:T(8,128)S(1)}, f32[32,32,128]{2,1,0:T(8,128)S(1)}, u32[]{:S(2)}, u32[]{:S(2)}) collective-permute-start(f32[32,32,128]{2,1,0:T(8,128)S(1)} %bitcast.15), channel_id=1, source_target_pairs={{0,32},{1,33},{2,34},{3,35},{4,36},{5,37},{6,38},{7,39},{8,40},{9,... | collective-permute-start | bytes 1572872 | tf_op jit(solution)/shard_map/ppermute | solution.py:30
  8.4 1.2 %collective-permute-start.2 = (f32[32,32,128]{2,1,0:T(8,128)S(1)}, f32[32,32,128]{2,1,0:T(8,128)S(1)}, u32[]{:S(2)}, u32[]{:S(2)}) collective-permute-start(f32[32,32,128]{2,1,0:T(8,128)S(1)} %bitcast.16), channel_id=1, source_target_pairs={{0,128},{1,129},{2,130},{3,131},{4,132},{5,133},{6,134},{7,135},{8... | collective-permute-start | bytes 1572872 | tf_op jit(solution)/shard_map/ppermute | solution.py:30
  9.7 2.2 %collective-permute-start.1 = (f32[32,32,128]{2,1,0:T(8,128)S(1)}, f32[32,32,128]{2,1,0:T(8,128)S(1)}, u32[]{:S(2)}, u32[]{:S(2)}) collective-permute-start(f32[32,32,128]{2,1,0:T(8,128)S(1)} %bitcast.17), channel_id=1, source_target_pairs={{0,64},{1,65},{2,66},{3,67},{4,68},{5,69},{6,70},{7,71},{8,72},{9,... | collective-permute-start | bytes 1572872 | tf_op jit(solution)/shard_map/ppermute | solution.py:30
  11.9 0.7 copy.10
  12.6 1.1 %copy.8 = f32[4,8,32,128]{3,2,1,0:T(8,128)S(1)} copy(f32[4,8,32,128]{3,1,2,0:T(8,128)} %bitcast.34) | data formatting | bytes 1048576
  13.7 0.1 pad_add_fusion.refs_0_
  13.8 3.1 %sections_a.1.refs_5_ = f32[129,32,128]{2,1,0:T(8,128)S(1)} custom-call(s32[3]{0:T(128)S(1)} %pad_add_fusion.refs_0_, s32[8,3,64]{2,1,0:T(4,128)S(1)} %bitcast.23, s32[8]{0:T(128)S(1)} %bitcast.28, f32[32,32,128]{2,1,0:T(8,128)S(1)} %bitcast.20, f32[32,32,128]{2,1,0:T(8,128)S(1)} %bitcast.19), custom_call_target="tpu_custom_call" | custom-call | tf_op jit(solution)/shard_map/sections_a/pallas_call | solution.py:172
  16.9 5.7 %collective-permute-done.3.refs_7_.refs_5_ = f32[32,32,128]{2,1,0:T(8,128)S(1)} collective-permute-done((f32[32,32,128]{2,1,0:T(8,128)S(1)}, f32[32,32,128]{2,1,0:T(8,128)S(1)}, u32[]{:S(2)}, u32[]{:S(2)}) %collective-permute-start.3) | collective-permute-done | bytes 524320 | tf_op jit(solution)/shard_map/ppermute | solution.py:30
  22.6 2.2 %collective-permute-done.2.refs_11_ = f32[32,32,128]{2,1,0:T(8,128)S(1)} collective-permute-done((f32[32,32,128]{2,1,0:T(8,128)S(1)}, f32[32,32,128]{2,1,0:T(8,128)S(1)}, u32[]{:S(2)}, u32[]{:S(2)}) %collective-permute-start.2) | collective-permute-done | bytes 524320 | tf_op jit(solution)/shard_map/ppermute | solution.py:30
  24.8 7.3 %collective-permute-done.1.refs_9_ = f32[32,32,128]{2,1,0:T(8,128)S(1)} collective-permute-done((f32[32,32,128]{2,1,0:T(8,128)S(1)}, f32[32,32,128]{2,1,0:T(8,128)S(1)}, u32[]{:S(2)}, u32[]{:S(2)}) %collective-permute-start.1) | collective-permute-done | bytes 524320 | tf_op jit(solution)/shard_map/ppermute | solution.py:30
  32.1 2.4 %collective-permute-done.refs_4_ = f32[32,32,128]{2,1,0:T(8,128)S(1)} collective-permute-done((f32[32,32,128]{2,1,0:T(8,128)S(1)}, f32[32,32,128]{2,1,0:T(8,128)S(1)}, u32[]{:S(2)}, u32[]{:S(2)}) %collective-permute-start) | collective-permute-done | bytes 524320 | tf_op jit(solution)/shard_map/ppermute | solution.py:30
  34.6 1.9 %collective-permute-start.7 = (f32[32,32,128]{2,1,0:T(8,128)S(1)}, f32[32,32,128]{2,1,0:T(8,128)S(1)}, u32[]{:S(2)}, u32[]{:S(2)}) collective-permute-start(f32[32,32,128]{2,1,0:T(8,128)S(1)} %bitcast.21), channel_id=1, source_target_pairs={{0,24},{1,25},{2,26},{3,27},{4,28},{5,29},{6,30},{7,31},{8,0},{9,1... | collective-permute-start | bytes 1572872 | tf_op jit(solution)/shard_map/ppermute | solution.py:30
  36.5 1.4 %collective-permute-start.6 = (f32[32,32,128]{2,1,0:T(8,128)S(1)}, f32[32,32,128]{2,1,0:T(8,128)S(1)}, u32[]{:S(2)}, u32[]{:S(2)}) collective-permute-start(f32[32,32,128]{2,1,0:T(8,128)S(1)} %collective-permute-done.3.refs_7_.refs_5_), channel_id=1, source_target_pairs={{0,128},{1,129},{2,130},{3,131},{4,132},{5,133},{6,134},{7,135},{8... | collective-permute-start | bytes 1572872 | tf_op jit(solution)/shard_map/ppermute | solution.py:30
  37.9 1.2 %collective-permute-start.5 = (f32[32,32,128]{2,1,0:T(8,128)S(1)}, f32[32,32,128]{2,1,0:T(8,128)S(1)}, u32[]{:S(2)}, u32[]{:S(2)}) collective-permute-start(f32[32,32,128]{2,1,0:T(8,128)S(1)} %collective-permute-done.3.refs_7_.refs_5_), channel_id=1, source_target_pairs={{0,64},{1,65},{2,66},{3,67},{4,68},{5,69},{6,70},{7,71},{8,72},{9,... | collective-permute-start | bytes 1572872 | tf_op jit(solution)/shard_map/ppermute | solution.py:30
  39.1 0.8 collective-permute-start.4
  39.9 8.5 %collective-permute-done.7.refs_3_ = f32[32,32,128]{2,1,0:T(8,128)S(1)} collective-permute-done((f32[32,32,128]{2,1,0:T(8,128)S(1)}, f32[32,32,128]{2,1,0:T(8,128)S(1)}, u32[]{:S(2)}, u32[]{:S(2)}) %collective-permute-start.7) | collective-permute-done | bytes 524320 | tf_op jit(solution)/shard_map/ppermute | solution.py:30
  48.4 3.7 %collective-permute-start.8 = (f32[32,32,128]{2,1,0:T(8,128)S(1)}, f32[32,32,128]{2,1,0:T(8,128)S(1)}, u32[]{:S(2)}, u32[]{:S(2)}) collective-permute-start(f32[32,32,128]{2,1,0:T(8,128)S(1)} %collective-permute-done.7.refs_3_), channel_id=1, source_target_pairs={{0,24},{1,25},{2,26},{3,27},{4,28},{5,29},{6,30},{7,31},{8,0},{9,1... | collective-permute-start | bytes 1572872 | tf_op jit(solution)/shard_map/ppermute | solution.py:30
  52.1 3.1 %sections_b.1.refs_12_ = f32[129,32,128]{2,1,0:T(8,128)S(1)} custom-call(s32[3]{0:T(128)S(1)} %pad_add_fusion.refs_0_, s32[8,3,64]{2,1,0:T(4,128)S(1)} %bitcast.24, s32[8]{0:T(128)S(1)} %bitcast.29, f32[32,32,128]{2,1,0:T(8,128)S(1)} %collective-permute-done.7.refs_3_, f32[32,32,128]{2,1,0:T(8,128)S(1)} %collective-permute-done.refs_4_, ...), custom_call_target="tpu_custom_call" | custom-call | tf_op jit(solution)/shard_map/sections_b/pallas_call | solution.py:172
  55.2 0.1 collective-permute-start.11
  55.4 5.0 %collective-permute-done.5.refs_10_.refs_8_ = f32[32,32,128]{2,1,0:T(8,128)S(1)} collective-permute-done((f32[32,32,128]{2,1,0:T(8,128)S(1)}, f32[32,32,128]{2,1,0:T(8,128)S(1)}, u32[]{:S(2)}, u32[]{:S(2)}) %collective-permute-start.5) | collective-permute-done | bytes 524320 | tf_op jit(solution)/shard_map/ppermute | solution.py:30
  60.4 2.4 %collective-permute-done.4.refs_8_.refs_6_ = f32[32,32,128]{2,1,0:T(8,128)S(1)} collective-permute-done((f32[32,32,128]{2,1,0:T(8,128)S(1)}, f32[32,32,128]{2,1,0:T(8,128)S(1)}, u32[]{:S(2)}, u32[]{:S(2)}) %collective-permute-start.4) | collective-permute-done | bytes 524320 | tf_op jit(solution)/shard_map/ppermute | solution.py:30
  62.8 0.0 collective-permute-start.12
  62.8 4.1 %collective-permute-start.9 = (f32[32,32,128]{2,1,0:T(8,128)S(1)}, f32[32,32,128]{2,1,0:T(8,128)S(1)}, u32[]{:S(2)}, u32[]{:S(2)}) collective-permute-start(f32[32,32,128]{2,1,0:T(8,128)S(1)} %collective-permute-done.8.refs_3_), channel_id=1, source_target_pairs={{0,24},{1,25},{2,26},{3,27},{4,28},{5,29},{6,30},{7,31},{8,0},{9,1... | collective-permute-start | bytes 1572872 | tf_op jit(solution)/shard_map/ppermute | solution.py:30
  66.9 9.1 %sections_c.1.refs_10_ = f32[129,32,128]{2,1,0:T(8,128)S(1)} custom-call(s32[3]{0:T(128)S(1)} %pad_add_fusion.refs_0_, s32[8,3,64]{2,1,0:T(4,128)S(1)} %bitcast.25, s32[8]{0:T(128)S(1)} %bitcast.30, f32[32,32,128]{2,1,0:T(8,128)S(1)} %collective-permute-done.8.refs_3_, f32[32,32,128]{2,1,0:T(8,128)S(1)} %collective-permute-done.10.refs_4_, ...), custom_call_target="tpu_custom_call" | custom-call | tf_op jit(solution)/shard_map/sections_c/pallas_call | solution.py:172
  76.1 2.7 %collective-permute-done.9.refs_4_ = f32[32,32,128]{2,1,0:T(8,128)S(1)} collective-permute-done((f32[32,32,128]{2,1,0:T(8,128)S(1)}, f32[32,32,128]{2,1,0:T(8,128)S(1)}, u32[]{:S(2)}, u32[]{:S(2)}) %collective-permute-start.9) | collective-permute-done | bytes 524320 | tf_op jit(solution)/shard_map/ppermute | solution.py:30
  78.8 1.9 %collective-permute-done.13.refs_3_ = f32[32,32,128]{2,1,0:T(8,128)S(1)} collective-permute-done((f32[32,32,128]{2,1,0:T(8,128)S(1)}, f32[32,32,128]{2,1,0:T(8,128)S(1)}, u32[]{:S(2)}, u32[]{:S(2)}) %collective-permute-start.13) | collective-permute-done | bytes 524320 | tf_op jit(solution)/shard_map/ppermute | solution.py:30
  80.7 5.1 %sections_e1.1 = (f32[32,16,128]{2,1,0:T(8,128)S(1)}, f32[16,16,128]{2,1,0:T(8,128)S(1)}, f32[32,16,128]{2,1,0:T(8,128)S(1)}, f32[32,16,128]{2,1,0:T(8,128)S(1)}, f32[16,16,128]{2,1,0:T(8,128)S(1)}) custom-call(s32[3]{0:T(128)S(1)} %pad_add_fusion.refs_0_, s32[8,3,64]{2,1,0:T(4,128)S(1)} %bitcast.26, s32[8]{0:T(128)S(1)} %bitcast.31, ...), custom_call_target="tpu_custom_call" | custom-call | tf_op jit(solution)/shard_map/sections_e1/pallas_call | solution.py:172
  85.8 0.1 collective-permute-start.18
  85.9 2.0 %collective-permute-start.19 = (f32[32,16,128]{2,1,0:T(8,128)S(1)}, f32[32,16,128]{2,1,0:T(8,128)S(1)}, u32[]{:S(2)}, u32[]{:S(2)}) collective-permute-start(f32[32,16,128]{2,1,0:T(8,128)S(1)} %get-tuple-element.60), channel_id=1, source_target_pairs={{0,3},{1,0},{2,1},{3,2},{4,7},{5,4},{6,5},{7,6},{8,11},{9,8},{10,9... | collective-permute-start | bytes 786440 | tf_op jit(solution)/shard_map/ppermute | solution.py:30
  87.9 5.1 %sections_e0.1 = (f32[32,16,128]{2,1,0:T(8,128)S(1)}, f32[16,16,128]{2,1,0:T(8,128)S(1)}, f32[32,16,128]{2,1,0:T(8,128)S(1)}, f32[32,16,128]{2,1,0:T(8,128)S(1)}, f32[16,16,128]{2,1,0:T(8,128)S(1)}) custom-call(s32[3]{0:T(128)S(1)} %pad_add_fusion.refs_0_, s32[8,3,64]{2,1,0:T(4,128)S(1)} %bitcast.27, s32[8]{0:T(128)S(1)} %bitcast.32, ...), custom_call_target="tpu_custom_call" | custom-call | tf_op jit(solution)/shard_map/sections_e0/pallas_call | solution.py:172
  93.0 0.4 collective-permute-start.14
  93.4 1.7 %collective-permute-start.15 = (f32[32,16,128]{2,1,0:T(8,128)S(1)}, f32[32,16,128]{2,1,0:T(8,128)S(1)}, u32[]{:S(2)}, u32[]{:S(2)}) collective-permute-start(f32[32,16,128]{2,1,0:T(8,128)S(1)} %get-tuple-element.51), channel_id=1, source_target_pairs={{0,3},{1,0},{2,1},{3,2},{4,7},{5,4},{6,5},{7,6},{8,11},{9,8},{10,9... | collective-permute-start | bytes 786440 | tf_op jit(solution)/shard_map/ppermute | solution.py:30
  95.1 0.5 collective-permute-done.19
  95.6 1.1 collective-permute-start.20
  96.7 1.1 collective-permute-start.21
  97.8 3.0 %collective-permute-done.14 = f32[32,16,128]{2,1,0:T(8,128)S(1)} collective-permute-done((f32[32,16,128]{2,1,0:T(8,128)S(1)}, f32[32,16,128]{2,1,0:T(8,128)S(1)}, u32[]{:S(2)}, u32[]{:S(2)}) %collective-permute-start.14) | collective-permute-done | bytes 262176 | tf_op jit(solution)/shard_map/ppermute | solution.py:30
  100.8 2.9 %collective-permute-done.15 = f32[32,16,128]{2,1,0:T(8,128)S(1)} collective-permute-done((f32[32,16,128]{2,1,0:T(8,128)S(1)}, f32[32,16,128]{2,1,0:T(8,128)S(1)}, u32[]{:S(2)}, u32[]{:S(2)}) %collective-permute-start.15) | collective-permute-done | bytes 262176 | tf_op jit(solution)/shard_map/ppermute | solution.py:30
  103.8 0.1 collective-permute-start.16
  103.9 0.0 copy-start.1
  103.9 2.1 %collective-permute-start.17 = (f32[16,16,128]{2,1,0:T(8,128)S(1)}, f32[16,16,128]{2,1,0:T(8,128)S(1)}, u32[]{:S(2)}, u32[]{:S(2)}) collective-permute-start(f32[16,16,128]{2,1,0:T(8,128)S(1)} %slice_add_fusion.2), channel_id=1, source_target_pairs={{0,3},{1,0},{2,1},{3,2},{4,7},{5,4},{6,5},{7,6},{8,11},{9,8},{10,9... | collective-permute-start | bytes 393224 | tf_op jit(solution)/shard_map/ppermute | solution.py:30
  106.0 0.2 collective-permute-done.21
  106.2 2.6 %collective-permute-done.16 = f32[16,16,128]{2,1,0:T(8,128)S(1)} collective-permute-done((f32[16,16,128]{2,1,0:T(8,128)S(1)}, f32[16,16,128]{2,1,0:T(8,128)S(1)}, u32[]{:S(2)}, u32[]{:S(2)}) %collective-permute-start.16) | collective-permute-done | bytes 131104 | tf_op jit(solution)/shard_map/ppermute | solution.py:30
  108.8 1.5 %collective-permute-done.17 = f32[16,16,128]{2,1,0:T(8,128)S(1)} collective-permute-done((f32[16,16,128]{2,1,0:T(8,128)S(1)}, f32[16,16,128]{2,1,0:T(8,128)S(1)}, u32[]{:S(2)}, u32[]{:S(2)}) %collective-permute-start.17) | collective-permute-done | bytes 131104 | tf_op jit(solution)/shard_map/ppermute | solution.py:30
  110.3 0.1 add_add_fusion.1
  110.4 0.1 maximum_multiply_fusion
  110.5 0.1 mul.27
  110.6 0.8 multiply_subtract_fusion
  (17 shorter events, 0.1 us)
Async XLA Ops:
  0.0 13.8 %copy-start = (s32[1,1,1,8]{3,2,1,0:T(1,128)S(1)}, s32[1,1,1,8]{3,2,1,0:T(1,128)}, u32[]{:S(2)}) copy-start(s32[1,1,1,8]{3,2,1,0:T(1,128)} %param.9) | copy-start | bytes 100
  1.2 21.5 %collective-permute-start.3 = (f32[32,32,128]{2,1,0:T(8,128)S(1)}, f32[32,32,128]{2,1,0:T(8,128)S(1)}, u32[]{:S(2)}, u32[]{:S(2)}) collective-permute-start(f32[32,32,128]{2,1,0:T(8,128)S(1)} %bitcast.15), channel_id=1, source_target_pairs={{0,32},{1,33},{2,34},{3,35},{4,36},{5,37},{6,38},{7,39},{8,40},{9,... | collective-permute-start | bytes 1572872 | tf_op jit(solution)/shard_map/ppermute | solution.py:30
  8.4 16.4 %collective-permute-start.2 = (f32[32,32,128]{2,1,0:T(8,128)S(1)}, f32[32,32,128]{2,1,0:T(8,128)S(1)}, u32[]{:S(2)}, u32[]{:S(2)}) collective-permute-start(f32[32,32,128]{2,1,0:T(8,128)S(1)} %bitcast.16), channel_id=1, source_target_pairs={{0,128},{1,129},{2,130},{3,131},{4,132},{5,133},{6,134},{7,135},{8... | collective-permute-start | bytes 1572872 | tf_op jit(solution)/shard_map/ppermute | solution.py:30
  9.7 22.5 %collective-permute-start.1 = (f32[32,32,128]{2,1,0:T(8,128)S(1)}, f32[32,32,128]{2,1,0:T(8,128)S(1)}, u32[]{:S(2)}, u32[]{:S(2)}) collective-permute-start(f32[32,32,128]{2,1,0:T(8,128)S(1)} %bitcast.17), channel_id=1, source_target_pairs={{0,64},{1,65},{2,66},{3,67},{4,68},{5,69},{6,70},{7,71},{8,72},{9,... | collective-permute-start | bytes 1572872 | tf_op jit(solution)/shard_map/ppermute | solution.py:30
  11.8 22.7 %collective-permute-start = (f32[32,32,128]{2,1,0:T(8,128)S(1)}, f32[32,32,128]{2,1,0:T(8,128)S(1)}, u32[]{:S(2)}, u32[]{:S(2)}) collective-permute-start(f32[32,32,128]{2,1,0:T(8,128)S(1)} %bitcast.18), channel_id=1, source_target_pairs={{0,192},{1,193},{2,194},{3,195},{4,196},{5,197},{6,198},{7,199},{8... | collective-permute-start | bytes 1572872 | tf_op jit(solution)/shard_map/ppermute | solution.py:30
  34.6 13.8 %collective-permute-start.7 = (f32[32,32,128]{2,1,0:T(8,128)S(1)}, f32[32,32,128]{2,1,0:T(8,128)S(1)}, u32[]{:S(2)}, u32[]{:S(2)}) collective-permute-start(f32[32,32,128]{2,1,0:T(8,128)S(1)} %bitcast.21), channel_id=1, source_target_pairs={{0,24},{1,25},{2,26},{3,27},{4,28},{5,29},{6,30},{7,31},{8,0},{9,1... | collective-permute-start | bytes 1572872 | tf_op jit(solution)/shard_map/ppermute | solution.py:30
  36.5 18.8 %collective-permute-start.6 = (f32[32,32,128]{2,1,0:T(8,128)S(1)}, f32[32,32,128]{2,1,0:T(8,128)S(1)}, u32[]{:S(2)}, u32[]{:S(2)}) collective-permute-start(f32[32,32,128]{2,1,0:T(8,128)S(1)} %collective-permute-done.3.refs_7_.refs_5_), channel_id=1, source_target_pairs={{0,128},{1,129},{2,130},{3,131},{4,132},{5,133},{6,134},{7,135},{8... | collective-permute-start | bytes 1572872 | tf_op jit(solution)/shard_map/ppermute | solution.py:30
  37.9 22.5 %collective-permute-start.5 = (f32[32,32,128]{2,1,0:T(8,128)S(1)}, f32[32,32,128]{2,1,0:T(8,128)S(1)}, u32[]{:S(2)}, u32[]{:S(2)}) collective-permute-start(f32[32,32,128]{2,1,0:T(8,128)S(1)} %collective-permute-done.3.refs_7_.refs_5_), channel_id=1, source_target_pairs={{0,64},{1,65},{2,66},{3,67},{4,68},{5,69},{6,70},{7,71},{8,72},{9,... | collective-permute-start | bytes 1572872 | tf_op jit(solution)/shard_map/ppermute | solution.py:30
  39.1 23.7 %collective-permute-start.4 = (f32[32,32,128]{2,1,0:T(8,128)S(1)}, f32[32,32,128]{2,1,0:T(8,128)S(1)}, u32[]{:S(2)}, u32[]{:S(2)}) collective-permute-start(f32[32,32,128]{2,1,0:T(8,128)S(1)} %collective-permute-done.3.refs_7_.refs_5_), channel_id=1, source_target_pairs={{0,192},{1,193},{2,194},{3,195},{4,196},{5,197},{6,198},{7,199},{8... | collective-permute-start | bytes 1572872 | tf_op jit(solution)/shard_map/ppermute | solution.py:30
  48.4 14.4 %collective-permute-start.8 = (f32[32,32,128]{2,1,0:T(8,128)S(1)}, f32[32,32,128]{2,1,0:T(8,128)S(1)}, u32[]{:S(2)}, u32[]{:S(2)}) collective-permute-start(f32[32,32,128]{2,1,0:T(8,128)S(1)} %collective-permute-done.7.refs_3_), channel_id=1, source_target_pairs={{0,24},{1,25},{2,26},{3,27},{4,28},{5,29},{6,30},{7,31},{8,0},{9,1... | collective-permute-start | bytes 1572872 | tf_op jit(solution)/shard_map/ppermute | solution.py:30
  52.1 14.8 %collective-permute-start.10 = (f32[32,32,128]{2,1,0:T(8,128)S(1)}, f32[32,32,128]{2,1,0:T(8,128)S(1)}, u32[]{:S(2)}, u32[]{:S(2)}) collective-permute-start(f32[32,32,128]{2,1,0:T(8,128)S(1)} %bitcast.22), channel_id=1, source_target_pairs={{0,4},{1,5},{2,6},{3,7},{4,0},{5,1},{6,2},{7,3},{8,12},{9,13},{10,... | collective-permute-start | bytes 1572872 | tf_op jit(solution)/shard_map/ppermute | solution.py:30
  55.2 11.7 %collective-permute-start.11 = (f32[32,32,128]{2,1,0:T(8,128)S(1)}, f32[32,32,128]{2,1,0:T(8,128)S(1)}, u32[]{:S(2)}, u32[]{:S(2)}) collective-permute-start(f32[32,32,128]{2,1,0:T(8,128)S(1)} %collective-permute-done.7.refs_3_), channel_id=1, source_target_pairs={{0,4},{1,5},{2,6},{3,7},{4,0},{5,1},{6,2},{7,3},{8,12},{9,13},{10,... | collective-permute-start | bytes 1572872 | tf_op jit(solution)/shard_map/ppermute | solution.py:30
  62.8 4.1 %collective-permute-start.12 = (f32[32,32,128]{2,1,0:T(8,128)S(1)}, f32[32,32,128]{2,1,0:T(8,128)S(1)}, u32[]{:S(2)}, u32[]{:S(2)}) collective-permute-start(f32[32,32,128]{2,1,0:T(8,128)S(1)} %collective-permute-done.8.refs_3_), channel_id=1, source_target_pairs={{0,4},{1,5},{2,6},{3,7},{4,0},{5,1},{6,2},{7,3},{8,12},{9,13},{10,... | collective-permute-start | bytes 1572872 | tf_op jit(solution)/shard_map/ppermute | solution.py:30
  62.8 16.0 %collective-permute-start.9 = (f32[32,32,128]{2,1,0:T(8,128)S(1)}, f32[32,32,128]{2,1,0:T(8,128)S(1)}, u32[]{:S(2)}, u32[]{:S(2)}) collective-permute-start(f32[32,32,128]{2,1,0:T(8,128)S(1)} %collective-permute-done.8.refs_3_), channel_id=1, source_target_pairs={{0,24},{1,25},{2,26},{3,27},{4,28},{5,29},{6,30},{7,31},{8,0},{9,1... | collective-permute-start | bytes 1572872 | tf_op jit(solution)/shard_map/ppermute | solution.py:30
  78.8 1.9 %collective-permute-start.13 = (f32[32,32,128]{2,1,0:T(8,128)S(1)}, f32[32,32,128]{2,1,0:T(8,128)S(1)}, u32[]{:S(2)}, u32[]{:S(2)}) collective-permute-start(f32[32,32,128]{2,1,0:T(8,128)S(1)} %collective-permute-done.9.refs_4_), channel_id=1, source_target_pairs={{0,4},{1,5},{2,6},{3,7},{4,0},{5,1},{6,2},{7,3},{8,12},{9,13},{10,... | collective-permute-start | bytes 1572872 | tf_op jit(solution)/shard_map/ppermute | solution.py:30
  85.8 9.3 %collective-permute-start.18 = (f32[32,16,128]{2,1,0:T(8,128)S(1)}, f32[32,16,128]{2,1,0:T(8,128)S(1)}, u32[]{:S(2)}, u32[]{:S(2)}) collective-permute-start(f32[32,16,128]{2,1,0:T(8,128)S(1)} %get-tuple-element.59), channel_id=1, source_target_pairs={{0,1},{1,2},{2,3},{3,0},{4,5},{5,6},{6,7},{7,4},{8,9},{9,10},{10,1... | collective-permute-start | bytes 786440 | tf_op jit(solution)/shard_map/ppermute | solution.py:30
  85.9 9.7 %collective-permute-start.19 = (f32[32,16,128]{2,1,0:T(8,128)S(1)}, f32[32,16,128]{2,1,0:T(8,128)S(1)}, u32[]{:S(2)}, u32[]{:S(2)}) collective-permute-start(f32[32,16,128]{2,1,0:T(8,128)S(1)} %get-tuple-element.60), channel_id=1, source_target_pairs={{0,3},{1,0},{2,1},{3,2},{4,7},{5,4},{6,5},{7,6},{8,11},{9,8},{10,9... | collective-permute-start | bytes 786440 | tf_op jit(solution)/shard_map/ppermute | solution.py:30
  93.0 7.9 %collective-permute-start.14 = (f32[32,16,128]{2,1,0:T(8,128)S(1)}, f32[32,16,128]{2,1,0:T(8,128)S(1)}, u32[]{:S(2)}, u32[]{:S(2)}) collective-permute-start(f32[32,16,128]{2,1,0:T(8,128)S(1)} %get-tuple-element.50), channel_id=1, source_target_pairs={{0,1},{1,2},{2,3},{3,0},{4,5},{5,6},{6,7},{7,4},{8,9},{9,10},{10,1... | collective-permute-start | bytes 786440 | tf_op jit(solution)/shard_map/ppermute | solution.py:30
  93.4 10.4 %collective-permute-start.15 = (f32[32,16,128]{2,1,0:T(8,128)S(1)}, f32[32,16,128]{2,1,0:T(8,128)S(1)}, u32[]{:S(2)}, u32[]{:S(2)}) collective-permute-start(f32[32,16,128]{2,1,0:T(8,128)S(1)} %get-tuple-element.51), channel_id=1, source_target_pairs={{0,3},{1,0},{2,1},{3,2},{4,7},{5,4},{6,5},{7,6},{8,11},{9,8},{10,9... | collective-permute-start | bytes 786440 | tf_op jit(solution)/shard_map/ppermute | solution.py:30
  95.6 10.4 %collective-permute-start.20 = (f32[16,16,128]{2,1,0:T(8,128)S(1)}, f32[16,16,128]{2,1,0:T(8,128)S(1)}, u32[]{:S(2)}, u32[]{:S(2)}) collective-permute-start(f32[16,16,128]{2,1,0:T(8,128)S(1)} %slice_add_fusion.1), channel_id=1, source_target_pairs={{0,1},{1,2},{2,3},{3,0},{4,5},{5,6},{6,7},{7,4},{8,9},{9,10},{10,1... | collective-permute-start | bytes 393224 | tf_op jit(solution)/shard_map/ppermute | solution.py:30
  96.7 9.5 %collective-permute-start.21 = (f32[16,16,128]{2,1,0:T(8,128)S(1)}, f32[16,16,128]{2,1,0:T(8,128)S(1)}, u32[]{:S(2)}, u32[]{:S(2)}) collective-permute-start(f32[16,16,128]{2,1,0:T(8,128)S(1)} %slice_add_fusion), channel_id=1, source_target_pairs={{0,3},{1,0},{2,1},{3,2},{4,7},{5,4},{6,5},{7,6},{8,11},{9,8},{10,9... | collective-permute-start | bytes 393224 | tf_op jit(solution)/shard_map/ppermute | solution.py:30
  103.8 5.0 %collective-permute-start.16 = (f32[16,16,128]{2,1,0:T(8,128)S(1)}, f32[16,16,128]{2,1,0:T(8,128)S(1)}, u32[]{:S(2)}, u32[]{:S(2)}) collective-permute-start(f32[16,16,128]{2,1,0:T(8,128)S(1)} %slice_add_fusion.3), channel_id=1, source_target_pairs={{0,1},{1,2},{2,3},{3,0},{4,5},{5,6},{6,7},{7,4},{8,9},{9,10},{10,1... | collective-permute-start | bytes 393224 | tf_op jit(solution)/shard_map/ppermute | solution.py:30
  103.9 6.7 %copy-start.1 = (f32[1,1,32,4096]{3,2,1,0:T(8,128)S(1)}, f32[1,1,32,4096]{3,2,1,0:T(8,128)}, u32[]{:S(2)}) copy-start(f32[1,1,32,4096]{3,2,1,0:T(8,128)} %param.7) | copy-start | bytes 1572868
  103.9 6.4 %collective-permute-start.17 = (f32[16,16,128]{2,1,0:T(8,128)S(1)}, f32[16,16,128]{2,1,0:T(8,128)S(1)}, u32[]{:S(2)}, u32[]{:S(2)}) collective-permute-start(f32[16,16,128]{2,1,0:T(8,128)S(1)} %slice_add_fusion.2), channel_id=1, source_target_pairs={{0,3},{1,0},{2,1},{3,2},{4,7},{5,4},{6,5},{7,6},{8,11},{9,8},{10,9... | collective-permute-start | bytes 393224 | tf_op jit(solution)/shard_map/ppermute | solution.py:30

commit v6 on v5

--- a/solution.py
+++ b/solution.py
@@ -55,17 +55,21 @@
     return high, p - high
 
 
-def section_kernel(jobs, n_left, n_right, has_acc, half, *refs):
+def section_kernel(jobs, later, n_left, n_right, has_acc, half, *refs):
     place, pairs, counts = refs[:3]
     lefts = refs[3 : 3 + n_left]
     rights = refs[3 + n_left : 3 + n_left + n_right]
     rest = refs[3 + n_left + n_right :]
     if has_acc:
         start, rest = rest[0], rest[1:]
+    outs, prepared = (), None
     if half is None:
-        outs, (out, lbuf, rbuf, rows, a3, b3, sem, acc_sem) = (), rest
+        out, rest = rest[0], rest[1:]
+        if later:
+            made, rest = rest[0], rest[1:]
+        lbuf, rbuf, rows, a3, b3, sem, acc_sem = rest
     else:
-        outs, (lbuf, rbuf, rows, a3, b3, sem, acc_sem, out) = rest[:5], rest[5:]
+        prepared, outs, (lbuf, a3, sem, acc_sem, out) = rest[0], rest[1:6], rest[6:]
     shift, core, depth = place[0], place[1], place[2]
     lane = lax.broadcasted_iota(jnp.int32, (32, 128), 1) < 64
     height = out.shape[1]
@@ -79,9 +83,12 @@
         return ref if half is None else ref.at[:, pl.ds(height * half, height)]
 
     def fetch(j):
-        k, odd, left, choices = jobs[j]
+        k, odd, left, choices = (jobs + later)[j]
         slot = j % 2
-        pltpu.make_async_copy(own_rows(lefts[left]), lbuf.at[slot], sem.at[slot, 0]).start()
+        if j < len(jobs):
+            pltpu.make_async_copy(own_rows(lefts[left]), lbuf.at[slot], sem.at[slot, 0]).start()
+        if prepared is not None:
+            return
         if len(choices) == 1:
             pltpu.make_async_copy(rights[choices[0][1]], rbuf.at[slot], sem.at[slot, 1]).start()
         else:
@@ -94,8 +101,28 @@
 
     def wait(j):
         slot = j % 2
-        pltpu.make_async_copy(own_rows(lefts[0]), lbuf.at[slot], sem.at[slot, 0]).wait()
-        pltpu.make_async_copy(rights[0], rbuf.at[slot], sem.at[slot, 1]).wait()
+        if j < len(jobs):
+            pltpu.make_async_copy(own_rows(lefts[0]), lbuf.at[slot], sem.at[slot, 0]).wait()
+        if prepared is None:
+            pltpu.make_async_copy(rights[0], rbuf.at[slot], sem.at[slot, 1]).wait()
+
+    def split_right(slot, target):
+        @pl.loop(0, TILES, unroll=4)
+        def _(t):
+            r = rbuf[slot, t]
+            rr = pltpu.roll(r, 64, 1)
+            rows[t, pl.ds(0, 32, stride=2)] = jnp.where(lane, r, rr)
+            rows[t, pl.ds(1, 32, stride=2)] = jnp.where(lane, rr, r)
+
+        @pl.loop(0, TILES, unroll=4)
+        def _(t):
+            h, low = split(rows[t])
+            h = h.astype(BF16)
+            low = low.astype(BF16)
+            target[t, 0:64] = h
+            target[t, 64:128] = low
+            target[t, 128:192] = h
+            target[t, 192:256] = low
 
     fetch(0)
     if has_acc:
@@ -104,7 +131,7 @@
     else:
         out[...] = jnp.zeros_like(out)
     for j in range(len(jobs)):
-        if j + 1 < len(jobs):
+        if j + 1 < len(jobs + later):
             fetch(j + 1)
         wait(j)
         slot = j % 2
@@ -118,21 +145,12 @@
             a3[t, height : 2 * height, 0:128] = jnp.where(lane_left, hr, h).astype(BF16)
             a3[t, 0:height, 128:256] = jnp.where(lane_left, low, lr).astype(BF16)
             a3[t, height : 2 * height, 128:256] = jnp.where(lane_left, lr, low).astype(BF16)
-            r = rbuf[slot, t]
-            rr = pltpu.roll(r, 64, 1)
-            rows[t, pl.ds(0, 32, stride=2)] = jnp.where(lane, r, rr)
-            rows[t, pl.ds(1, 32, stride=2)] = jnp.where(lane, rr, r)
-
-        @pl.loop(0, TILES, unroll=4)
-        def _(t):
-            h, low = split(rows[t])
-            h = h.astype(BF16)
-            low = low.astype(BF16)
-            b3[t, 0:64] = h
-            b3[t, 64:128] = low
-            b3[t, 128:192] = h
-            b3[t, 192:256] = low
-
+
+        if prepared is None:
+            weights = b3
+            split_right(slot, weights)
+        else:
+            weights = prepared.at[j]
         if j == 0 and has_acc:
             load.wait()
         s = section(jobs[j])
@@ -143,19 +161,26 @@
             sums, slots = [], []
             for u in range(UNROLL):
                 p = block * UNROLL + u
-                c = jnp.dot(a3[pairs[s, 0, p]], b3[pairs[s, 1, p]], preferred_element_type=F32)
+                c = jnp.dot(a3[pairs[s, 0, p]], weights[pairs[s, 1, p]], preferred_element_type=F32)
                 sums.append(jnp.where(lane_left, c[0:height], c[height : 2 * height]))
                 g = lax.rem(pairs[s, 2, p] + (4 - depth) * 32, SLOTS)
                 slots.append(jnp.where(p < live, g, SLOTS))
             for u in range(UNROLL):
                 out[slots[u]] += sums[u]
 
+    for i in range(len(later)):
+        j = len(jobs) + i
+        if j + 1 < len(jobs + later):
+            fetch(j + 1)
+        wait(j)
+        split_right(j % 2, made.at[i])
     for ref, (first, last) in zip(outs, PARTS):
         ref[...] = out[first:last]
 
 
-def add_sections(jobs, place, pattern, limits, lefts, rights, acc, name, half=None):
+def add_sections(jobs, place, pattern, limits, lefts, rights, acc, name, later=[], half=None, prepared=None):
     smem = pl.BlockSpec(memory_space=pltpu.SMEM)
+    vmem = pl.BlockSpec(memory_space=pltpu.VMEM)
     anywhere = pl.BlockSpec(memory_space=pl.ANY)
     operands = [place, pattern, limits, *lefts, *rights]
     specs = [smem] * 3 + [anywhere] * (len(lefts) + len(rights))
@@ -163,31 +188,34 @@
         operands.append(acc)
         specs.append(anywhere)
     height = 32 if half is None else 16
-    vmem = pl.BlockSpec(memory_space=pltpu.VMEM)
-    shape = jax.ShapeDtypeStruct((SLOTS + 1, height, 128), F32)
-    scratch = []
+    scratch = [
+        pltpu.VMEM((2, TILES, height, 128), F32),
+        pltpu.VMEM((2, TILES, 32, 128), F32),
+        pltpu.VMEM((TILES, 64, 128), F32),
+        pltpu.VMEM((TILES, 2 * height, 256), BF16),
+        pltpu.VMEM((TILES, 256, 128), BF16),
+        pltpu.SemaphoreType.DMA((2, 2)),
+        pltpu.SemaphoreType.DMA((1,)),
+    ]
+    shapes = [jax.ShapeDtypeStruct((SLOTS + 1, height, 128), F32)]
+    if later:
+        shapes.append(jax.ShapeDtypeStruct((len(later), TILES, 256, 128), BF16))
     if half is not None:
-        shape = [jax.ShapeDtypeStruct((last - first, height, 128), F32) for first, last in PARTS]
-        scratch = [pltpu.VMEM((SLOTS + 1, height, 128), F32)]
-    return pl.pallas_call(
-        functools.partial(section_kernel, jobs, len(lefts), len(rights), acc is not None, half),
-        out_shape=shape,
+        operands.append(prepared)
+        specs.append(vmem)
+        shapes = [jax.ShapeDtypeStruct((last - first, height, 128), F32) for first, last in PARTS]
+        scratch = [scratch[0], scratch[3], *scratch[5:], pltpu.VMEM((SLOTS + 1, height, 128), F32)]
+    out = pl.pallas_call(
+        functools.partial(section_kernel, jobs, later, len(lefts), len(rights), acc is not None, half),
+        out_shape=shapes,
         in_specs=specs,
-        out_specs=vmem if half is None else [vmem] * len(PARTS),
-        scratch_shapes=[
-            pltpu.VMEM((2, TILES, height, 128), F32),
-            pltpu.VMEM((2, TILES, 32, 128), F32),
-            pltpu.VMEM((TILES, 64, 128), F32),
-            pltpu.VMEM((TILES, 2 * height, 256), BF16),
-            pltpu.VMEM((TILES, 256, 128), BF16),
-            pltpu.SemaphoreType.DMA((2, 2)),
-            pltpu.SemaphoreType.DMA((1,)),
-        ]
-        + scratch,
-        compiler_params=pltpu.CompilerParams(vmem_limit_bytes=24 << 20),
+        out_specs=[vmem] * len(shapes),
+        scratch_shapes=scratch,
+        compiler_params=pltpu.CompilerParams(vmem_limit_bytes=28 << 20),
         cost_estimate=pl.CostEstimate(flops=0, bytes_accessed=0, transcendentals=0),
         name=name,
     )(*operands)
+    return out[0] if len(out) == 1 else out
 
 
 def reduce_over_depth(parts):
@@ -215,26 +243,29 @@
     same1, same3, same2 = by_y(right, -1), by_y(right, 1), by_y(right, 2)
     twin0 = swap_core(left)
     acc = add_sections([(0, False, 0, [(0, 0)])], *args, [left], [right], None, "sections_a")
-    same1, same3, same2, other0, acc, left_now = lax.optimization_barrier((same1, same3, same2, other0, acc, left))
-
-    left1 = by_zl(left_now, -1)
+    other0, acc, left = lax.optimization_barrier((other0, acc, left))
+    left1 = by_zl(left, -1)
+    same1, same3, same2, other0, acc = lax.optimization_barrier((same1, same3, same2, other0, acc))
+
     other1, other3, other2 = by_y(other0, -1), by_y(other0, 1), by_y(other0, 2)
     left2 = by_zl(left1, -1)
     twin1 = swap_core(left1)
     acc = add_sections([(1, False, 0, [(1, 0)])], *args, [left1], [same1], acc, "sections_b")
-    other1, other3, other2, left2, acc = lax.optimization_barrier((other1, other3, other2, left2, acc))
+    other1, other3, left2, acc = lax.optimization_barrier((other1, other3, left2, acc))
 
     left3 = by_zl(left2, -1)
     twin2 = swap_core(left2)
     other = [other0, other1, other2, other3]
     jobs = [(2, False, 0, [(2, 4)])] + [(k, True, k + 1, choices) for k in range(3)]
-    acc = add_sections(jobs, *args, [left2, twin0, twin1, twin2], other + [same2], acc, "sections_c")
-
-    jobs = [(3, False, 1, [(3, 4)]), (3, True, 0, choices)]
+    last = [(3, False, 1, [(3, 5)]), (3, True, 0, choices)]
+    acc, prepared = add_sections(
+        jobs, *args, [left2, twin0, twin1, twin2], other + [same2, same3], acc, "sections_c", last
+    )
+
     left3, acc = lax.optimization_barrier((left3, acc))
     twin3 = swap_core(left3)
     share = [
-        add_sections(jobs, *args, [twin3, left3], other + [same3], acc, f"sections_e{h}", h) for h in range(2)
+        add_sections(last, *args, [twin3, left3], [], acc, f"sections_e{h}", [], h, prepared) for h in range(2)
     ]
     share = [reduce_over_depth(half) for half in share]
     share = jnp.concatenate(share, axis=1)

time: 112 us -> 109 us (0.973); the launches traced: 111 us -> 107 us
  waiting for transfers between devices: 48.9 us -> 35.5 us
  Pallas kernels: 25.5 us -> 30.3 us
  starting transfers between devices: 32.6 us -> 36.5 us
    ppermute x22, waiting for transfers between devices: 48.9 us -> 35.5 us  [moved(): return lax.ppermute(x, AXES, pairs)]
    pallas_call x5, Pallas kernels: 25.5 us -> 30.3 us  [add_sections(): pl.pallas_call(functools.partial(section_kernel, jobs, later, len(lefts),...]
    ppermute x22, starting transfers between devices: 32.6 us -> 36.5 us  [moved(): return lax.ppermute(x, AXES, pairs)]
  transfers between devices with their start and end apart: 22 -> 22, of which waited for: 15 -> 13; matrix products, arithmetic and copies ran while one was open for 2% -> 2% of each run, Pallas kernels for 18% -> 24%
where the time goes in v6:
time: 109 us; the launch traced here: 107 us
  starting transfers between devices  36.5 us (33%)
  waiting for transfers between devices  35.5 us (33%)
  Pallas kernels  30.3 us (28%)
  local copies, waits for them, and re-layouts  3.11 us (3%)
  other arithmetic  1.17 us (1%)
    ppermute x22, starting transfers between devices, moved(): return lax.ppermute(x, AXES, pairs)  36.5 us
    ppermute x22, waiting for transfers between devices, moved(): return lax.ppermute(x, AXES, pairs)  35.5 us
    pallas_call x5, Pallas kernels, add_sections(): pl.pallas_call(functools.partial(section_kernel, jobs, later, len(lefts),...  30.3 us
    unnamed x7, local copies, waits for them, and re-layouts  3.01 us
  transfers between devices with their start and end apart: 22, of which 13 were waited for; matrix products, arithmetic and copies ran while one was open for 2% of the time, Pallas kernels for 24%

profile of v6, /device:TPU:30, one launch (start us, length us, event | category | flops | bytes accessed | tf_op | source)
XLA Modules:
  0.0 106.7 jit_solution(11285648576677557813)
XLA Ops:
  0.0 1.1 %copy.7 = f32[4,8,32,128]{3,2,1,0:T(8,128)S(1)} copy(f32[4,8,32,128]{3,1,2,0:T(8,128)} %bitcast.33) | data formatting | bytes 1048576
  1.2 7.3 %collective-permute-start.3 = (f32[32,32,128]{2,1,0:T(8,128)S(1)}, f32[32,32,128]{2,1,0:T(8,128)S(1)}, u32[]{:S(2)}, u32[]{:S(2)}) collective-permute-start(f32[32,32,128]{2,1,0:T(8,128)S(1)} %bitcast.15), channel_id=1, source_target_pairs={{0,32},{1,33},{2,34},{3,35},{4,36},{5,37},{6,38},{7,39},{8,40},{9,... | collective-permute-start | bytes 1572872 | tf_op jit(solution)/shard_map/ppermute | solution.py:30
  8.4 1.2 %collective-permute-start.2 = (f32[32,32,128]{2,1,0:T(8,128)S(1)}, f32[32,32,128]{2,1,0:T(8,128)S(1)}, u32[]{:S(2)}, u32[]{:S(2)}) collective-permute-start(f32[32,32,128]{2,1,0:T(8,128)S(1)} %bitcast.16), channel_id=1, source_target_pairs={{0,128},{1,129},{2,130},{3,131},{4,132},{5,133},{6,134},{7,135},{8... | collective-permute-start | bytes 1572872 | tf_op jit(solution)/shard_map/ppermute | solution.py:30
  9.7 2.2 %collective-permute-start.1 = (f32[32,32,128]{2,1,0:T(8,128)S(1)}, f32[32,32,128]{2,1,0:T(8,128)S(1)}, u32[]{:S(2)}, u32[]{:S(2)}) collective-permute-start(f32[32,32,128]{2,1,0:T(8,128)S(1)} %bitcast.17), channel_id=1, source_target_pairs={{0,64},{1,65},{2,66},{3,67},{4,68},{5,69},{6,70},{7,71},{8,72},{9,... | collective-permute-start | bytes 1572872 | tf_op jit(solution)/shard_map/ppermute | solution.py:30
  11.8 0.0 collective-permute-start
  11.9 0.7 copy.10
  12.6 0.1 pad_add_fusion.refs_0_
  12.6 1.1 %copy.8 = f32[4,8,32,128]{3,2,1,0:T(8,128)S(1)} copy(f32[4,8,32,128]{3,1,2,0:T(8,128)} %bitcast.34) | data formatting | bytes 1048576
  13.8 3.7 %sections_a.1.refs_5_ = f32[129,32,128]{2,1,0:T(8,128)S(1)} custom-call(s32[3]{0:T(128)S(1)} %pad_add_fusion.refs_0_, s32[8,3,64]{2,1,0:T(4,128)S(1)} %bitcast.23, s32[8]{0:T(128)S(1)} %bitcast.28, f32[32,32,128]{2,1,0:T(8,128)S(1)} %bitcast.20, f32[32,32,128]{2,1,0:T(8,128)S(1)} %bitcast.19), custom_call_target="tpu_custom_call" | custom-call | tf_op jit(solution)/shard_map/sections_a/pallas_call | solution.py:208
  17.5 5.1 %collective-permute-done.3.refs_7_ = f32[32,32,128]{2,1,0:T(8,128)S(1)} collective-permute-done((f32[32,32,128]{2,1,0:T(8,128)S(1)}, f32[32,32,128]{2,1,0:T(8,128)S(1)}, u32[]{:S(2)}, u32[]{:S(2)}) %collective-permute-start.3) | collective-permute-done | bytes 524320 | tf_op jit(solution)/shard_map/ppermute | solution.py:30
  22.6 7.0 %collective-permute-start.6 = (f32[32,32,128]{2,1,0:T(8,128)S(1)}, f32[32,32,128]{2,1,0:T(8,128)S(1)}, u32[]{:S(2)}, u32[]{:S(2)}) collective-permute-start(f32[32,32,128]{2,1,0:T(8,128)S(1)} %bitcast.21), channel_id=1, source_target_pairs={{0,24},{1,25},{2,26},{3,27},{4,28},{5,29},{6,30},{7,31},{8,0},{9,1... | collective-permute-start | bytes 1572872 | tf_op jit(solution)/shard_map/ppermute | solution.py:30
  29.6 0.0 collective-permute-done.2.refs_11_
  29.6 2.5 %collective-permute-done.1.refs_12_ = f32[32,32,128]{2,1,0:T(8,128)S(1)} collective-permute-done((f32[32,32,128]{2,1,0:T(8,128)S(1)}, f32[32,32,128]{2,1,0:T(8,128)S(1)}, u32[]{:S(2)}, u32[]{:S(2)}) %collective-permute-start.1) | collective-permute-done | bytes 524320 | tf_op jit(solution)/shard_map/ppermute | solution.py:30
  32.1 2.4 %collective-permute-done.refs_4_ = f32[32,32,128]{2,1,0:T(8,128)S(1)} collective-permute-done((f32[32,32,128]{2,1,0:T(8,128)S(1)}, f32[32,32,128]{2,1,0:T(8,128)S(1)}, u32[]{:S(2)}, u32[]{:S(2)}) %collective-permute-start) | collective-permute-done | bytes 524320 | tf_op jit(solution)/shard_map/ppermute | solution.py:30
  34.6 0.6 collective-permute-start.5
  35.2 1.4 %collective-permute-start.4 = (f32[32,32,128]{2,1,0:T(8,128)S(1)}, f32[32,32,128]{2,1,0:T(8,128)S(1)}, u32[]{:S(2)}, u32[]{:S(2)}) collective-permute-start(f32[32,32,128]{2,1,0:T(8,128)S(1)} %collective-permute-done.3.refs_7_), channel_id=1, source_target_pairs={{0,192},{1,193},{2,194},{3,195},{4,196},{5,197},{6,198},{7,199},{8... | collective-permute-start | bytes 1572872 | tf_op jit(solution)/shard_map/ppermute | solution.py:30
  36.6 7.4 %collective-permute-done.6.refs_3_ = f32[32,32,128]{2,1,0:T(8,128)S(1)} collective-permute-done((f32[32,32,128]{2,1,0:T(8,128)S(1)}, f32[32,32,128]{2,1,0:T(8,128)S(1)}, u32[]{:S(2)}, u32[]{:S(2)}) %collective-permute-start.6) | collective-permute-done | bytes 524320 | tf_op jit(solution)/shard_map/ppermute | solution.py:30
  44.0 1.8 %collective-permute-start.7 = (f32[32,32,128]{2,1,0:T(8,128)S(1)}, f32[32,32,128]{2,1,0:T(8,128)S(1)}, u32[]{:S(2)}, u32[]{:S(2)}) collective-permute-start(f32[32,32,128]{2,1,0:T(8,128)S(1)} %collective-permute-done.6.refs_3_), channel_id=1, source_target_pairs={{0,24},{1,25},{2,26},{3,27},{4,28},{5,29},{6,30},{7,31},{8,0},{9,1... | collective-permute-start | bytes 1572872 | tf_op jit(solution)/shard_map/ppermute | solution.py:30
  45.8 1.2 %collective-permute-start.12 = (f32[32,32,128]{2,1,0:T(8,128)S(1)}, f32[32,32,128]{2,1,0:T(8,128)S(1)}, u32[]{:S(2)}, u32[]{:S(2)}) collective-permute-start(f32[32,32,128]{2,1,0:T(8,128)S(1)} %collective-permute-done.3.refs_7_), channel_id=1, source_target_pairs={{0,128},{1,129},{2,130},{3,131},{4,132},{5,133},{6,134},{7,135},{8... | collective-permute-start | bytes 1572872 | tf_op jit(solution)/shard_map/ppermute | solution.py:30
  47.0 3.7 %sections_b.1.refs_13_ = f32[129,32,128]{2,1,0:T(8,128)S(1)} custom-call(s32[3]{0:T(128)S(1)} %pad_add_fusion.refs_0_, s32[8,3,64]{2,1,0:T(4,128)S(1)} %bitcast.24, s32[8]{0:T(128)S(1)} %bitcast.29, f32[32,32,128]{2,1,0:T(8,128)S(1)} %collective-permute-done.6.refs_3_, f32[32,32,128]{2,1,0:T(8,128)S(1)} %collective-permute-done.refs_4_, ...), custom_call_target="tpu_custom_call" | custom-call | tf_op jit(solution)/shard_map/sections_b/pallas_call | solution.py:208
  50.7 0.1 collective-permute-start.10
  50.8 5.7 %collective-permute-done.7.refs_3_ = f32[32,32,128]{2,1,0:T(8,128)S(1)} collective-permute-done((f32[32,32,128]{2,1,0:T(8,128)S(1)}, f32[32,32,128]{2,1,0:T(8,128)S(1)}, u32[]{:S(2)}, u32[]{:S(2)}) %collective-permute-start.7) | collective-permute-done | bytes 524320 | tf_op jit(solution)/shard_map/ppermute | solution.py:30
  56.6 4.3 %collective-permute-start.8 = (f32[32,32,128]{2,1,0:T(8,128)S(1)}, f32[32,32,128]{2,1,0:T(8,128)S(1)}, u32[]{:S(2)}, u32[]{:S(2)}) collective-permute-start(f32[32,32,128]{2,1,0:T(8,128)S(1)} %collective-permute-done.7.refs_3_), channel_id=1, source_target_pairs={{0,24},{1,25},{2,26},{3,27},{4,28},{5,29},{6,30},{7,31},{8,0},{9,1... | collective-permute-start | bytes 1572872 | tf_op jit(solution)/shard_map/ppermute | solution.py:30
  60.9 0.7 collective-permute-done.12.refs_9_
  61.6 13.9 %sections_c.1 = (f32[129,32,128]{2,1,0:T(8,128)S(1)}, bf16[2,32,256,128]{3,2,1,0:T(8,128)(2,1)S(1)}) custom-call(s32[3]{0:T(128)S(1)} %pad_add_fusion.refs_0_, s32[8,3,64]{2,1,0:T(4,128)S(1)} %bitcast.25, s32[8]{0:T(128)S(1)} %bitcast.30, f32[32,32,128]{2,1,0:T(8,128)S(1)} %collective-permute-done.7.refs_3_, ...), custom_call_target="tpu_custom_call" | custom-call | tf_op jit(solution)/shard_map/sections_c/pallas_call | solution.py:208
  75.5 0.1 collective-permute-start.13
  75.6 1.9 %collective-permute-done.13.refs_3_ = f32[32,32,128]{2,1,0:T(8,128)S(1)} collective-permute-done((f32[32,32,128]{2,1,0:T(8,128)S(1)}, f32[32,32,128]{2,1,0:T(8,128)S(1)}, u32[]{:S(2)}, u32[]{:S(2)}) %collective-permute-start.13) | collective-permute-done | bytes 524320 | tf_op jit(solution)/shard_map/ppermute | solution.py:30
  77.5 4.5 %sections_e1.1 = (f32[32,16,128]{2,1,0:T(8,128)S(1)}, f32[16,16,128]{2,1,0:T(8,128)S(1)}, f32[32,16,128]{2,1,0:T(8,128)S(1)}, f32[32,16,128]{2,1,0:T(8,128)S(1)}, f32[16,16,128]{2,1,0:T(8,128)S(1)}) custom-call(s32[3]{0:T(128)S(1)} %pad_add_fusion.refs_0_, s32[8,3,64]{2,1,0:T(4,128)S(1)} %bitcast.26, s32[8]{0:T(128)S(1)} %bitcast.31, ...), custom_call_target="tpu_custom_call" | custom-call | tf_op jit(solution)/shard_map/sections_e1/pallas_call | solution.py:208
  82.0 0.5 collective-permute-start.18
  82.5 1.6 %collective-permute-start.19 = (f32[32,16,128]{2,1,0:T(8,128)S(1)}, f32[32,16,128]{2,1,0:T(8,128)S(1)}, u32[]{:S(2)}, u32[]{:S(2)}) collective-permute-start(f32[32,16,128]{2,1,0:T(8,128)S(1)} %get-tuple-element.66), channel_id=1, source_target_pairs={{0,3},{1,0},{2,1},{3,2},{4,7},{5,4},{6,5},{7,6},{8,11},{9,8},{10,9... | collective-permute-start | bytes 786440 | tf_op jit(solution)/shard_map/ppermute | solution.py:30
  84.1 4.5 %sections_e0.1 = (f32[32,16,128]{2,1,0:T(8,128)S(1)}, f32[16,16,128]{2,1,0:T(8,128)S(1)}, f32[32,16,128]{2,1,0:T(8,128)S(1)}, f32[32,16,128]{2,1,0:T(8,128)S(1)}, f32[16,16,128]{2,1,0:T(8,128)S(1)}) custom-call(s32[3]{0:T(128)S(1)} %pad_add_fusion.refs_0_, s32[8,3,64]{2,1,0:T(4,128)S(1)} %bitcast.27, s32[8]{0:T(128)S(1)} %bitcast.32, ...), custom_call_target="tpu_custom_call" | custom-call | tf_op jit(solution)/shard_map/sections_e0/pallas_call | solution.py:208
  88.6 1.7 %collective-permute-start.14 = (f32[32,16,128]{2,1,0:T(8,128)S(1)}, f32[32,16,128]{2,1,0:T(8,128)S(1)}, u32[]{:S(2)}, u32[]{:S(2)}) collective-permute-start(f32[32,16,128]{2,1,0:T(8,128)S(1)} %get-tuple-element.56), channel_id=1, source_target_pairs={{0,1},{1,2},{2,3},{3,0},{4,5},{5,6},{6,7},{7,4},{8,9},{9,10},{10,1... | collective-permute-start | bytes 786440 | tf_op jit(solution)/shard_map/ppermute | solution.py:30
  90.3 0.4 collective-permute-start.15
  90.7 0.1 collective-permute-done.19
  90.8 2.8 %collective-permute-start.20 = (f32[16,16,128]{2,1,0:T(8,128)S(1)}, f32[16,16,128]{2,1,0:T(8,128)S(1)}, u32[]{:S(2)}, u32[]{:S(2)}) collective-permute-start(f32[16,16,128]{2,1,0:T(8,128)S(1)} %slice_add_fusion.1), channel_id=1, source_target_pairs={{0,1},{1,2},{2,3},{3,0},{4,5},{5,6},{6,7},{7,4},{8,9},{9,10},{10,1... | collective-permute-start | bytes 393224 | tf_op jit(solution)/shard_map/ppermute | solution.py:30
  93.7 0.1 collective-permute-start.21
  93.8 2.7 %collective-permute-done.14 = f32[32,16,128]{2,1,0:T(8,128)S(1)} collective-permute-done((f32[32,16,128]{2,1,0:T(8,128)S(1)}, f32[32,16,128]{2,1,0:T(8,128)S(1)}, u32[]{:S(2)}, u32[]{:S(2)}) %collective-permute-start.14) | collective-permute-done | bytes 262176 | tf_op jit(solution)/shard_map/ppermute | solution.py:30
  96.4 2.5 %collective-permute-done.15 = f32[32,16,128]{2,1,0:T(8,128)S(1)} collective-permute-done((f32[32,16,128]{2,1,0:T(8,128)S(1)}, f32[32,16,128]{2,1,0:T(8,128)S(1)}, u32[]{:S(2)}, u32[]{:S(2)}) %collective-permute-start.15) | collective-permute-done | bytes 262176 | tf_op jit(solution)/shard_map/ppermute | solution.py:30
  99.0 0.3 collective-permute-start.16
  99.3 0.0 copy-start.1
  99.3 1.9 %collective-permute-start.17 = (f32[16,16,128]{2,1,0:T(8,128)S(1)}, f32[16,16,128]{2,1,0:T(8,128)S(1)}, u32[]{:S(2)}, u32[]{:S(2)}) collective-permute-start(f32[16,16,128]{2,1,0:T(8,128)S(1)} %slice_add_fusion.2), channel_id=1, source_target_pairs={{0,3},{1,0},{2,1},{3,2},{4,7},{5,4},{6,5},{7,6},{8,11},{9,8},{10,9... | collective-permute-start | bytes 393224 | tf_op jit(solution)/shard_map/ppermute | solution.py:30
  101.2 0.2 collective-permute-done.21
  101.4 2.7 %collective-permute-done.16 = f32[16,16,128]{2,1,0:T(8,128)S(1)} collective-permute-done((f32[16,16,128]{2,1,0:T(8,128)S(1)}, f32[16,16,128]{2,1,0:T(8,128)S(1)}, u32[]{:S(2)}, u32[]{:S(2)}) %collective-permute-start.16) | collective-permute-done | bytes 131104 | tf_op jit(solution)/shard_map/ppermute | solution.py:30
  104.0 1.5 %collective-permute-done.17 = f32[16,16,128]{2,1,0:T(8,128)S(1)} collective-permute-done((f32[16,16,128]{2,1,0:T(8,128)S(1)}, f32[16,16,128]{2,1,0:T(8,128)S(1)}, u32[]{:S(2)}, u32[]{:S(2)}) %collective-permute-start.17) | collective-permute-done | bytes 131104 | tf_op jit(solution)/shard_map/ppermute | solution.py:30
  105.6 0.1 add_add_fusion.1
  105.7 0.1 maximum_multiply_fusion
  105.8 0.1 mul.27
  105.9 0.8 multiply_subtract_fusion
  (17 shorter events, 0.1 us)
Async XLA Ops:
  0.0 13.8 %copy-start = (s32[1,1,1,8]{3,2,1,0:T(1,128)S(1)}, s32[1,1,1,8]{3,2,1,0:T(1,128)}, u32[]{:S(2)}) copy-start(s32[1,1,1,8]{3,2,1,0:T(1,128)} %param.9) | copy-start | bytes 100
  1.2 21.5 %collective-permute-start.3 = (f32[32,32,128]{2,1,0:T(8,128)S(1)}, f32[32,32,128]{2,1,0:T(8,128)S(1)}, u32[]{:S(2)}, u32[]{:S(2)}) collective-permute-start(f32[32,32,128]{2,1,0:T(8,128)S(1)} %bitcast.15), channel_id=1, source_target_pairs={{0,32},{1,33},{2,34},{3,35},{4,36},{5,37},{6,38},{7,39},{8,40},{9,... | collective-permute-start | bytes 1572872 | tf_op jit(solution)/shard_map/ppermute | solution.py:30
  8.4 21.2 %collective-permute-start.2 = (f32[32,32,128]{2,1,0:T(8,128)S(1)}, f32[32,32,128]{2,1,0:T(8,128)S(1)}, u32[]{:S(2)}, u32[]{:S(2)}) collective-permute-start(f32[32,32,128]{2,1,0:T(8,128)S(1)} %bitcast.16), channel_id=1, source_target_pairs={{0,128},{1,129},{2,130},{3,131},{4,132},{5,133},{6,134},{7,135},{8... | collective-permute-start | bytes 1572872 | tf_op jit(solution)/shard_map/ppermute | solution.py:30
  9.7 22.5 %collective-permute-start.1 = (f32[32,32,128]{2,1,0:T(8,128)S(1)}, f32[32,32,128]{2,1,0:T(8,128)S(1)}, u32[]{:S(2)}, u32[]{:S(2)}) collective-permute-start(f32[32,32,128]{2,1,0:T(8,128)S(1)} %bitcast.17), channel_id=1, source_target_pairs={{0,64},{1,65},{2,66},{3,67},{4,68},{5,69},{6,70},{7,71},{8,72},{9,... | collective-permute-start | bytes 1572872 | tf_op jit(solution)/shard_map/ppermute | solution.py:30
  11.8 22.7 %collective-permute-start = (f32[32,32,128]{2,1,0:T(8,128)S(1)}, f32[32,32,128]{2,1,0:T(8,128)S(1)}, u32[]{:S(2)}, u32[]{:S(2)}) collective-permute-start(f32[32,32,128]{2,1,0:T(8,128)S(1)} %bitcast.18), channel_id=1, source_target_pairs={{0,192},{1,193},{2,194},{3,195},{4,196},{5,197},{6,198},{7,199},{8... | collective-permute-start | bytes 1572872 | tf_op jit(solution)/shard_map/ppermute | solution.py:30
  22.6 21.4 %collective-permute-start.6 = (f32[32,32,128]{2,1,0:T(8,128)S(1)}, f32[32,32,128]{2,1,0:T(8,128)S(1)}, u32[]{:S(2)}, u32[]{:S(2)}) collective-permute-start(f32[32,32,128]{2,1,0:T(8,128)S(1)} %bitcast.21), channel_id=1, source_target_pairs={{0,24},{1,25},{2,26},{3,27},{4,28},{5,29},{6,30},{7,31},{8,0},{9,1... | collective-permute-start | bytes 1572872 | tf_op jit(solution)/shard_map/ppermute | solution.py:30
  34.6 16.2 %collective-permute-start.5 = (f32[32,32,128]{2,1,0:T(8,128)S(1)}, f32[32,32,128]{2,1,0:T(8,128)S(1)}, u32[]{:S(2)}, u32[]{:S(2)}) collective-permute-start(f32[32,32,128]{2,1,0:T(8,128)S(1)} %collective-permute-done.3.refs_7_), channel_id=1, source_target_pairs={{0,64},{1,65},{2,66},{3,67},{4,68},{5,69},{6,70},{7,71},{8,72},{9,... | collective-permute-start | bytes 1572872 | tf_op jit(solution)/shard_map/ppermute | solution.py:30
  35.2 15.7 %collective-permute-start.4 = (f32[32,32,128]{2,1,0:T(8,128)S(1)}, f32[32,32,128]{2,1,0:T(8,128)S(1)}, u32[]{:S(2)}, u32[]{:S(2)}) collective-permute-start(f32[32,32,128]{2,1,0:T(8,128)S(1)} %collective-permute-done.3.refs_7_), channel_id=1, source_target_pairs={{0,192},{1,193},{2,194},{3,195},{4,196},{5,197},{6,198},{7,199},{8... | collective-permute-start | bytes 1572872 | tf_op jit(solution)/shard_map/ppermute | solution.py:30
  44.0 12.6 %collective-permute-start.7 = (f32[32,32,128]{2,1,0:T(8,128)S(1)}, f32[32,32,128]{2,1,0:T(8,128)S(1)}, u32[]{:S(2)}, u32[]{:S(2)}) collective-permute-start(f32[32,32,128]{2,1,0:T(8,128)S(1)} %collective-permute-done.6.refs_3_), channel_id=1, source_target_pairs={{0,24},{1,25},{2,26},{3,27},{4,28},{5,29},{6,30},{7,31},{8,0},{9,1... | collective-permute-start | bytes 1572872 | tf_op jit(solution)/shard_map/ppermute | solution.py:30
  45.8 15.1 %collective-permute-start.9 = (f32[32,32,128]{2,1,0:T(8,128)S(1)}, f32[32,32,128]{2,1,0:T(8,128)S(1)}, u32[]{:S(2)}, u32[]{:S(2)}) collective-permute-start(f32[32,32,128]{2,1,0:T(8,128)S(1)} %bitcast.22), channel_id=1, source_target_pairs={{0,4},{1,5},{2,6},{3,7},{4,0},{5,1},{6,2},{7,3},{8,12},{9,13},{10,... | collective-permute-start | bytes 1572872 | tf_op jit(solution)/shard_map/ppermute | solution.py:30
  45.8 15.8 %collective-permute-start.12 = (f32[32,32,128]{2,1,0:T(8,128)S(1)}, f32[32,32,128]{2,1,0:T(8,128)S(1)}, u32[]{:S(2)}, u32[]{:S(2)}) collective-permute-start(f32[32,32,128]{2,1,0:T(8,128)S(1)} %collective-permute-done.3.refs_7_), channel_id=1, source_target_pairs={{0,128},{1,129},{2,130},{3,131},{4,132},{5,133},{6,134},{7,135},{8... | collective-permute-start | bytes 1572872 | tf_op jit(solution)/shard_map/ppermute | solution.py:30
  50.7 10.9 %collective-permute-start.10 = (f32[32,32,128]{2,1,0:T(8,128)S(1)}, f32[32,32,128]{2,1,0:T(8,128)S(1)}, u32[]{:S(2)}, u32[]{:S(2)}) collective-permute-start(f32[32,32,128]{2,1,0:T(8,128)S(1)} %collective-permute-done.6.refs_3_), channel_id=1, source_target_pairs={{0,4},{1,5},{2,6},{3,7},{4,0},{5,1},{6,2},{7,3},{8,12},{9,13},{10,... | collective-permute-start | bytes 1572872 | tf_op jit(solution)/shard_map/ppermute | solution.py:30
  56.6 5.0 %collective-permute-start.11 = (f32[32,32,128]{2,1,0:T(8,128)S(1)}, f32[32,32,128]{2,1,0:T(8,128)S(1)}, u32[]{:S(2)}, u32[]{:S(2)}) collective-permute-start(f32[32,32,128]{2,1,0:T(8,128)S(1)} %collective-permute-done.7.refs_3_), channel_id=1, source_target_pairs={{0,4},{1,5},{2,6},{3,7},{4,0},{5,1},{6,2},{7,3},{8,12},{9,13},{10,... | collective-permute-start | bytes 1572872 | tf_op jit(solution)/shard_map/ppermute | solution.py:30
  56.6 18.9 %collective-permute-start.8 = (f32[32,32,128]{2,1,0:T(8,128)S(1)}, f32[32,32,128]{2,1,0:T(8,128)S(1)}, u32[]{:S(2)}, u32[]{:S(2)}) collective-permute-start(f32[32,32,128]{2,1,0:T(8,128)S(1)} %collective-permute-done.7.refs_3_), channel_id=1, source_target_pairs={{0,24},{1,25},{2,26},{3,27},{4,28},{5,29},{6,30},{7,31},{8,0},{9,1... | collective-permute-start | bytes 1572872 | tf_op jit(solution)/shard_map/ppermute | solution.py:30
  75.5 2.0 %collective-permute-start.13 = (f32[32,32,128]{2,1,0:T(8,128)S(1)}, f32[32,32,128]{2,1,0:T(8,128)S(1)}, u32[]{:S(2)}, u32[]{:S(2)}) collective-permute-start(f32[32,32,128]{2,1,0:T(8,128)S(1)} %collective-permute-done.8.refs_4_), channel_id=1, source_target_pairs={{0,4},{1,5},{2,6},{3,7},{4,0},{5,1},{6,2},{7,3},{8,12},{9,13},{10,... | collective-permute-start | bytes 1572872 | tf_op jit(solution)/shard_map/ppermute | solution.py:30
  82.0 8.7 %collective-permute-start.18 = (f32[32,16,128]{2,1,0:T(8,128)S(1)}, f32[32,16,128]{2,1,0:T(8,128)S(1)}, u32[]{:S(2)}, u32[]{:S(2)}) collective-permute-start(f32[32,16,128]{2,1,0:T(8,128)S(1)} %get-tuple-element.65), channel_id=1, source_target_pairs={{0,1},{1,2},{2,3},{3,0},{4,5},{5,6},{6,7},{7,4},{8,9},{9,10},{10,1... | collective-permute-start | bytes 786440 | tf_op jit(solution)/shard_map/ppermute | solution.py:30
  82.5 8.3 %collective-permute-start.19 = (f32[32,16,128]{2,1,0:T(8,128)S(1)}, f32[32,16,128]{2,1,0:T(8,128)S(1)}, u32[]{:S(2)}, u32[]{:S(2)}) collective-permute-start(f32[32,16,128]{2,1,0:T(8,128)S(1)} %get-tuple-element.66), channel_id=1, source_target_pairs={{0,3},{1,0},{2,1},{3,2},{4,7},{5,4},{6,5},{7,6},{8,11},{9,8},{10,9... | collective-permute-start | bytes 786440 | tf_op jit(solution)/shard_map/ppermute | solution.py:30
  88.6 7.8 %collective-permute-start.14 = (f32[32,16,128]{2,1,0:T(8,128)S(1)}, f32[32,16,128]{2,1,0:T(8,128)S(1)}, u32[]{:S(2)}, u32[]{:S(2)}) collective-permute-start(f32[32,16,128]{2,1,0:T(8,128)S(1)} %get-tuple-element.56), channel_id=1, source_target_pairs={{0,1},{1,2},{2,3},{3,0},{4,5},{5,6},{6,7},{7,4},{8,9},{9,10},{10,1... | collective-permute-start | bytes 786440 | tf_op jit(solution)/shard_map/ppermute | solution.py:30
  90.3 8.7 %collective-permute-start.15 = (f32[32,16,128]{2,1,0:T(8,128)S(1)}, f32[32,16,128]{2,1,0:T(8,128)S(1)}, u32[]{:S(2)}, u32[]{:S(2)}) collective-permute-start(f32[32,16,128]{2,1,0:T(8,128)S(1)} %get-tuple-element.57), channel_id=1, source_target_pairs={{0,3},{1,0},{2,1},{3,2},{4,7},{5,4},{6,5},{7,6},{8,11},{9,8},{10,9... | collective-permute-start | bytes 786440 | tf_op jit(solution)/shard_map/ppermute | solution.py:30
  90.8 10.4 %collective-permute-start.20 = (f32[16,16,128]{2,1,0:T(8,128)S(1)}, f32[16,16,128]{2,1,0:T(8,128)S(1)}, u32[]{:S(2)}, u32[]{:S(2)}) collective-permute-start(f32[16,16,128]{2,1,0:T(8,128)S(1)} %slice_add_fusion.1), channel_id=1, source_target_pairs={{0,1},{1,2},{2,3},{3,0},{4,5},{5,6},{6,7},{7,4},{8,9},{9,10},{10,1... | collective-permute-start | bytes 393224 | tf_op jit(solution)/shard_map/ppermute | solution.py:30
  93.7 7.7 %collective-permute-start.21 = (f32[16,16,128]{2,1,0:T(8,128)S(1)}, f32[16,16,128]{2,1,0:T(8,128)S(1)}, u32[]{:S(2)}, u32[]{:S(2)}) collective-permute-start(f32[16,16,128]{2,1,0:T(8,128)S(1)} %slice_add_fusion), channel_id=1, source_target_pairs={{0,3},{1,0},{2,1},{3,2},{4,7},{5,4},{6,5},{7,6},{8,11},{9,8},{10,9... | collective-permute-start | bytes 393224 | tf_op jit(solution)/shard_map/ppermute | solution.py:30
  99.0 5.0 %collective-permute-start.16 = (f32[16,16,128]{2,1,0:T(8,128)S(1)}, f32[16,16,128]{2,1,0:T(8,128)S(1)}, u32[]{:S(2)}, u32[]{:S(2)}) collective-permute-start(f32[16,16,128]{2,1,0:T(8,128)S(1)} %slice_add_fusion.3), channel_id=1, source_target_pairs={{0,1},{1,2},{2,3},{3,0},{4,5},{5,6},{6,7},{7,4},{8,9},{9,10},{10,1... | collective-permute-start | bytes 393224 | tf_op jit(solution)/shard_map/ppermute | solution.py:30
  99.3 6.6 %copy-start.1 = (f32[1,1,32,4096]{3,2,1,0:T(8,128)S(1)}, f32[1,1,32,4096]{3,2,1,0:T(8,128)}, u32[]{:S(2)}) copy-start(f32[1,1,32,4096]{3,2,1,0:T(8,128)} %param.7) | copy-start | bytes 1572868
  99.3 6.3 %collective-permute-start.17 = (f32[16,16,128]{2,1,0:T(8,128)S(1)}, f32[16,16,128]{2,1,0:T(8,128)S(1)}, u32[]{:S(2)}, u32[]{:S(2)}) collective-permute-start(f32[16,16,128]{2,1,0:T(8,128)S(1)} %slice_add_fusion.2), channel_id=1, source_target_pairs={{0,3},{1,0},{2,1},{3,2},{4,7},{5,4},{6,5},{7,6},{8,11},{9,8},{10,9... | collective-permute-start | bytes 393224 | tf_op jit(solution)/shard_map/ppermute | solution.py:30

commit v7 on v6

v7 whole, which is shorter than its diff:
```python
import functools

import jax
import jax.numpy as jnp
from jax import lax
from jax.experimental import pallas as pl
from jax.experimental.pallas import tpu as pltpu
from jax.sharding import PartitionSpec as P

AXES = ("row", "col", "depth")
F32 = jnp.float32
BF16 = jnp.bfloat16
TILES = 32
SLOTS = 128
UNROLL = 32
PARTS = ((0, 32), (32, 48), (48, 80), (80, 112), (112, 128))


def moved(x, target):
    pairs = []
    for y in range(4):
        for zh in range(2):
            for zl in range(4):
                for c in range(2):
                    for d in range(4):
                        ty, th, tl, tc, td = target(y, zh, zl, c, d)
                        source = ((y * 2 + zh) * 8 + zl * 2 + c) * 4 + d
                        dest = ((ty % 4 * 2 + th % 2) * 8 + tl % 4 * 2 + tc % 2) * 4 + td % 4
                        pairs.append((source, dest))
    return lax.ppermute(x, AXES, pairs)


def by_y(x, k):
    return moved(x, lambda y, zh, zl, c, d: (y + k, zh, zl, c, d))


def by_zl(x, k):
    return moved(x, lambda y, zh, zl, c, d: (y, zh, zl + k, c, d))


def by_depth(x, k):
    return moved(x, lambda y, zh, zl, c, d: (y, zh, zl, c, d + k))


def swap_zh(x):
    return moved(x, lambda y, zh, zl, c, d: (y, zh + 1, zl, c, d))


def swap_core(x):
    return moved(x, lambda y, zh, zl, c, d: (y, zh, zl, c + 1, d))


def split(p):
    high = p.astype(BF16).astype(F32)
    return high, p - high


def section_kernel(jobs, later, n_left, n_right, n_made, has_acc, half, *refs):
    def take(n):
        nonlocal refs
        taken, refs = refs[:n], refs[n:]
        return taken

    place, pairs, counts = take(3)
    lefts, rights, made = take(n_left), take(n_right), take(n_made)
    start = take(1) if has_acc else ()
    outs = take(len(PARTS)) if half is not None else ()
    out = take(1)[0]
    splits = take(len(later))
    a3 = take(1)[0]
    if rights:
        rows, b3 = take(2)
    shift, core, depth = place[0], place[1], place[2]
    lane = lax.broadcasted_iota(jnp.int32, (32, 128), 1) < 64
    height = out.shape[1]
    lane_left = lane[:height]

    def section(job):
        k, odd = job[0], job[1]
        return lax.rem(2 * k + 9 - 2 * core, 8) if odd else 2 * k

    def split_left(left, t):
        p = left[t] if half is None else left[t, height * half : height * half + height]
        h, low = split(p)
        hr = pltpu.roll(h, 64, 1)
        lr = pltpu.roll(low, 64, 1)
        a3[t, 0:height, 0:128] = jnp.where(lane_left, h, hr).astype(BF16)
        a3[t, height : 2 * height, 0:128] = jnp.where(lane_left, hr, h).astype(BF16)
        a3[t, 0:height, 128:256] = jnp.where(lane_left, low, lr).astype(BF16)
        a3[t, height : 2 * height, 128:256] = jnp.where(lane_left, lr, low).astype(BF16)

    def split_right(job, target):
        k, _, _, choices = job

        def interleave(ref):
            @pl.loop(0, TILES, unroll=4)
            def _(t):
                r = ref[t]
                rr = pltpu.roll(r, 64, 1)
                rows[t, pl.ds(0, 32, stride=2)] = jnp.where(lane, r, rr)
                rows[t, pl.ds(1, 32, stride=2)] = jnp.where(lane, rr, r)

        if len(choices) == 1:
            interleave(rights[choices[0][1]])
        else:
            want = lax.rem(k + shift + 4, 4)
            for offset, index in choices:
                pl.when(want == offset)(functools.partial(interleave, rights[index]))

        @pl.loop(0, TILES, unroll=4)
        def _(t):
            h, low = split(rows[t])
            h = h.astype(BF16)
            low = low.astype(BF16)
            target[t, 0:64] = h
            target[t, 64:128] = low
            target[t, 128:192] = h
            target[t, 192:256] = low

    if not has_acc:
        out[...] = jnp.zeros_like(out)
    elif half is None:
        out[...] = start[0][...]
    else:
        out[...] = start[0][:, height * half : height * half + height]
    for j, job in enumerate(jobs):
        left = lefts[job[2]]

        @pl.loop(0, TILES, unroll=4)
        def _(t):
            split_left(left, t)

        if made:
            weights = made[j]
        else:
            weights = b3
            split_right(job, weights)
        s = section(job)
        live = counts[s]

        @pl.loop(0, (live + UNROLL - 1) // UNROLL)
        def _(block):
            sums, slots = [], []
            for u in range(UNROLL):
                p = block * UNROLL + u
                c = jnp.dot(a3[pairs[s, 0, p]], weights[pairs[s, 1, p]], preferred_element_type=F32)
                sums.append(jnp.where(lane_left, c[0:height], c[height : 2 * height]))
                g = lax.rem(pairs[s, 2, p] + (4 - depth) * 32, SLOTS)
                slots.append(jnp.where(p < live, g, SLOTS))
            for u in range(UNROLL):
                out[slots[u]] += sums[u]

    for job, target in zip(later, splits):
        split_right(job, target)
    for ref, (first, last) in zip(outs, PARTS):
        ref[...] = out[first:last]


def add_sections(jobs, place, pattern, limits, lefts, rights, acc, name, later=[], half=None, made=[]):
    smem = pl.BlockSpec(memory_space=pltpu.SMEM)
    vmem = pl.BlockSpec(memory_space=pltpu.VMEM)
    operands = [*lefts, *rights, *made] + ([] if acc is None else [acc])
    height = 32 if half is None else 16
    sums = (SLOTS + 1, height, 128)
    shapes = [jax.ShapeDtypeStruct(sums, F32)]
    shapes += [jax.ShapeDtypeStruct((TILES, 256, 128), BF16) for _ in later]
    scratch = [pltpu.VMEM((TILES, 2 * height, 256), BF16)]
    if rights:
        scratch += [pltpu.VMEM((TILES, 64, 128), F32), pltpu.VMEM((TILES, 256, 128), BF16)]
    if half is not None:
        shapes = [jax.ShapeDtypeStruct((last - first, height, 128), F32) for first, last in PARTS]
        scratch = [pltpu.VMEM(sums, F32)] + scratch
    out = pl.pallas_call(
        functools.partial(
            section_kernel, jobs, later, len(lefts), len(rights), len(made), acc is not None, half
        ),
        out_shape=shapes,
        in_specs=[smem] * 3 + [vmem] * len(operands),
        out_specs=[vmem] * len(shapes),
        scratch_shapes=scratch,
        compiler_params=pltpu.CompilerParams(vmem_limit_bytes=28 << 20),
        cost_estimate=pl.CostEstimate(flops=0, bytes_accessed=0, transcendentals=0),
        name=name,
    )(place, pattern, limits, *operands)
    return out[0] if len(out) == 1 else out


def reduce_over_depth(parts):
    own, low, up, down, high = parts
    up, down = by_depth(up, 1), by_depth(down, -1)
    up, down = lax.optimization_barrier((up, down))
    up2 = by_depth(low + up[16:32], 1)
    down2 = by_depth(high + down[0:16], -1)
    up2, down2 = lax.optimization_barrier((up2, down2))
    return jnp.concatenate([own[0:16] + down[16:32] + up2, own[16:32] + up[0:16] + down2])


def on_device(left_tiles, right_tiles, square_tiles, pairs, counts):
    row, col = lax.axis_index("row"), lax.axis_index("col")
    core = col % 2
    place = jnp.stack([row % 2 - core, core, lax.axis_index("depth")]).astype(jnp.int32)
    pattern, limits = pairs[0, 0, 0], counts[0, 0, 0]

    right = right_tiles[0, 0, 0, 0].reshape(TILES, 32, 128)
    left = left_tiles[0, 0, 0].reshape(TILES, 32, 128)

    args = (place, pattern, limits)
    choices = [(i, i) for i in range(4)]
    other0 = swap_zh(right)
    same1, same3, same2 = by_y(right, -1), by_y(right, 1), by_y(right, 2)
    twin0 = swap_core(left)
    acc = add_sections([(0, False, 0, [(0, 0)])], *args, [left], [right], None, "sections_a")
    other0, acc, left = lax.optimization_barrier((other0, acc, left))
    left1 = by_zl(left, -1)
    same1, same3, same2, other0, acc = lax.optimization_barrier((same1, same3, same2, other0, acc))

    other1, other3, other2 = by_y(other0, -1), by_y(other0, 1), by_y(other0, 2)
    left2 = by_zl(left1, -1)
    twin1 = swap_core(left1)
    even3, odd3 = (3, False, 1, [(3, 1)]), (3, True, 0, choices)
    acc, made_even = add_sections(
        [(1, False, 0, [(1, 0)])], *args, [left1], [same1, same3], acc, "sections_b", [even3]
    )
    other1, other3, left2, acc = lax.optimization_barrier((other1, other3, left2, acc))

    left3 = by_zl(left2, -1)
    twin2 = swap_core(left2)
    acc = add_sections([(2, False, 0, [(2, 0)])], *args, [left2], [same2], acc, "sections_c")
    other2, acc = lax.optimization_barrier((other2, acc))
    other = [other0, other1, other2, other3]
    jobs = [(k, True, k, choices) for k in range(3)]
    acc, made_odd = add_sections(jobs, *args, [twin0, twin1, twin2], other, acc, "sections_d", [odd3])

    left3, acc = lax.optimization_barrier((left3, acc))
    twin3 = swap_core(left3)
    made, lefts = [made_even, made_odd], [twin3, left3]
    share = [
        add_sections([even3, odd3], *args, lefts, [], acc, f"sections_e{h}", [], h, made) for h in range(2)
    ]
    share = [reduce_over_depth(half) for half in share]
    share = jnp.concatenate(share, axis=1)
    purified = 3.0 * square_tiles[0, 0] - 2.0 * share.reshape(TILES, 4096)
    return purified[None, None]


def solution(mesh):
    in_specs = (
        P("row", "col", "depth", None, None),
        P("row", "col", "depth", None, None, None),
        P("row", "col", "depth", None),
        P("row", "col", "depth", None, None, None),
        P("row", "col", "depth", None),
    )
    out_specs = P("row", "col", "depth", None)
    return jax.shard_map(
        on_device, mesh=mesh, in_specs=in_specs, out_specs=out_specs, check_vma=False
    )
```

time: 109 us -> 106 us (0.972)
  Pallas kernels: 30.3 us -> 25.1 us
  starting transfers between devices: 36.5 us -> 38.7 us
    pallas_call x5 -> x6, Pallas kernels: 30.3 us -> 25.1 us  [add_sections(): pl.pallas_call(functools.partial(section_kernel, jobs, later, len(lefts),...]
    ppermute x22, starting transfers between devices: 36.5 us -> 38.7 us  [moved(): return lax.ppermute(x, AXES, pairs)]
  transfers between devices with their start and end apart: 22 -> 22, of which waited for: 13 -> 11; matrix products, arithmetic and copies ran while one was open for 2% -> 2% of each run, Pallas kernels for 24% -> 21%
where the time goes in v7:
time: 106 us; the launch traced here: 104 us
  starting transfers between devices  38.7 us (37%)
  waiting for transfers between devices  35.8 us (34%)
  Pallas kernels  25.1 us (24%)
  local copies, waits for them, and re-layouts  3.11 us (3%)
  other arithmetic  1.16 us (1%)
    ppermute x22, starting transfers between devices, moved(): return lax.ppermute(x, AXES, pairs)  38.7 us
    ppermute x22, waiting for transfers between devices, moved(): return lax.ppermute(x, AXES, pairs)  35.8 us
    pallas_call x6, Pallas kernels, add_sections(): pl.pallas_call(functools.partial(section_kernel, jobs, later, len(lefts),...  25.1 us
    unnamed x7, local copies, waits for them, and re-layouts  3.01 us
  transfers between devices with their start and end apart: 22, of which 11 were waited for; matrix products, arithmetic and copies ran while one was open for 2% of the time, Pallas kernels for 21%

profile of v7, /device:TPU:30, one launch (start us, length us, event | category | flops | bytes accessed | tf_op | source)
XLA Modules:
  0.0 104.1 jit_solution(7606573728434603846)
XLA Ops:
  0.0 1.1 %copy.7 = f32[4,8,32,128]{3,2,1,0:T(8,128)S(1)} copy(f32[4,8,32,128]{3,1,2,0:T(8,128)} %bitcast.35) | data formatting | bytes 1048576
  1.2 7.3 %collective-permute-start.3 = (f32[32,32,128]{2,1,0:T(8,128)S(1)}, f32[32,32,128]{2,1,0:T(8,128)S(1)}, u32[]{:S(2)}, u32[]{:S(2)}) collective-permute-start(f32[32,32,128]{2,1,0:T(8,128)S(1)} %bitcast.15), channel_id=1, source_target_pairs={{0,32},{1,33},{2,34},{3,35},{4,36},{5,37},{6,38},{7,39},{8,40},{9,... | collective-permute-start | bytes 1572872 | tf_op jit(solution)/shard_map/ppermute | solution.py:30
  8.4 1.2 %collective-permute-start.2 = (f32[32,32,128]{2,1,0:T(8,128)S(1)}, f32[32,32,128]{2,1,0:T(8,128)S(1)}, u32[]{:S(2)}, u32[]{:S(2)}) collective-permute-start(f32[32,32,128]{2,1,0:T(8,128)S(1)} %bitcast.16), channel_id=1, source_target_pairs={{0,128},{1,129},{2,130},{3,131},{4,132},{5,133},{6,134},{7,135},{8... | collective-permute-start | bytes 1572872 | tf_op jit(solution)/shard_map/ppermute | solution.py:30
  9.7 2.2 %collective-permute-start.1 = (f32[32,32,128]{2,1,0:T(8,128)S(1)}, f32[32,32,128]{2,1,0:T(8,128)S(1)}, u32[]{:S(2)}, u32[]{:S(2)}) collective-permute-start(f32[32,32,128]{2,1,0:T(8,128)S(1)} %bitcast.17), channel_id=1, source_target_pairs={{0,64},{1,65},{2,66},{3,67},{4,68},{5,69},{6,70},{7,71},{8,72},{9,... | collective-permute-start | bytes 1572872 | tf_op jit(solution)/shard_map/ppermute | solution.py:30
  11.8 0.0 collective-permute-start
  11.9 0.7 copy.10
  12.6 0.1 pad_add_fusion.refs_0_
  12.6 1.1 %copy.8 = f32[4,8,32,128]{3,2,1,0:T(8,128)S(1)} copy(f32[4,8,32,128]{3,1,2,0:T(8,128)} %bitcast.36) | data formatting | bytes 1048576
  13.8 3.1 %sections_a.1.refs_6_ = f32[129,32,128]{2,1,0:T(8,128)S(1)} custom-call(s32[3]{0:T(128)S(1)} %pad_add_fusion.refs_0_, s32[8,3,64]{2,1,0:T(4,128)S(1)} %bitcast.23, s32[8]{0:T(128)S(1)} %bitcast.29, f32[32,32,128]{2,1,0:T(8,128)S(1)} %bitcast.20, f32[32,32,128]{2,1,0:T(8,128)S(1)} %bitcast.19), custom_call_target="tpu_custom_call" | custom-call | tf_op jit(solution)/shard_map/sections_a/pallas_call | solution.py:173
  16.9 5.7 %collective-permute-done.3.refs_6_ = f32[32,32,128]{2,1,0:T(8,128)S(1)} collective-permute-done((f32[32,32,128]{2,1,0:T(8,128)S(1)}, f32[32,32,128]{2,1,0:T(8,128)S(1)}, u32[]{:S(2)}, u32[]{:S(2)}) %collective-permute-start.3) | collective-permute-done | bytes 524320 | tf_op jit(solution)/shard_map/ppermute | solution.py:30
  22.6 7.0 %collective-permute-start.6 = (f32[32,32,128]{2,1,0:T(8,128)S(1)}, f32[32,32,128]{2,1,0:T(8,128)S(1)}, u32[]{:S(2)}, u32[]{:S(2)}) collective-permute-start(f32[32,32,128]{2,1,0:T(8,128)S(1)} %bitcast.21), channel_id=1, source_target_pairs={{0,24},{1,25},{2,26},{3,27},{4,28},{5,29},{6,30},{7,31},{8,0},{9,1... | collective-permute-start | bytes 1572872 | tf_op jit(solution)/shard_map/ppermute | solution.py:30
  29.6 2.5 %collective-permute-done.1.refs_5_ = f32[32,32,128]{2,1,0:T(8,128)S(1)} collective-permute-done((f32[32,32,128]{2,1,0:T(8,128)S(1)}, f32[32,32,128]{2,1,0:T(8,128)S(1)}, u32[]{:S(2)}, u32[]{:S(2)}) %collective-permute-start.1) | collective-permute-done | bytes 524320 | tf_op jit(solution)/shard_map/ppermute | solution.py:30
  32.1 2.4 %collective-permute-done.refs_4_ = f32[32,32,128]{2,1,0:T(8,128)S(1)} collective-permute-done((f32[32,32,128]{2,1,0:T(8,128)S(1)}, f32[32,32,128]{2,1,0:T(8,128)S(1)}, u32[]{:S(2)}, u32[]{:S(2)}) %collective-permute-start) | collective-permute-done | bytes 524320 | tf_op jit(solution)/shard_map/ppermute | solution.py:30
  34.6 0.6 collective-permute-start.5
  35.2 1.4 %collective-permute-start.4 = (f32[32,32,128]{2,1,0:T(8,128)S(1)}, f32[32,32,128]{2,1,0:T(8,128)S(1)}, u32[]{:S(2)}, u32[]{:S(2)}) collective-permute-start(f32[32,32,128]{2,1,0:T(8,128)S(1)} %collective-permute-done.3.refs_6_), channel_id=1, source_target_pairs={{0,192},{1,193},{2,194},{3,195},{4,196},{5,197},{6,198},{7,199},{8... | collective-permute-start | bytes 1572872 | tf_op jit(solution)/shard_map/ppermute | solution.py:30
  36.6 7.4 %collective-permute-done.6.refs_3_ = f32[32,32,128]{2,1,0:T(8,128)S(1)} collective-permute-done((f32[32,32,128]{2,1,0:T(8,128)S(1)}, f32[32,32,128]{2,1,0:T(8,128)S(1)}, u32[]{:S(2)}, u32[]{:S(2)}) %collective-permute-start.6) | collective-permute-done | bytes 524320 | tf_op jit(solution)/shard_map/ppermute | solution.py:30
  44.0 1.8 %collective-permute-start.7 = (f32[32,32,128]{2,1,0:T(8,128)S(1)}, f32[32,32,128]{2,1,0:T(8,128)S(1)}, u32[]{:S(2)}, u32[]{:S(2)}) collective-permute-start(f32[32,32,128]{2,1,0:T(8,128)S(1)} %collective-permute-done.6.refs_3_), channel_id=1, source_target_pairs={{0,24},{1,25},{2,26},{3,27},{4,28},{5,29},{6,30},{7,31},{8,0},{9,1... | collective-permute-start | bytes 1572872 | tf_op jit(solution)/shard_map/ppermute | solution.py:30
  45.8 0.0 collective-permute-start.9
  45.8 1.2 %collective-permute-start.12 = (f32[32,32,128]{2,1,0:T(8,128)S(1)}, f32[32,32,128]{2,1,0:T(8,128)S(1)}, u32[]{:S(2)}, u32[]{:S(2)}) collective-permute-start(f32[32,32,128]{2,1,0:T(8,128)S(1)} %collective-permute-done.3.refs_6_), channel_id=1, source_target_pairs={{0,128},{1,129},{2,130},{3,131},{4,132},{5,133},{6,134},{7,135},{8... | collective-permute-start | bytes 1572872 | tf_op jit(solution)/shard_map/ppermute | solution.py:30
  47.0 3.9 %sections_b.1 = (f32[129,32,128]{2,1,0:T(8,128)S(1)}, bf16[32,256,128]{2,1,0:T(8,128)(2,1)S(1)}) custom-call(s32[3]{0:T(128)S(1)} %pad_add_fusion.refs_0_, s32[8,3,64]{2,1,0:T(4,128)S(1)} %bitcast.24, s32[8]{0:T(128)S(1)} %bitcast.30, f32[32,32,128]{2,1,0:T(8,128)S(1)} %collective-permute-done.6.refs_3_, f32[32,32,128]{2,1,0:T(8,128)S(1)} %collective-permute-done.refs_4_, ...), custom_call_target="tpu_custom_call" | custom-call | tf_op jit(solution)/shard_map/sections_b/pallas_call | solution.py:173
  50.9 0.0 collective-permute-done.5.refs_9_
  50.9 0.3 collective-permute-start.10
  51.2 5.3 %collective-permute-done.7.refs_3_ = f32[32,32,128]{2,1,0:T(8,128)S(1)} collective-permute-done((f32[32,32,128]{2,1,0:T(8,128)S(1)}, f32[32,32,128]{2,1,0:T(8,128)S(1)}, u32[]{:S(2)}, u32[]{:S(2)}) %collective-permute-start.7) | collective-permute-done | bytes 524320 | tf_op jit(solution)/shard_map/ppermute | solution.py:30
  56.6 4.3 %collective-permute-start.8 = (f32[32,32,128]{2,1,0:T(8,128)S(1)}, f32[32,32,128]{2,1,0:T(8,128)S(1)}, u32[]{:S(2)}, u32[]{:S(2)}) collective-permute-start(f32[32,32,128]{2,1,0:T(8,128)S(1)} %collective-permute-done.7.refs_3_), channel_id=1, source_target_pairs={{0,24},{1,25},{2,26},{3,27},{4,28},{5,29},{6,30},{7,31},{8,0},{9,1... | collective-permute-start | bytes 1572872 | tf_op jit(solution)/shard_map/ppermute | solution.py:30
  60.9 3.1 %sections_c.1.refs_10_ = f32[129,32,128]{2,1,0:T(8,128)S(1)} custom-call(s32[3]{0:T(128)S(1)} %pad_add_fusion.refs_0_, s32[8,3,64]{2,1,0:T(4,128)S(1)} %bitcast.25, s32[8]{0:T(128)S(1)} %bitcast.31, f32[32,32,128]{2,1,0:T(8,128)S(1)} %collective-permute-done.7.refs_3_, f32[32,32,128]{2,1,0:T(8,128)S(1)} %collective-permute-done.2.refs_4_, ...), custom_call_target="tpu_custom_call" | custom-call | tf_op jit(solution)/shard_map/sections_c/pallas_call | solution.py:173
  64.0 8.5 %sections_d.1 = (f32[129,32,128]{2,1,0:T(8,128)S(1)}, bf16[32,256,128]{2,1,0:T(8,128)(2,1)S(1)}) custom-call(s32[3]{0:T(128)S(1)} %pad_add_fusion.refs_0_, s32[8,3,64]{2,1,0:T(4,128)S(1)} %bitcast.26, s32[8]{0:T(128)S(1)} %bitcast.32, f32[32,32,128]{2,1,0:T(8,128)S(1)} %collective-permute-done.9.refs_3_, f32[32,32,128]{2,1,0:T(8,128)S(1)} %collective-permute-done.10.refs_4_, ...), custom_call_target="tpu_custom_call" | custom-call | tf_op jit(solution)/shard_map/sections_d/pallas_call | solution.py:173
  72.5 0.3 collective-permute-done.8.refs_4_
  72.7 0.0 collective-permute-start.13
  72.7 1.9 %collective-permute-done.13.refs_3_ = f32[32,32,128]{2,1,0:T(8,128)S(1)} collective-permute-done((f32[32,32,128]{2,1,0:T(8,128)S(1)}, f32[32,32,128]{2,1,0:T(8,128)S(1)}, u32[]{:S(2)}, u32[]{:S(2)}) %collective-permute-start.13) | collective-permute-done | bytes 524320 | tf_op jit(solution)/shard_map/ppermute | solution.py:30
  74.6 3.3 %sections_e1.1 = (f32[32,16,128]{2,1,0:T(8,128)S(1)}, f32[16,16,128]{2,1,0:T(8,128)S(1)}, f32[32,16,128]{2,1,0:T(8,128)S(1)}, f32[32,16,128]{2,1,0:T(8,128)S(1)}, f32[16,16,128]{2,1,0:T(8,128)S(1)}) custom-call(s32[3]{0:T(128)S(1)} %pad_add_fusion.refs_0_, s32[8,3,64]{2,1,0:T(4,128)S(1)} %bitcast.27, s32[8]{0:T(128)S(1)} %bitcast.33, ...), custom_call_target="tpu_custom_call" | custom-call | tf_op jit(solution)/shard_map/sections_e1/pallas_call | solution.py:173
  77.9 0.6 collective-permute-start.18
  78.5 3.2 %collective-permute-start.19 = (f32[32,16,128]{2,1,0:T(8,128)S(1)}, f32[32,16,128]{2,1,0:T(8,128)S(1)}, u32[]{:S(2)}, u32[]{:S(2)}) collective-permute-start(f32[32,16,128]{2,1,0:T(8,128)S(1)} %get-tuple-element.74), channel_id=1, source_target_pairs={{0,3},{1,0},{2,1},{3,2},{4,7},{5,4},{6,5},{7,6},{8,11},{9,8},{10,9... | collective-permute-start | bytes 786440 | tf_op jit(solution)/shard_map/ppermute | solution.py:30
  81.7 3.3 %sections_e0.1 = (f32[32,16,128]{2,1,0:T(8,128)S(1)}, f32[16,16,128]{2,1,0:T(8,128)S(1)}, f32[32,16,128]{2,1,0:T(8,128)S(1)}, f32[32,16,128]{2,1,0:T(8,128)S(1)}, f32[16,16,128]{2,1,0:T(8,128)S(1)}) custom-call(s32[3]{0:T(128)S(1)} %pad_add_fusion.refs_0_, s32[8,3,64]{2,1,0:T(4,128)S(1)} %bitcast.28, s32[8]{0:T(128)S(1)} %bitcast.34, ...), custom_call_target="tpu_custom_call" | custom-call | tf_op jit(solution)/shard_map/sections_e0/pallas_call | solution.py:173
  85.0 0.2 collective-permute-start.14
  85.1 2.9 %collective-permute-start.15 = (f32[32,16,128]{2,1,0:T(8,128)S(1)}, f32[32,16,128]{2,1,0:T(8,128)S(1)}, u32[]{:S(2)}, u32[]{:S(2)}) collective-permute-start(f32[32,16,128]{2,1,0:T(8,128)S(1)} %get-tuple-element.65), channel_id=1, source_target_pairs={{0,3},{1,0},{2,1},{3,2},{4,7},{5,4},{6,5},{7,6},{8,11},{9,8},{10,9... | collective-permute-start | bytes 786440 | tf_op jit(solution)/shard_map/ppermute | solution.py:30
  88.0 2.3 %collective-permute-start.20 = (f32[16,16,128]{2,1,0:T(8,128)S(1)}, f32[16,16,128]{2,1,0:T(8,128)S(1)}, u32[]{:S(2)}, u32[]{:S(2)}) collective-permute-start(f32[16,16,128]{2,1,0:T(8,128)S(1)} %slice_add_fusion.1), channel_id=1, source_target_pairs={{0,1},{1,2},{2,3},{3,0},{4,5},{5,6},{6,7},{7,4},{8,9},{9,10},{10,1... | collective-permute-start | bytes 393224 | tf_op jit(solution)/shard_map/ppermute | solution.py:30
  90.4 0.1 collective-permute-start.21
  90.5 3.8 %collective-permute-done.14 = f32[32,16,128]{2,1,0:T(8,128)S(1)} collective-permute-done((f32[32,16,128]{2,1,0:T(8,128)S(1)}, f32[32,16,128]{2,1,0:T(8,128)S(1)}, u32[]{:S(2)}, u32[]{:S(2)}) %collective-permute-start.14) | collective-permute-done | bytes 262176 | tf_op jit(solution)/shard_map/ppermute | solution.py:30
  94.2 1.0 collective-permute-done.15
  95.3 1.4 %collective-permute-start.16 = (f32[16,16,128]{2,1,0:T(8,128)S(1)}, f32[16,16,128]{2,1,0:T(8,128)S(1)}, u32[]{:S(2)}, u32[]{:S(2)}) collective-permute-start(f32[16,16,128]{2,1,0:T(8,128)S(1)} %slice_add_fusion.3), channel_id=1, source_target_pairs={{0,1},{1,2},{2,3},{3,0},{4,5},{5,6},{6,7},{7,4},{8,9},{9,10},{10,1... | collective-permute-start | bytes 393224 | tf_op jit(solution)/shard_map/ppermute | solution.py:30
  96.7 0.0 copy-start.1
  96.7 0.8 collective-permute-start.17
  97.5 2.8 %collective-permute-done.16 = f32[16,16,128]{2,1,0:T(8,128)S(1)} collective-permute-done((f32[16,16,128]{2,1,0:T(8,128)S(1)}, f32[16,16,128]{2,1,0:T(8,128)S(1)}, u32[]{:S(2)}, u32[]{:S(2)}) %collective-permute-start.16) | collective-permute-done | bytes 131104 | tf_op jit(solution)/shard_map/ppermute | solution.py:30
  100.3 2.7 %collective-permute-done.17 = f32[16,16,128]{2,1,0:T(8,128)S(1)} collective-permute-done((f32[16,16,128]{2,1,0:T(8,128)S(1)}, f32[16,16,128]{2,1,0:T(8,128)S(1)}, u32[]{:S(2)}, u32[]{:S(2)}) %collective-permute-start.17) | collective-permute-done | bytes 131104 | tf_op jit(solution)/shard_map/ppermute | solution.py:30
  103.0 0.1 add_add_fusion.1
  103.1 0.1 maximum_multiply_fusion
  103.1 0.1 mul.27
  103.3 0.8 multiply_subtract_fusion
  (18 shorter events, 0.1 us)
Async XLA Ops:
  0.0 13.8 %copy-start = (s32[1,1,1,8]{3,2,1,0:T(1,128)S(1)}, s32[1,1,1,8]{3,2,1,0:T(1,128)}, u32[]{:S(2)}) copy-start(s32[1,1,1,8]{3,2,1,0:T(1,128)} %param.9) | copy-start | bytes 100
  1.2 21.5 %collective-permute-start.3 = (f32[32,32,128]{2,1,0:T(8,128)S(1)}, f32[32,32,128]{2,1,0:T(8,128)S(1)}, u32[]{:S(2)}, u32[]{:S(2)}) collective-permute-start(f32[32,32,128]{2,1,0:T(8,128)S(1)} %bitcast.15), channel_id=1, source_target_pairs={{0,32},{1,33},{2,34},{3,35},{4,36},{5,37},{6,38},{7,39},{8,40},{9,... | collective-permute-start | bytes 1572872 | tf_op jit(solution)/shard_map/ppermute | solution.py:30
  8.4 21.2 %collective-permute-start.2 = (f32[32,32,128]{2,1,0:T(8,128)S(1)}, f32[32,32,128]{2,1,0:T(8,128)S(1)}, u32[]{:S(2)}, u32[]{:S(2)}) collective-permute-start(f32[32,32,128]{2,1,0:T(8,128)S(1)} %bitcast.16), channel_id=1, source_target_pairs={{0,128},{1,129},{2,130},{3,131},{4,132},{5,133},{6,134},{7,135},{8... | collective-permute-start | bytes 1572872 | tf_op jit(solution)/shard_map/ppermute | solution.py:30
  9.7 22.5 %collective-permute-start.1 = (f32[32,32,128]{2,1,0:T(8,128)S(1)}, f32[32,32,128]{2,1,0:T(8,128)S(1)}, u32[]{:S(2)}, u32[]{:S(2)}) collective-permute-start(f32[32,32,128]{2,1,0:T(8,128)S(1)} %bitcast.17), channel_id=1, source_target_pairs={{0,64},{1,65},{2,66},{3,67},{4,68},{5,69},{6,70},{7,71},{8,72},{9,... | collective-permute-start | bytes 1572872 | tf_op jit(solution)/shard_map/ppermute | solution.py:30
  11.8 22.7 %collective-permute-start = (f32[32,32,128]{2,1,0:T(8,128)S(1)}, f32[32,32,128]{2,1,0:T(8,128)S(1)}, u32[]{:S(2)}, u32[]{:S(2)}) collective-permute-start(f32[32,32,128]{2,1,0:T(8,128)S(1)} %bitcast.18), channel_id=1, source_target_pairs={{0,192},{1,193},{2,194},{3,195},{4,196},{5,197},{6,198},{7,199},{8... | collective-permute-start | bytes 1572872 | tf_op jit(solution)/shard_map/ppermute | solution.py:30
  22.6 21.4 %collective-permute-start.6 = (f32[32,32,128]{2,1,0:T(8,128)S(1)}, f32[32,32,128]{2,1,0:T(8,128)S(1)}, u32[]{:S(2)}, u32[]{:S(2)}) collective-permute-start(f32[32,32,128]{2,1,0:T(8,128)S(1)} %bitcast.21), channel_id=1, source_target_pairs={{0,24},{1,25},{2,26},{3,27},{4,28},{5,29},{6,30},{7,31},{8,0},{9,1... | collective-permute-start | bytes 1572872 | tf_op jit(solution)/shard_map/ppermute | solution.py:30
  34.6 16.4 %collective-permute-start.5 = (f32[32,32,128]{2,1,0:T(8,128)S(1)}, f32[32,32,128]{2,1,0:T(8,128)S(1)}, u32[]{:S(2)}, u32[]{:S(2)}) collective-permute-start(f32[32,32,128]{2,1,0:T(8,128)S(1)} %collective-permute-done.3.refs_6_), channel_id=1, source_target_pairs={{0,64},{1,65},{2,66},{3,67},{4,68},{5,69},{6,70},{7,71},{8,72},{9,... | collective-permute-start | bytes 1572872 | tf_op jit(solution)/shard_map/ppermute | solution.py:30
  35.2 16.1 %collective-permute-start.4 = (f32[32,32,128]{2,1,0:T(8,128)S(1)}, f32[32,32,128]{2,1,0:T(8,128)S(1)}, u32[]{:S(2)}, u32[]{:S(2)}) collective-permute-start(f32[32,32,128]{2,1,0:T(8,128)S(1)} %collective-permute-done.3.refs_6_), channel_id=1, source_target_pairs={{0,192},{1,193},{2,194},{3,195},{4,196},{5,197},{6,198},{7,199},{8... | collective-permute-start | bytes 1572872 | tf_op jit(solution)/shard_map/ppermute | solution.py:30
  44.0 12.6 %collective-permute-start.7 = (f32[32,32,128]{2,1,0:T(8,128)S(1)}, f32[32,32,128]{2,1,0:T(8,128)S(1)}, u32[]{:S(2)}, u32[]{:S(2)}) collective-permute-start(f32[32,32,128]{2,1,0:T(8,128)S(1)} %collective-permute-done.6.refs_3_), channel_id=1, source_target_pairs={{0,24},{1,25},{2,26},{3,27},{4,28},{5,29},{6,30},{7,31},{8,0},{9,1... | collective-permute-start | bytes 1572872 | tf_op jit(solution)/shard_map/ppermute | solution.py:30
  45.8 18.2 %collective-permute-start.9 = (f32[32,32,128]{2,1,0:T(8,128)S(1)}, f32[32,32,128]{2,1,0:T(8,128)S(1)}, u32[]{:S(2)}, u32[]{:S(2)}) collective-permute-start(f32[32,32,128]{2,1,0:T(8,128)S(1)} %bitcast.22), channel_id=1, source_target_pairs={{0,4},{1,5},{2,6},{3,7},{4,0},{5,1},{6,2},{7,3},{8,12},{9,13},{10,... | collective-permute-start | bytes 1572872 | tf_op jit(solution)/shard_map/ppermute | solution.py:30
  45.8 18.2 %collective-permute-start.12 = (f32[32,32,128]{2,1,0:T(8,128)S(1)}, f32[32,32,128]{2,1,0:T(8,128)S(1)}, u32[]{:S(2)}, u32[]{:S(2)}) collective-permute-start(f32[32,32,128]{2,1,0:T(8,128)S(1)} %collective-permute-done.3.refs_6_), channel_id=1, source_target_pairs={{0,128},{1,129},{2,130},{3,131},{4,132},{5,133},{6,134},{7,135},{8... | collective-permute-start | bytes 1572872 | tf_op jit(solution)/shard_map/ppermute | solution.py:30
  50.9 13.0 %collective-permute-start.10 = (f32[32,32,128]{2,1,0:T(8,128)S(1)}, f32[32,32,128]{2,1,0:T(8,128)S(1)}, u32[]{:S(2)}, u32[]{:S(2)}) collective-permute-start(f32[32,32,128]{2,1,0:T(8,128)S(1)} %collective-permute-done.6.refs_3_), channel_id=1, source_target_pairs={{0,4},{1,5},{2,6},{3,7},{4,0},{5,1},{6,2},{7,3},{8,12},{9,13},{10,... | collective-permute-start | bytes 1572872 | tf_op jit(solution)/shard_map/ppermute | solution.py:30
  56.6 7.4 %collective-permute-start.11 = (f32[32,32,128]{2,1,0:T(8,128)S(1)}, f32[32,32,128]{2,1,0:T(8,128)S(1)}, u32[]{:S(2)}, u32[]{:S(2)}) collective-permute-start(f32[32,32,128]{2,1,0:T(8,128)S(1)} %collective-permute-done.7.refs_3_), channel_id=1, source_target_pairs={{0,4},{1,5},{2,6},{3,7},{4,0},{5,1},{6,2},{7,3},{8,12},{9,13},{10,... | collective-permute-start | bytes 1572872 | tf_op jit(solution)/shard_map/ppermute | solution.py:30
  56.6 16.1 %collective-permute-start.8 = (f32[32,32,128]{2,1,0:T(8,128)S(1)}, f32[32,32,128]{2,1,0:T(8,128)S(1)}, u32[]{:S(2)}, u32[]{:S(2)}) collective-permute-start(f32[32,32,128]{2,1,0:T(8,128)S(1)} %collective-permute-done.7.refs_3_), channel_id=1, source_target_pairs={{0,24},{1,25},{2,26},{3,27},{4,28},{5,29},{6,30},{7,31},{8,0},{9,1... | collective-permute-start | bytes 1572872 | tf_op jit(solution)/shard_map/ppermute | solution.py:30
  72.7 1.9 %collective-permute-start.13 = (f32[32,32,128]{2,1,0:T(8,128)S(1)}, f32[32,32,128]{2,1,0:T(8,128)S(1)}, u32[]{:S(2)}, u32[]{:S(2)}) collective-permute-start(f32[32,32,128]{2,1,0:T(8,128)S(1)} %collective-permute-done.8.refs_4_), channel_id=1, source_target_pairs={{0,4},{1,5},{2,6},{3,7},{4,0},{5,1},{6,2},{7,3},{8,12},{9,13},{10,... | collective-permute-start | bytes 1572872 | tf_op jit(solution)/shard_map/ppermute | solution.py:30
  77.9 10.1 %collective-permute-start.18 = (f32[32,16,128]{2,1,0:T(8,128)S(1)}, f32[32,16,128]{2,1,0:T(8,128)S(1)}, u32[]{:S(2)}, u32[]{:S(2)}) collective-permute-start(f32[32,16,128]{2,1,0:T(8,128)S(1)} %get-tuple-element.73), channel_id=1, source_target_pairs={{0,1},{1,2},{2,3},{3,0},{4,5},{5,6},{6,7},{7,4},{8,9},{9,10},{10,1... | collective-permute-start | bytes 786440 | tf_op jit(solution)/shard_map/ppermute | solution.py:30
  78.5 9.5 %collective-permute-start.19 = (f32[32,16,128]{2,1,0:T(8,128)S(1)}, f32[32,16,128]{2,1,0:T(8,128)S(1)}, u32[]{:S(2)}, u32[]{:S(2)}) collective-permute-start(f32[32,16,128]{2,1,0:T(8,128)S(1)} %get-tuple-element.74), channel_id=1, source_target_pairs={{0,3},{1,0},{2,1},{3,2},{4,7},{5,4},{6,5},{7,6},{8,11},{9,8},{10,9... | collective-permute-start | bytes 786440 | tf_op jit(solution)/shard_map/ppermute | solution.py:30
  85.0 9.3 %collective-permute-start.14 = (f32[32,16,128]{2,1,0:T(8,128)S(1)}, f32[32,16,128]{2,1,0:T(8,128)S(1)}, u32[]{:S(2)}, u32[]{:S(2)}) collective-permute-start(f32[32,16,128]{2,1,0:T(8,128)S(1)} %get-tuple-element.64), channel_id=1, source_target_pairs={{0,1},{1,2},{2,3},{3,0},{4,5},{5,6},{6,7},{7,4},{8,9},{9,10},{10,1... | collective-permute-start | bytes 786440 | tf_op jit(solution)/shard_map/ppermute | solution.py:30
  85.1 10.1 %collective-permute-start.15 = (f32[32,16,128]{2,1,0:T(8,128)S(1)}, f32[32,16,128]{2,1,0:T(8,128)S(1)}, u32[]{:S(2)}, u32[]{:S(2)}) collective-permute-start(f32[32,16,128]{2,1,0:T(8,128)S(1)} %get-tuple-element.65), channel_id=1, source_target_pairs={{0,3},{1,0},{2,1},{3,2},{4,7},{5,4},{6,5},{7,6},{8,11},{9,8},{10,9... | collective-permute-start | bytes 786440 | tf_op jit(solution)/shard_map/ppermute | solution.py:30
  88.0 9.4 %collective-permute-start.20 = (f32[16,16,128]{2,1,0:T(8,128)S(1)}, f32[16,16,128]{2,1,0:T(8,128)S(1)}, u32[]{:S(2)}, u32[]{:S(2)}) collective-permute-start(f32[16,16,128]{2,1,0:T(8,128)S(1)} %slice_add_fusion.1), channel_id=1, source_target_pairs={{0,1},{1,2},{2,3},{3,0},{4,5},{5,6},{6,7},{7,4},{8,9},{9,10},{10,1... | collective-permute-start | bytes 393224 | tf_op jit(solution)/shard_map/ppermute | solution.py:30
  90.4 7.1 %collective-permute-start.21 = (f32[16,16,128]{2,1,0:T(8,128)S(1)}, f32[16,16,128]{2,1,0:T(8,128)S(1)}, u32[]{:S(2)}, u32[]{:S(2)}) collective-permute-start(f32[16,16,128]{2,1,0:T(8,128)S(1)} %slice_add_fusion), channel_id=1, source_target_pairs={{0,3},{1,0},{2,1},{3,2},{4,7},{5,4},{6,5},{7,6},{8,11},{9,8},{10,9... | collective-permute-start | bytes 393224 | tf_op jit(solution)/shard_map/ppermute | solution.py:30
  95.3 5.0 %collective-permute-start.16 = (f32[16,16,128]{2,1,0:T(8,128)S(1)}, f32[16,16,128]{2,1,0:T(8,128)S(1)}, u32[]{:S(2)}, u32[]{:S(2)}) collective-permute-start(f32[16,16,128]{2,1,0:T(8,128)S(1)} %slice_add_fusion.3), channel_id=1, source_target_pairs={{0,1},{1,2},{2,3},{3,0},{4,5},{5,6},{6,7},{7,4},{8,9},{9,10},{10,1... | collective-permute-start | bytes 393224 | tf_op jit(solution)/shard_map/ppermute | solution.py:30
  96.7 6.6 %copy-start.1 = (f32[1,1,32,4096]{3,2,1,0:T(8,128)S(1)}, f32[1,1,32,4096]{3,2,1,0:T(8,128)}, u32[]{:S(2)}) copy-start(f32[1,1,32,4096]{3,2,1,0:T(8,128)} %param.7) | copy-start | bytes 1572868
  96.7 6.3 %collective-permute-start.17 = (f32[16,16,128]{2,1,0:T(8,128)S(1)}, f32[16,16,128]{2,1,0:T(8,128)S(1)}, u32[]{:S(2)}, u32[]{:S(2)}) collective-permute-start(f32[16,16,128]{2,1,0:T(8,128)S(1)} %slice_add_fusion.2), channel_id=1, source_target_pairs={{0,3},{1,0},{2,1},{3,2},{4,7},{5,4},{6,5},{7,6},{8,11},{9,8},{10,9... | collective-permute-start | bytes 393224 | tf_op jit(solution)/shard_map/ppermute | solution.py:30
